TPU v7x, 128 devices: a whole 4x4x4 slice. The times are simulated.
128 devices in a mesh: section: 2 (over y_hi), dp: 16 (over x, y_lo, core), expert: 4 (over z).
Axes of the slice: x: 4, y: 4 (y_hi: 2, y_lo: 2; y = y_hi * 2 + y_lo), z: 4, core: 2. Of those that a mesh axis runs over, the one named last changes fastest.
Arguments:
- block_input: bfloat16 [2, 4096, 1536], P(None, ('dp', 'expert')), may hold values from -6 to 6
- segments: int32 [2, 4096], P(None, ('dp', 'expert')), may hold values from 0 to 47, as said below
- expert_ids: int32 [2, 2, 4096, 8], P('section', None, ('dp', 'expert')), may hold values from 0 to 15, all different within a row; in each aligned block of 64 rows (0 to 63, 64 to 127, ..., all dimensions but the last counted through in order) at most 36 rows name the same one
- route_weights: float32 [2, 2, 4096, 8], P('section', None, ('dp', 'expert')), may hold values from 0.06 to 0.2
- attn_gain: float32 [2, 1536], P('section'), may hold values from 0.5 to 1.5
- w_query: bfloat16 [2, 1536, 1536], P('section'), may hold values from -0.15625 to 0.15625
- key_projection_weight: bfloat16 [2, 1536, 512], P('section'), may hold values from -0.15625 to 0.15625
- value_projection_weight: bfloat16 [2, 1536, 512], P('section'), may hold values from -0.15625 to 0.15625
- w_out: bfloat16 [2, 1536, 1536], P('section'), may hold values from -0.625 to 0.625
- ffn_gain: float32 [2, 1536], P('section'), may hold values from 0.5 to 1.5
- w_gate: bfloat16 [2, 16, 1536, 512], P('section', 'expert', 'dp'), may hold values from -0.15625 to 0.15625
- w_up: bfloat16 [2, 16, 1536, 512], P('section', 'expert', 'dp'), may hold values from -0.15625 to 0.15625
- w_down: bfloat16 [2, 16, 512, 1536], P('section', 'expert', 'dp'), may hold values from -1 to 1
- out_grad: bfloat16 [2, 4096, 1536], P(None, ('dp', 'expert')), may hold values from -6 to 6
Outputs:
- layer_outputs: bfloat16 [2, 2, 4096, 1536], P('section', None, ('dp', 'expert'))
- input_grads: float32 [2, 2, 4096, 1536], P('section', None, ('dp', 'expert'))
- attn_gain_grad: float32 [2, 1536], P('section')
- w_query_grad: float32 [2, 1536, 1536], P('section')
- w_key_grad: float32 [2, 1536, 512], P('section')
- w_value_grad: float32 [2, 1536, 512], P('section')
- w_out_grad: float32 [2, 1536, 1536], P('section')
- ffn_gain_grad: float32 [2, 1536], P('section')
- w_gate_grad: float32 [2, 16, 1536, 512], P('section', 'expert', 'dp')
- w_up_grad: float32 [2, 16, 1536, 512], P('section', 'expert', 'dp')
- w_down_grad: float32 [2, 16, 512, 1536], P('section', 'expert', 'dp')
Inputs may be any that keep to these rules, and one draw needn't show every extreme that they name: `segments`: each sequence of 256 consecutive tokens holds three documents numbered 3 j, 3 j + 1, 3 j + 2 for the j-th sequence of a micro-batch, in that order; the first and last hold 1 to 32 tokens each. `expert_ids`: each row names 8 different experts; within the rows of one device of one layer and micro-batch no expert is named more than 36 times, a bound that some block reaches.
All inputs are finite; a program needn't handle non-finite values.
Results may differ from a plain program's by a relative error of at most 0.028.
Values may be sent and summed in bfloat16 or wider, within the bound.
No kernel may reach another device: no remote copies, remote signals or barrier semaphores. Data moves between devices by JAX's collectives and lax.ppermute only.
A program may use at most 256 MiB of HBM per device.

v0:
```python
import jax
import jax.numpy as jnp
from jax import lax
from jax.sharding import PartitionSpec as P

QUERY_HEADS = 24
KEY_VALUE_HEADS = 8
HEAD_SIZE = 64
CAP = 36


EPS = 1e-06


def passed_along(block, axis, distance):
    devices = range(lax.axis_size(axis))
    route = [(i - distance, i) for i in devices if i - distance in devices]
    return lax.ppermute(block, axis, route)


def norm_rows(values, gain):
    scale = lax.rsqrt(jnp.mean(values * values, -1, keepdims=True) + EPS)
    return (scale, values * scale * gain)


def norm_back(grad_normed, values, scale, gain):
    scaled = grad_normed * gain
    gain_grad = jnp.sum(grad_normed * values * scale, 0)
    inner = jnp.mean(scaled * values, -1, keepdims=True)
    return (scale * scaled - values * scale * scale * scale * inner, gain_grad)


def rotary_tables(place):
    half_size = HEAD_SIZE // 2
    frequency = 10000.0 ** (-jnp.arange(half_size, dtype=jnp.float32) * 2.0 / HEAD_SIZE)
    angles = place.astype(jnp.float32)[:, None] * frequency[None, :]
    angles = jnp.concatenate([angles, angles], -1)
    return (jnp.cos(angles), jnp.sin(angles))


def rotary_apply(values, cosine_table, sine_table):
    half_size = values.shape[-1] // 2
    turned = jnp.concatenate([-values[..., half_size:], values[..., :half_size]], -1)
    return values * cosine_table[:, None, :] + turned * sine_table[:, None, :]


def rotary_inverse(grads, cosine_table, sine_table):
    half_size = grads.shape[-1] // 2
    scaled = grads * sine_table[:, None, :]
    turned = jnp.concatenate([scaled[..., half_size:], -scaled[..., :half_size]], -1)
    return grads * cosine_table[:, None, :] + turned


def pick_item(array, index):
    return lax.dynamic_index_in_dim(array, index, 0, keepdims=False)


def query_places(token_count):
    return lax.axis_index("expert") * token_count + jnp.arange(token_count, dtype=jnp.int32)


def score_block(grouped_heads, every_key, allowed):
    raw_scores = jnp.einsum(
        "tkgd,skd->kgts", grouped_heads, every_key, preferred_element_type=jnp.float32
    )
    return jnp.where(allowed[None, None], raw_scores * 0.125, -1e30)


def route_slots(routes, total):
    flat = routes.reshape(-1)
    hits = (flat[:, None] == jnp.arange(total, dtype=jnp.int32)[None, :]).astype(jnp.int32)
    order = jnp.sum(hits * (jnp.cumsum(hits, 0) - 1), 1)
    return flat * CAP + order


def layer_forward(inputs, document_labels, routes, gates, dense, experts):
    attn_g, w_q, key_weight, value_weight, w_o, ffn_g = dense
    gate_all, up_all, down_all = experts
    token_count, width = inputs.shape
    query_groups = lax.axis_size("expert")
    local_experts = gate_all.shape[0]
    place = query_places(token_count)
    cosine_table, sine_table = rotary_tables(place)
    widened = inputs.astype(jnp.float32)
    scale_attn, normed_input = norm_rows(widened, attn_g)
    normed_input = normed_input.astype(jnp.bfloat16)
    query_rows = rotary_apply(
        jnp.dot(normed_input, w_q, preferred_element_type=jnp.float32).reshape(
            token_count, QUERY_HEADS, HEAD_SIZE
        ),
        cosine_table,
        sine_table,
    ).astype(jnp.bfloat16)
    keys_own = rotary_apply(
        jnp.dot(normed_input, key_weight, preferred_element_type=jnp.float32).reshape(
            token_count, KEY_VALUE_HEADS, HEAD_SIZE
        ),
        cosine_table,
        sine_table,
    ).astype(jnp.bfloat16)
    values_own = (
        jnp.dot(normed_input, value_weight, preferred_element_type=jnp.float32)
        .astype(jnp.bfloat16)
        .reshape(token_count, KEY_VALUE_HEADS, HEAD_SIZE)
    )
    label_low = document_labels.astype(jnp.bfloat16)
    every_key, every_value, key_labels = (
        lax.all_gather(keys_own, "expert", axis=0, tiled=True),
        lax.all_gather(values_own, "expert", axis=0, tiled=True),
        lax.all_gather(label_low, "expert", axis=0, tiled=True),
    )
    key_place = jnp.arange(every_key.shape[0], dtype=jnp.int32)
    allowed = (key_place[None, :] <= place[:, None]) & (key_labels[None, :] == label_low[:, None])
    grouped_heads = query_rows.reshape(
        token_count, KEY_VALUE_HEADS, QUERY_HEADS // KEY_VALUE_HEADS, HEAD_SIZE
    )
    scores = score_block(grouped_heads, every_key, allowed)
    peak = jnp.max(scores, -1, keepdims=True)
    log_total = peak + jnp.log(jnp.sum(jnp.exp(scores - peak), -1, keepdims=True))
    probs = jnp.exp(scores - log_total).astype(jnp.bfloat16)
    mixed_heads = jnp.einsum(
        "kgts,skd->tkgd", probs, every_value, preferred_element_type=jnp.float32
    )
    mixed_heads = mixed_heads.reshape(token_count, QUERY_HEADS * HEAD_SIZE).astype(jnp.bfloat16)
    after_attn = widened + jnp.dot(mixed_heads, w_o, preferred_element_type=jnp.float32)
    scale_ffn, normed_ffn = norm_rows(after_attn, ffn_g)
    normed_ffn = normed_ffn.astype(jnp.bfloat16)
    total_experts = query_groups * local_experts
    slots = route_slots(routes, total_experts)
    owner = (
        jnp.full((total_experts * CAP,), token_count, jnp.int32)
        .at[slots]
        .set(jnp.arange(slots.shape[0], dtype=jnp.int32) // routes.shape[1])
    )
    padded = jnp.concatenate([normed_ffn, jnp.zeros((1, width), jnp.bfloat16)], 0)
    outgoing = padded[owner].reshape(query_groups, local_experts, CAP, width)
    arrived = lax.all_to_all(outgoing, "expert", split_axis=0, concat_axis=2, tiled=True)[0]
    gate_pre = jnp.einsum("ecd,edf->ecf", arrived, gate_all, preferred_element_type=jnp.float32)
    up_pre = jnp.einsum("ecd,edf->ecf", arrived, up_all, preferred_element_type=jnp.float32)
    hidden_units = (jax.nn.silu(gate_pre) * up_pre).astype(jnp.bfloat16)
    produced = jnp.einsum(
        "ecf,efd->ecd", hidden_units, down_all, preferred_element_type=jnp.float32
    ).astype(jnp.bfloat16)
    returned = lax.all_to_all(
        produced[None], "expert", split_axis=2, concat_axis=0, tiled=True
    ).reshape(total_experts * CAP, width)
    picked = returned[slots].reshape(token_count, routes.shape[1], width)
    mixture = jnp.einsum("tk,tkd->td", gates, picked.astype(jnp.float32))
    result = (after_attn + mixture).astype(jnp.bfloat16)
    saved = (
        widened,
        scale_attn,
        normed_input,
        query_rows,
        every_key,
        every_value,
        allowed,
        log_total,
        mixed_heads,
        after_attn,
        scale_ffn,
        normed_ffn,
        slots,
        arrived,
        gate_pre,
        up_pre,
        hidden_units,
        gates,
    )
    return (result, saved)


def layer_backward(upstream, saved, dense, experts):
    attn_g, w_q, key_weight, value_weight, w_o, ffn_g = dense
    gate_all, up_all, down_all = experts
    (
        widened,
        scale_attn,
        normed_input,
        query_rows,
        every_key,
        every_value,
        allowed,
        log_total,
        mixed_heads,
        after_attn,
        scale_ffn,
        normed_ffn,
        slots,
        arrived,
        gate_pre,
        up_pre,
        hidden_units,
        gates,
    ) = saved
    token_count, width = upstream.shape
    query_groups = lax.axis_size("expert")
    local_experts = gate_all.shape[0]
    total_experts = query_groups * local_experts
    routed = (gates[:, :, None] * upstream[:, None, :]).astype(jnp.bfloat16).reshape(-1, width)
    route_buffer = jnp.zeros((total_experts * CAP, width), jnp.bfloat16).at[slots].set(routed)
    route_buffer = route_buffer.reshape(query_groups, local_experts, CAP, width)
    out_grads = lax.all_to_all(route_buffer, "expert", split_axis=0, concat_axis=2, tiled=True)[0]
    hidden_grad = jnp.einsum(
        "ecd,efd->ecf", out_grads, down_all, preferred_element_type=jnp.float32
    )
    down_grad = jnp.einsum(
        "ecf,ecd->efd", hidden_units, out_grads, preferred_element_type=jnp.float32
    )
    sigma = jax.nn.sigmoid(gate_pre)
    gate_grad = (hidden_grad * up_pre * sigma * (1.0 + gate_pre * (1.0 - sigma))).astype(
        jnp.bfloat16
    )
    up_grad = (hidden_grad * jax.nn.silu(gate_pre)).astype(jnp.bfloat16)
    gate_w_grad = jnp.einsum("ecd,ecf->edf", arrived, gate_grad, preferred_element_type=jnp.float32)
    up_w_grad = jnp.einsum("ecd,ecf->edf", arrived, up_grad, preferred_element_type=jnp.float32)
    slot_grads = jnp.einsum("ecf,edf->ecd", gate_grad, gate_all, preferred_element_type=jnp.float32)
    slot_grads = (
        slot_grads + jnp.einsum("ecf,edf->ecd", up_grad, up_all, preferred_element_type=jnp.float32)
    ).astype(jnp.bfloat16)
    token_side = lax.all_to_all(
        slot_grads[None], "expert", split_axis=2, concat_axis=0, tiled=True
    ).reshape(total_experts * CAP, width)
    normed_ffn_grad = jnp.sum(
        token_side[slots].reshape(token_count, -1, width).astype(jnp.float32), 1
    )
    norm_part, ffn_g_grad = norm_back(normed_ffn_grad, after_attn, scale_ffn, ffn_g)
    after_grad = upstream + norm_part
    attn_out_grad = after_grad.astype(jnp.bfloat16)
    w_o_grad = jnp.einsum(
        "tq,td->qd", mixed_heads, attn_out_grad, preferred_element_type=jnp.float32
    )
    mixed_heads_gradient = jnp.einsum(
        "td,qd->tq", attn_out_grad, w_o, preferred_element_type=jnp.float32
    ).astype(jnp.bfloat16)
    mixed_heads_gradient = mixed_heads_gradient.reshape(
        token_count, KEY_VALUE_HEADS, QUERY_HEADS // KEY_VALUE_HEADS, HEAD_SIZE
    )
    grouped_heads = query_rows.reshape(
        token_count, KEY_VALUE_HEADS, QUERY_HEADS // KEY_VALUE_HEADS, HEAD_SIZE
    )
    probs = jnp.exp(score_block(grouped_heads, every_key, allowed) - log_total)
    prob_grad = jnp.einsum(
        "tkgd,skd->kgts", mixed_heads_gradient, every_value, preferred_element_type=jnp.float32
    )
    centre = jnp.sum(probs * prob_grad, -1, keepdims=True)
    score_grad = (probs * (prob_grad - centre) * 0.125).astype(jnp.bfloat16)
    query_grad = jnp.einsum(
        "kgts,skd->tkgd", score_grad, every_key, preferred_element_type=jnp.float32
    ).reshape(token_count, QUERY_HEADS, HEAD_SIZE)
    key_grad_all = jnp.einsum(
        "kgts,tkgd->skd", score_grad, grouped_heads, preferred_element_type=jnp.float32
    )
    value_grad_all = jnp.einsum(
        "kgts,tkgd->skd",
        probs.astype(jnp.bfloat16),
        mixed_heads_gradient,
        preferred_element_type=jnp.float32,
    )
    key_gradient, value_gradient = (
        lax.psum_scatter(
            key_grad_all.astype(jnp.bfloat16), "expert", scatter_dimension=0, tiled=True
        ).astype(jnp.float32),
        lax.psum_scatter(
            value_grad_all.astype(jnp.bfloat16), "expert", scatter_dimension=0, tiled=True
        ).astype(jnp.float32),
    )
    cosine_table, sine_table = rotary_tables(query_places(token_count))
    query_pre = (
        rotary_inverse(query_grad, cosine_table, sine_table)
        .reshape(token_count, QUERY_HEADS * HEAD_SIZE)
        .astype(jnp.bfloat16)
    )
    key_unrotated = (
        rotary_inverse(key_gradient, cosine_table, sine_table)
        .reshape(token_count, KEY_VALUE_HEADS * HEAD_SIZE)
        .astype(jnp.bfloat16)
    )
    value_projected = value_gradient.reshape(token_count, KEY_VALUE_HEADS * HEAD_SIZE).astype(
        jnp.bfloat16
    )
    w_q_grad = jnp.einsum("td,tq->dq", normed_input, query_pre, preferred_element_type=jnp.float32)
    w_k_grad = jnp.einsum(
        "td,tq->dq", normed_input, key_unrotated, preferred_element_type=jnp.float32
    )
    w_v_grad = jnp.einsum(
        "td,tq->dq", normed_input, value_projected, preferred_element_type=jnp.float32
    )
    normed_grad = jnp.einsum("tq,dq->td", query_pre, w_q, preferred_element_type=jnp.float32)
    normed_grad = normed_grad + jnp.einsum(
        "tq,dq->td", key_unrotated, key_weight, preferred_element_type=jnp.float32
    )
    normed_grad = normed_grad + jnp.einsum(
        "tq,dq->td", value_projected, value_weight, preferred_element_type=jnp.float32
    )
    input_part, attn_g_grad = norm_back(normed_grad, widened, scale_attn, attn_g)
    input_grad = after_grad + input_part
    return (
        input_grad,
        (attn_g_grad, w_q_grad, w_k_grad, w_v_grad, w_o_grad, ffn_g_grad),
        (gate_w_grad, up_w_grad, down_grad),
    )


def masked(active, grads):
    return tuple((jnp.where(active, grad, jnp.zeros_like(grad)) for grad in grads))


def local(
    block_input,
    segments,
    expert_ids,
    route_weights,
    attn_gain,
    w_query,
    key_projection_weight,
    value_projection_weight,
    w_out,
    ffn_gain,
    w_gate,
    w_up,
    w_down,
    out_grad,
):
    sections = lax.axis_size("section")
    section = lax.axis_index("section")
    micro = block_input.shape[0]
    turns = micro + sections - 1
    dense = (
        attn_gain[0],
        w_query[0],
        key_projection_weight[0],
        value_projection_weight[0],
        w_out[0],
        ffn_gain[0],
    )
    experts = (
        lax.all_gather(w_gate[0], "dp", axis=1, tiled=True),
        lax.all_gather(w_up[0], "dp", axis=1, tiled=True),
        lax.all_gather(w_down[0], "dp", axis=1, tiled=True),
    )
    received = jnp.zeros(block_input.shape[1:], jnp.bfloat16)
    results = []
    kept = []
    for turn_index in range(turns):
        offset = turn_index - section
        batch = jnp.clip(offset, 0, micro - 1)
        inputs = jnp.where(section == 0, pick_item(block_input, batch), received)
        labels_now = pick_item(segments, batch)
        routes_now = pick_item(expert_ids[0], batch)
        gates_now = pick_item(route_weights[0], batch)
        output, saved = layer_forward(inputs, labels_now, routes_now, gates_now, dense, experts)
        results.append(output)
        kept.append(saved)
        if turn_index + 1 < turns:
            received = passed_along(output, "section", 1)
    layer_outputs = lax.dynamic_slice_in_dim(jnp.stack(results), section, micro, 0)[None]
    kept_all = jax.tree.map(lambda *leaves: jnp.stack(leaves), *kept)
    experts_back = (
        lax.all_gather(w_gate[0], "dp", axis=1, tiled=True),
        lax.all_gather(w_up[0], "dp", axis=1, tiled=True),
        lax.all_gather(w_down[0], "dp", axis=1, tiled=True),
    )
    dense_total = tuple((jnp.zeros(item.shape, jnp.float32) for item in dense))
    expert_total = tuple((jnp.zeros(item.shape, jnp.float32) for item in experts))
    expert_share = tuple(
        (jnp.zeros(item.shape, jnp.float32) for item in (w_gate[0], w_up[0], w_down[0]))
    )
    back_received = jnp.zeros(block_input.shape[1:], jnp.bfloat16)
    reverse = sections - 1 - section
    input_list = []
    for turn_index in range(turns):
        offset = turn_index - reverse
        batch = jnp.clip(offset, 0, micro - 1)
        active = (offset >= 0) & (offset < micro)
        upstream = jnp.where(
            section == sections - 1,
            pick_item(out_grad, batch).astype(jnp.float32),
            back_received.astype(jnp.float32),
        )
        saved = jax.tree.map(lambda leaf: pick_item(leaf, batch + section), kept_all)
        input_grad, dense_grads, expert_grads = layer_backward(upstream, saved, dense, experts_back)
        dense_grads = masked(active, dense_grads)
        expert_grads = masked(active, expert_grads)
        dense_total = tuple((total + grad for total, grad in zip(dense_total, dense_grads)))
        expert_total = tuple((total + grad for total, grad in zip(expert_total, expert_grads)))
        input_list.append(input_grad)
        if turn_index + 1 < turns:
            back_received = passed_along(input_grad.astype(jnp.bfloat16), "section", -1)
    expert_share = (
        lax.psum_scatter(
            expert_total[0].astype(jnp.bfloat16), "dp", scatter_dimension=1, tiled=True
        ).astype(jnp.float32),
        lax.psum_scatter(
            expert_total[1].astype(jnp.bfloat16), "dp", scatter_dimension=1, tiled=True
        ).astype(jnp.float32),
        lax.psum_scatter(
            expert_total[2].astype(jnp.bfloat16), "dp", scatter_dimension=1, tiled=True
        ).astype(jnp.float32),
    )
    input_grads = lax.dynamic_slice_in_dim(jnp.stack(input_list), reverse, micro, 0)[None]
    summed = lax.psum(
        (
            dense_total[0],
            dense_total[1],
            dense_total[2],
            dense_total[3],
            dense_total[4],
            dense_total[5],
        ),
        ("dp", "expert"),
    )
    return (
        layer_outputs,
        input_grads,
        summed[0][None],
        summed[1][None],
        summed[2][None],
        summed[3][None],
        summed[4][None],
        summed[5][None],
        expert_share[0][None],
        expert_share[1][None],
        expert_share[2][None],
    )


def solution(mesh):
    placed = (
        P(None, ("dp", "expert"), None),
        P(None, ("dp", "expert")),
        P("section", None, ("dp", "expert"), None),
        P("section", None, ("dp", "expert"), None),
        P("section", None),
        P("section", None, None),
        P("section", None, None),
        P("section", None, None),
        P("section", None, None),
        P("section", None),
        P("section", "expert", "dp", None),
        P("section", "expert", "dp", None),
        P("section", "expert", "dp", None),
        P(None, ("dp", "expert"), None),
    )
    return jax.shard_map(
        local,
        mesh=mesh,
        in_specs=placed,
        out_specs=(
            P("section", None, ("dp", "expert"), None),
            P("section", None, ("dp", "expert"), None),
            P("section", None),
            P("section", None, None),
            P("section", None, None),
            P("section", None, None),
            P("section", None, None),
            P("section", None),
            P("section", "expert", "dp", None),
            P("section", "expert", "dp", None),
            P("section", "expert", "dp", None),
        ),
        check_vma=False,
    )
```

profile of v0, /device:TPU:1, one launch (start us, length us, event | category | flops | bytes accessed | tf_op | source)
XLA Modules:
  0.0 1749.2 jit_solution(16203346791920953224)
XLA Ops:
  12.2 6.6 copy.211
  32.8 10.5 all-reduce.8
  43.3 10.8 all_gather.41
  54.1 10.7 all_gather.39
  84.7 18.4 %all_to_all.189 = bf16[4,4,36,1536]{3,1,2,0:T(4,128)(2,1)S(1)} all-to-all(bf16[4,4,36,1536]{3,1,2,0:T(4,128)(2,1)S(1)} %copy.219), channel_id=1, replica_groups=mesh['section'=2,'dp'=16,'expert'=4] {'expert'}, dimensions={0} | all-to-all | bytes 3538944 | tf_op jit(solution)/shard_map/all_to_all | solution.py:137
  114.2 31.1 %all-gather.14.cloned.1.call-done = bf16[1,4,512,1536]{3,2,1,0:T(8,128)(2,1)} async-done(((bf16[1,4,32,1536]{3,2,1,0:T(8,128)(2,1)}), bf16[1,4,512,1536]{3,2,1,0:T(8,128)(2,1)}) %all-gather.14.cloned.1.call-update) | async-done | bytes 6291472 | tf_op jit(solution)/shard_map/all_gather | solution.py:340
  164.5 14.2 all-to-all-done.1
  203.0 11.3 all_gather.47
  217.6 10.6 all_gather.45
  289.9 8.3 all-to-all-done.3
  325.7 9.9 all_gather.50
  341.1 10.1 all_gather.48
  483.3 32.5 %reduce-scatter.28.cloned.1.call-done = bf16[64,512]{1,0:T(8,128)(2,1)} async-done(((bf16[256,512]{1,0:T(8,128)(2,1)}), bf16[64,512]{1,0:T(8,128)(2,1)}) %reduce-scatter.28.cloned.1.call-update) | async-done | bytes 65552
  523.8 14.9 reduce-scatter.30.cloned.1.call-done
  561.0 21.3 %all_to_all.190 = bf16[4,4,36,1536]{3,1,2,0:T(4,128)(2,1)S(1)} all-to-all(bf16[4,4,36,1536]{3,1,2,0:T(4,128)(2,1)S(1)} %copy.265), channel_id=1, replica_groups=mesh['section'=2,'dp'=16,'expert'=4] {'expert'}, dimensions={0} | all-to-all | bytes 3538944 | tf_op jit(solution)/shard_map/all_to_all | solution.py:203
  606.7 10.3 all-to-all-done.9
  648.3 17.8 %reduce-scatter.32.cloned.1.call-done = bf16[64,512]{1,0:T(8,128)(2,1)} async-done(((bf16[256,512]{1,0:T(8,128)(2,1)}), bf16[64,512]{1,0:T(8,128)(2,1)}) %reduce-scatter.32.cloned.1.call-update) | async-done | bytes 65552
  675.1 14.0 reduce-scatter.34.cloned.1.call-done
  721.4 11.7 all-to-all-done.10
  768.1 6.5 fusion.138
  799.6 7.8 fusion.134
  810.6 11.5 add_convert_fusion.2
  822.2 8.2 fusion.136
  830.3 6.6 fusion.132
  836.9 10.2 add_convert_fusion.1
  849.7 8.1 fusion.199
  857.8 6.6 fusion.196
  864.4 7.9 add_convert_fusion
  935.0 17.2 all-to-all-done.5
  969.9 277.9 %all-reduce.6 = (f32[1,1536]{1,0:T(1,128)}, f32[1,1536]{1,0:T(1,128)}) all-reduce(f32[1,1536]{1,0:T(1,128)} %broadcast_in_dim.118, f32[1,1536]{1,0:T(1,128)S(1)} %broadcast_in_dim.123), channel_id=1, replica_groups=mesh['section'=2,'dp'=16,'expert'=4] {'dp','expert'}, use_global_device_ids=true, to_apply=%region_48.49 | all-reduce | flops 3072 | bytes 24576 | tf_op jit(solution)/shard_map/psum | solution.py:402
  1256.6 468.0 %all-reduce.11.cloned.1.call-done = (f32[1,1536,1536]{2,1,0:T(8,128)}, f32[1,1536,512]{2,1,0:T(8,128)}, f32[1,1536,512]{2,1,0:T(8,128)}, f32[1,1536,1536]{2,1,0:T(8,128)}) async-done(((f32[1,1536,1536]{2,1,0:T(8,128)}, f32[1,1536,512]{2,1,0:T(8,128)}, f32[1,1536,512]{2,1,0:T(8,128)}, f32[1,1536,1536]{2,1,0:T(8,128)}), (f32[1,1536,1536]{2,1,0:T(8,128)}, f32[1,1536,512]{2,1,0:T(8,128)}, ...) | async-done | bytes 25165840 | tf_op jit(solution)/shard_map/psum | solution.py:402
  1724.6 9.4 copy.469
  (864 shorter events, 610.8 us)
Async XLA Ops:
  7.2 95.9 %all-gather.10.cloned.1.call-start = ((), (), s32[]{:S(2)}) async-start(), calls=%async_computation.24 | async-start | bytes 6684672 | tf_op jit(solution)/shard_map/all_gather | solution.py:338
  7.9 100.7 %all-gather.12.cloned.1.call-start = ((), (), s32[]{:S(2)}) async-start(), calls=%async_computation.25 | async-start | bytes 6684672 | tf_op jit(solution)/shard_map/all_gather | solution.py:339
  8.7 136.6 %all-gather.14.cloned.1.call-start = ((), (), s32[]{:S(2)}) async-start(), calls=%async_computation.26 | async-start | bytes 6684672 | tf_op jit(solution)/shard_map/all_gather | solution.py:340
  20.7 670.7 %copy-start.118 = (f32[1536]{0:T(1024)}, f32[1536]{0:T(1024)S(1)}, u32[]{:S(2)}) copy-start(f32[1536]{0:T(1024)S(1)} %reduce) | copy-start | bytes 18436
  21.0 48.9 %copy-start.42 = (f32[64,64]{0,1:T(8,128)}, f32[64,64]{0,1:T(8,128)S(1)}, u32[]{:S(2)}) copy-start(f32[64,64]{0,1:T(8,128)S(1)} %get-tuple-element.94) | copy-start | bytes 49156
  152.0 26.7 %all-to-all-start.1 = ((bf16[1,4,144,1536]{3,1,0,2:T(4,128)(2,1)}), bf16[1,4,144,1536]{3,1,0,2:T(4,128)(2,1)S(1)}, u32[]{:S(2)}, u32[]{:S(2)}) async-start(bf16[1,4,144,1536]{3,1,0,2:T(4,128)(2,1)} %copy.222), calls=%async_computation.1 | async-start | bytes 3538944 | tf_op jit(solution)/shard_map/all_to_all | solution.py:144
  187.7 7.1 collective-permute-start
  244.8 20.3 %all-to-all-start.2 = ((bf16[4,4,36,1536]{3,1,2,0:T(4,128)(2,1)}), bf16[4,4,36,1536]{3,1,2,0:T(4,128)(2,1)S(1)}, u32[]{:S(2)}, u32[]{:S(2)}) async-start(bf16[4,4,36,1536]{3,1,2,0:T(4,128)(2,1)} %copy.232), calls=%async_computation.2 | async-start | bytes 3538944 | tf_op jit(solution)/shard_map/all_to_all | solution.py:137
  279.0 19.2 %all-to-all-start.3 = ((bf16[1,4,144,1536]{3,1,0,2:T(4,128)(2,1)}), bf16[1,4,144,1536]{3,1,0,2:T(4,128)(2,1)S(1)}, u32[]{:S(2)}, u32[]{:S(2)}) async-start(bf16[1,4,144,1536]{3,1,0,2:T(4,128)(2,1)} %copy.235), calls=%async_computation.3 | async-start | bytes 3538944 | tf_op jit(solution)/shard_map/all_to_all | solution.py:144
  307.4 8.5 collective-permute-start.1
  367.8 26.6 %all-to-all-start.4 = ((bf16[4,4,36,1536]{3,1,2,0:T(4,128)(2,1)}), bf16[4,4,36,1536]{3,1,2,0:T(4,128)(2,1)S(1)}, u32[]{:S(2)}, u32[]{:S(2)}) async-start(bf16[4,4,36,1536]{3,1,2,0:T(4,128)(2,1)} %copy.245), calls=%async_computation.4 | async-start | bytes 3538944 | tf_op jit(solution)/shard_map/all_to_all | solution.py:137
  394.4 18.1 %all-to-all-start.6 = ((bf16[4,4,36,1536]{3,1,2,0:T(4,128)(2,1)}), bf16[4,4,36,1536]{3,1,2,0:T(4,128)(2,1)}, u32[]{:S(2)}, u32[]{:S(2)}) async-start(bf16[4,4,36,1536]{3,1,2,0:T(4,128)(2,1)} %copy.254), calls=%async_computation.6 | async-start | bytes 3538944 | tf_op jit(solution)/shard_map/all_to_all | solution.py:203
  431.7 18.5 %all-to-all-start.7 = ((bf16[1,4,144,1536]{3,1,0,2:T(4,128)(2,1)}), bf16[1,4,144,1536]{3,1,0,2:T(4,128)(2,1)S(1)}, u32[]{:S(2)}, u32[]{:S(2)}) async-start(bf16[1,4,144,1536]{3,1,0,2:T(4,128)(2,1)} %copy.256), calls=%async_computation.7 | async-start | bytes 3538944 | tf_op jit(solution)/shard_map/all_to_all | solution.py:221
  435.9 79.9 %reduce-scatter.28.cloned.1.call-start = ((), (), s32[]{:S(2)}) async-start(), calls=%async_computation.27 | async-start | bytes 327680
  479.3 59.4 %reduce-scatter.30.cloned.1.call-start = ((), (), s32[]{:S(2)}) async-start(), calls=%async_computation.28 | async-start | bytes 327680 | tf_op jit(solution)/shard_map/convert_element_type | solution.py:279
  543.3 8.1 collective-permute-start.2
  595.8 21.1 %all-to-all-start.9 = ((bf16[1,4,144,1536]{3,1,0,2:T(4,128)(2,1)}), bf16[1,4,144,1536]{3,1,0,2:T(4,128)(2,1)S(1)}, u32[]{:S(2)}, u32[]{:S(2)}) async-start(bf16[1,4,144,1536]{3,1,0,2:T(4,128)(2,1)} %copy.267), calls=%async_computation.9 | async-start | bytes 3538944 | tf_op jit(solution)/shard_map/all_to_all | solution.py:221
  599.5 66.6 %reduce-scatter.32.cloned.1.call-start = ((), (), s32[]{:S(2)}) async-start(), calls=%async_computation.29 | async-start | bytes 327680
  627.4 64.0 %copy-start.26 = (f32[64,1536]{1,0:T(8,128)}, f32[64,1536]{1,0:T(8,128)S(1)}, u32[]{:S(2)}) copy-start(f32[64,1536]{1,0:T(8,128)S(1)} %fusion.336) | copy-start | bytes 1179652
  644.0 45.1 %reduce-scatter.34.cloned.1.call-start = ((), (), s32[]{:S(2)}) async-start(), calls=%async_computation.30 | async-start | bytes 327680 | tf_op jit(solution)/shard_map/convert_element_type | solution.py:279
  692.4 8.1 collective-permute-start.3
  710.7 22.4 %all-to-all-start.10 = ((bf16[4,4,36,1536]{3,1,2,0:T(4,128)(2,1)}), bf16[4,4,36,1536]{3,1,2,0:T(4,128)(2,1)S(1)}, u32[]{:S(2)}, u32[]{:S(2)}) async-start(bf16[4,4,36,1536]{3,1,2,0:T(4,128)(2,1)} %copy.276), calls=%async_computation.10 | async-start | bytes 3538944 | tf_op jit(solution)/shard_map/all_to_all | solution.py:203
  752.5 22.1 %all-to-all-start.11 = ((bf16[1,4,144,1536]{3,1,0,2:T(4,128)(2,1)}), bf16[1,4,144,1536]{3,1,0,2:T(4,128)(2,1)}, u32[]{:S(2)}, u32[]{:S(2)}) async-start(bf16[1,4,144,1536]{3,1,0,2:T(4,128)(2,1)} %copy.278), calls=%async_computation.11 | async-start | bytes 3538944 | tf_op jit(solution)/shard_map/all_to_all | solution.py:221
  757.0 156.1 %reduce-scatter.36.cloned.1.call-start = ((), (), s32[]{:S(2)}) async-start(), calls=%async_computation.31 | async-start | bytes 327680
  799.5 118.8 %reduce-scatter.38.cloned.1.call-start = ((), (), s32[]{:S(2)}) async-start(), calls=%async_computation.32 | async-start | bytes 327680 | tf_op jit(solution)/shard_map/convert_element_type | solution.py:279
  810.2 440.5 %reduce-scatter.22.cloned.1.call-start = ((), (), s32[]{:S(2)}) async-start(), calls=%async_computation.21 | async-start | bytes 6684672 | tf_op jit(solution)/shard_map/reduce_scatter | solution.py:391
  822.1 430.5 %reduce-scatter.24.cloned.1.call-start = ((), (), s32[]{:S(2)}) async-start(), calls=%async_computation.22 | async-start | bytes 6684672 | tf_op jit(solution)/shard_map/reduce_scatter | solution.py:394
  847.2 407.4 %reduce-scatter.26.cloned.1.call-start = ((), (), s32[]{:S(2)}) async-start(), calls=%async_computation.23 | async-start | bytes 6684672 | tf_op jit(solution)/shard_map/reduce_scatter | solution.py:397
  872.4 852.2 %all-reduce.11.cloned.1.call-start = ((), (), s32[]{:S(2)}) async-start(), calls=%async_computation.33 | async-start | bytes 50331648 | tf_op jit(solution)/shard_map/psum | solution.py:402
  930.5 21.8 %all-to-all-start.5 = ((bf16[1,4,144,1536]{3,1,0,2:T(4,128)(2,1)}), bf16[1,4,144,1536]{3,1,0,2:T(4,128)(2,1)S(1)}, u32[]{:S(2)}, u32[]{:S(2)}) async-start(bf16[1,4,144,1536]{3,1,0,2:T(4,128)(2,1)} %copy.248), calls=%async_computation.5 | async-start | bytes 3538944 | tf_op jit(solution)/shard_map/all_to_all | solution.py:144
  967.2 281.3 %copy-start.41 = (f32[64,1536]{1,0:T(8,128)S(1)}, f32[64,1536]{1,0:T(8,128)}, u32[]{:S(2)}) copy-start(f32[64,1536]{1,0:T(8,128)} %copy-done.39) | copy-start | bytes 1179652
  967.3 282.4 %copy-start.121 = (f32[64,1536]{1,0:T(8,128)S(1)}, f32[64,1536]{1,0:T(8,128)}, u32[]{:S(2)}) copy-start(f32[64,1536]{1,0:T(8,128)} %get-tuple-element.33) | copy-start | bytes 1179652
  (222 other events, 1438.4 us)
Sparse Core Ops, SparseCore 0:
  9.7 45.9 all-gather.9
  57.4 43.0 all-gather.11
  102.2 43.0 all-gather.13
  479.4 36.3 reduce-scatter.27
  518.1 20.5 reduce-scatter.29
  644.1 21.9 reduce-scatter.31
  668.6 20.4 reduce-scatter.33
  799.6 23.0 reduce-scatter.35
  825.2 20.4 reduce-scatter.37
  848.0 78.4 reduce-scatter.21
  928.9 77.4 reduce-scatter.23
  1008.6 77.0 reduce-scatter.25
  1089.1 635.4 all-reduce.10
where the time goes:
time: 1760 us; the launch traced here: 1750 us
  waiting for transfers between devices  658 us (37%)
  blocking collectives  391 us (22%)
  matrix products  307 us (17%)
  local copies, waits for them, and re-layouts  214 us (12%)
  other arithmetic  106 us (6%)
  starting transfers between devices  55.7 us (3%)
  between operations  17.7 us (1%)
    psum x1, waiting for transfers between devices, local(): lax.psum((dense_total[0], dense_total[1], dense_total[2], dense_total[3],...  468 us
    psum x1, blocking collectives, local(): lax.psum((dense_total[0], dense_total[1], dense_total[2], dense_total[3],...  278 us
    unnamed x474, local copies, waits for them, and re-layouts  57 us
    unnamed x16, waiting for transfers between devices  52.5 us
    all_to_all x3, waiting for transfers between devices, layer_forward(): lax.all_to_all(produced[None], 'expert', split_axis=2, concat_axis=0, til...  39.7 us
  transfers between devices with their start and end apart: 27, of which 15 were waited for; matrix products, arithmetic and copies ran while one was open for 19% of the time, Pallas kernels for 0%

commit v1 on v0

v1 whole, which is shorter than its diff:
```python
import functools

import jax
import jax.numpy as jnp
from jax import lax
from jax.experimental import pallas as pl
from jax.experimental.pallas import tpu as pltpu
from jax.sharding import PartitionSpec as P

QUERY_HEADS = 24
KEY_VALUE_HEADS = 8
HEAD_SIZE = 64
GROUP = QUERY_HEADS // KEY_VALUE_HEADS
EPS = 1e-06
LOW = jnp.bfloat16
F32 = jnp.float32
VMEM_BYTES = 56 * 1024 * 1024


def params(*semantics):
    return pltpu.CompilerParams(dimension_semantics=semantics, vmem_limit_bytes=VMEM_BYTES)


def dot(left, right):
    return jnp.dot(left, right, preferred_element_type=F32)


def dot_nt(left, right):
    return lax.dot_general(left, right, (((1,), (1,)), ((), ())), preferred_element_type=F32)


def dot_tn(left, right):
    return lax.dot_general(left, right, (((0,), (0,)), ((), ())), preferred_element_type=F32)


def shifted(block, by):
    size = lax.axis_size("expert")
    return lax.ppermute(block, "expert", [(i, (i + by) % size) for i in range(size)])


def gather_group(block):
    size = lax.axis_size("expert")
    return jnp.concatenate([block] + [shifted(block, j) for j in range(1, size)], 1)


def sum_to_owners(partial, tokens):
    size = lax.axis_size("expert")
    total = partial[:, :tokens].astype(F32)
    for j in range(1, size):
        total = total + shifted(partial[:, j * tokens : (j + 1) * tokens], size - j).astype(F32)
    return total


def to_section(block, target):
    return lax.ppermute(block, "section", [(1 - target, target)])


RING, PAIR, CORES = 4, 2, 2


def moved(block, x=0, y=0, core=0):
    route = []
    for i in range(RING):
        for j in range(PAIR):
            for k in range(CORES):
                target = ((i + x) % RING * PAIR + (j + y) % PAIR) * CORES + (k + core) % CORES
                route.append(((i * PAIR + j) * CORES + k, target))
    return lax.ppermute(block, "dp", route)


def added(*terms):
    total = terms[0].astype(F32)
    for term in terms[1:]:
        total = total + term.astype(F32)
    return total


def ring_sum(blocks):
    flat = blocks.reshape((2 * RING,) + blocks.shape[2:])
    from_below = moved(flat[3:5], x=1)
    from_above = moved(flat[5:7], x=-1)
    below = moved(added(flat[2], from_below[1]).astype(LOW), x=1)
    above = moved(added(flat[7], from_above[0]).astype(LOW), x=-1)
    return added(flat[0], from_above[1], below), added(flat[1], from_below[0], above)


def ring_first_sum(blocks):
    first, second = ring_sum(blocks)
    away = jnp.stack([first[1], second[1]]).astype(LOW)
    return added(jnp.stack([first[0], second[0]]), moved(away, y=1))


def pair_first_sum(blocks):
    return jnp.stack(ring_sum(added(blocks[0], moved(blocks[1], y=1)).astype(LOW)))


def ring_gather(block):
    below, above = moved(block, x=1), moved(block, x=-1)
    across = jnp.stack([moved(below[0], x=1), moved(above[1], x=-1)])
    return jnp.stack([block, below, across, above])


def pair_gather(block):
    return jnp.stack([block, moved(block, y=1)])


def group_stack(block):
    return jnp.stack([block] + [shifted(block, j) for j in range(1, lax.axis_size("expert"))])


def sum_everywhere(values):
    for axis in ("dp", "expert"):
        size, bit = lax.axis_size(axis), 1
        while bit < size:
            values = values + lax.ppermute(values, axis, [(i, i ^ bit) for i in range(size)])
            bit *= 2
    return values


def swap_halves(values):
    half = HEAD_SIZE // 2
    lanes = values.shape[-1]
    lane = lax.broadcasted_iota(jnp.int32, values.shape, values.ndim - 1)
    ahead = pltpu.roll(values, lanes - half, values.ndim - 1)
    behind = pltpu.roll(values, half, values.ndim - 1)
    return jnp.where(lane % HEAD_SIZE < half, ahead, behind)


def widen_table(table, lanes):
    return jnp.concatenate([table] * (lanes // table.shape[-1]), -1)


def project_kernel(query_steps, x_ref, gain_ref, wq_ref, wk_ref, wv_ref, cos_ref, sin_ref, out_ref, xn_ref):
    step = pl.program_id(0)

    @pl.when(step == 0)
    def _():
        wide = x_ref[...].astype(F32)
        scale = lax.rsqrt(jnp.mean(wide * wide, -1, keepdims=True) + EPS)
        xn_ref[...] = (wide * scale * gain_ref[...]).astype(LOW)

    def turned(weight):
        product = dot(xn_ref[...], weight)
        lanes = product.shape[-1]
        cos, sin = widen_table(cos_ref[...], lanes), widen_table(sin_ref[...], lanes)
        return (product * cos + swap_halves(product) * sin).astype(LOW)

    @pl.when(step < query_steps)
    def _():
        out_ref[...] = turned(wq_ref[...])

    @pl.when(step == query_steps)
    def _():
        out_ref[...] = turned(wk_ref[...])

    @pl.when(step == query_steps + 1)
    def _():
        out_ref[...] = dot(xn_ref[...], wv_ref[...]).astype(LOW)


def project(x, gain, wq, wk, wv, cos, sin):
    rows, width = x.shape
    lanes = wk.shape[1]
    query_steps = wq.shape[1] // lanes
    whole = lambda *shape: pl.BlockSpec(shape, lambda i: (0,) * len(shape))
    return pl.pallas_call(
        functools.partial(project_kernel, query_steps),
        grid=(query_steps + 2,),
        in_specs=[
            whole(rows, width),
            whole(1, width),
            pl.BlockSpec((width, lanes), lambda i: (0, jnp.minimum(i, query_steps - 1))),
            whole(width, lanes),
            whole(width, lanes),
            whole(rows, cos.shape[1]),
            whole(rows, cos.shape[1]),
        ],
        out_specs=[pl.BlockSpec((rows, lanes), lambda i: (0, i)), whole(rows, width)],
        out_shape=[
            jax.ShapeDtypeStruct((rows, lanes * (query_steps + 2)), LOW),
            jax.ShapeDtypeStruct((rows, width), LOW),
        ],
        compiler_params=params("arbitrary"),
        cost_estimate=pl.CostEstimate(
            flops=2 * rows * width * lanes * (query_steps + 2),
            bytes_accessed=2 * width * lanes * (query_steps + 2) + 8 * rows * width,
            transcendentals=0,
        ),
        name="project",
    )(x, gain, wq, wk, wv, cos, sin)


def head(values, index):
    return values[:, index * HEAD_SIZE : (index + 1) * HEAD_SIZE]


def softmax_parts(stacked_q, key, allowed):
    scores = jnp.where(allowed, dot_nt(stacked_q, key) * 0.125, -1e30)
    raised = jnp.exp(scores - jnp.max(scores, -1, keepdims=True))
    return raised / jnp.sum(raised, -1, keepdims=True)


def allowed_mask(place_col, place_row, label_col, label_row):
    one = (place_row <= place_col) & (label_row == label_col)
    return jnp.concatenate([one] * GROUP, 0)


def attend_kernel(
    q_ref, k_ref, v_ref, pc_ref, pr_ref, lc_ref, lr_ref, x_ref, wo_ref, gain_ref,
    o_ref, h1_ref, xn2_ref, total_ref,
):
    chunk = pl.program_id(1)
    allowed = allowed_mask(pc_ref[...], pr_ref[...], lc_ref[0], lr_ref[0])
    q, k, v = q_ref[0], k_ref[0], v_ref[0]
    rows = q.shape[0]
    mixed = []
    for pair in range(k.shape[1] // HEAD_SIZE):
        stacked = jnp.concatenate([head(q, pair * GROUP + j) for j in range(GROUP)], 0)
        probs = softmax_parts(stacked, head(k, pair), allowed).astype(LOW)
        out = dot(probs, head(v, pair))
        mixed += [out[j * rows : (j + 1) * rows] for j in range(GROUP)]
    mixed = jnp.concatenate(mixed, -1).astype(LOW)
    o_ref[0] = mixed
    part = dot(mixed, wo_ref[...])

    @pl.when(chunk == 0)
    def _():
        total_ref[...] = x_ref[0].astype(F32) + part

    @pl.when(chunk > 0)
    def _():
        total_ref[...] += part

    @pl.when(chunk == pl.num_programs(1) - 1)
    def _():
        total = total_ref[...]
        scale = lax.rsqrt(jnp.mean(total * total, -1, keepdims=True) + EPS)
        h1_ref[0] = total[: h1_ref.shape[1]]
        xn2_ref[0] = (total * scale * gain_ref[...]).astype(LOW)


def attend(qkv, x, wo, gain, marks, parts, own):
    batches, rows, width = x.shape
    place_col, place_row, label_col, label_row = marks
    q_lanes, k_lanes = wo.shape[0] // parts, KEY_VALUE_HEADS * HEAD_SIZE // parts
    k_at = wo.shape[0] // k_lanes
    full = lambda *shape: pl.BlockSpec(shape, lambda b, c: (0,) * len(shape))
    batch = lambda *shape: pl.BlockSpec((1,) + shape, lambda b, c: (b, 0, 0))
    return pl.pallas_call(
        attend_kernel,
        grid=(batches, parts),
        in_specs=[
            pl.BlockSpec((1, rows, q_lanes), lambda b, c: (b, 0, c)),
            pl.BlockSpec((1, rows, k_lanes), lambda b, c: (b, 0, k_at + c)),
            pl.BlockSpec((1, rows, k_lanes), lambda b, c: (b, 0, k_at + parts + c)),
            full(rows, 1),
            full(1, rows),
            batch(rows, 1),
            batch(1, rows),
            batch(rows, width),
            pl.BlockSpec((q_lanes, width), lambda b, c: (c, 0)),
            full(1, width),
        ],
        out_specs=[
            pl.BlockSpec((1, rows, q_lanes), lambda b, c: (b, 0, c)),
            batch(own, width),
            batch(rows, width),
        ],
        out_shape=[
            jax.ShapeDtypeStruct((batches, rows, wo.shape[0]), LOW),
            jax.ShapeDtypeStruct((batches, own, width), F32),
            jax.ShapeDtypeStruct((batches, rows, width), LOW),
        ],
        scratch_shapes=[pltpu.VMEM((rows, width), F32)],
        compiler_params=params("arbitrary", "arbitrary"),
        cost_estimate=pl.CostEstimate(
            flops=2 * batches * rows * width * wo.shape[0] + 16 * batches * rows * rows * wo.shape[0],
            bytes_accessed=4 * width * wo.shape[0] + 12 * batches * rows * width,
            transcendentals=batches * rows * rows * QUERY_HEADS,
        ),
        name="attend",
    )(qkv, qkv, qkv, place_col, place_row, label_col, label_row, x, wo, gain)


def expert_hidden(xn_ref, share_ref, wg_ref, wu_ref):
    gate, up = dot(xn_ref[...], wg_ref[0]), dot(xn_ref[...], wu_ref[0])
    share = share_ref[0]
    sigma = jax.nn.sigmoid(gate)
    silu = gate * sigma
    return gate, up, share, sigma, silu


def experts_forward_kernel(xn_ref, share_ref, wg_ref, wu_ref, wd_ref, out_ref, total_ref):
    step = pl.program_id(0)
    _, up, share, _, silu = expert_hidden(xn_ref, share_ref, wg_ref, wu_ref)
    part = dot((silu * up * share).astype(LOW), wd_ref[0])

    @pl.when(step == 0)
    def _():
        total_ref[...] = part

    @pl.when(step > 0)
    def _():
        total_ref[...] += part

    @pl.when(step == pl.num_programs(0) - 1)
    def _():
        out_ref[...] = total_ref[...].astype(LOW)


def experts_keep_kernel(xn_ref, share_ref, wg_ref, wu_ref, hidden_ref, to_up_ref, to_gate_ref):
    gate, up, share, sigma, silu = expert_hidden(xn_ref, share_ref, wg_ref, wu_ref)
    shared = silu * share
    hidden_ref[...] = (shared * up).astype(LOW)
    to_up_ref[...] = shared.astype(LOW)
    to_gate_ref[...] = (share * up * sigma * (1.0 + gate * (1.0 - sigma))).astype(LOW)


def expert_specs(rows, width, units):
    return [
        pl.BlockSpec((rows, width), lambda e: (0, 0)),
        pl.BlockSpec((1, rows, 1), lambda e: (e, 0, 0)),
        pl.BlockSpec((1, width, units), lambda e: (e, 0, 0)),
        pl.BlockSpec((1, width, units), lambda e: (e, 0, 0)),
    ]


def experts_forward(xn, share, wg, wu, wd):
    rows, width = xn.shape
    count, _, units = wg.shape
    return pl.pallas_call(
        experts_forward_kernel,
        grid=(count,),
        in_specs=expert_specs(rows, width, units)
        + [pl.BlockSpec((1, units, width), lambda e: (e, 0, 0))],
        out_specs=pl.BlockSpec((rows, width), lambda e: (0, 0)),
        out_shape=jax.ShapeDtypeStruct((rows, width), LOW),
        scratch_shapes=[pltpu.VMEM((rows, width), F32)],
        compiler_params=params("arbitrary"),
        cost_estimate=pl.CostEstimate(
            flops=6 * rows * width * units * count,
            bytes_accessed=6 * width * units * count,
            transcendentals=rows * units * count,
        ),
        name="experts_forward",
    )(xn, share, wg, wu, wd)


def experts_keep(xn, share, wg, wu):
    rows, width = xn.shape
    count, _, units = wg.shape
    kept = pl.BlockSpec((rows, units), lambda e: (0, e))
    return pl.pallas_call(
        experts_keep_kernel,
        grid=(count,),
        in_specs=expert_specs(rows, width, units),
        out_specs=[kept] * 3,
        out_shape=[jax.ShapeDtypeStruct((rows, units * count), LOW)] * 3,
        compiler_params=params("arbitrary"),
        cost_estimate=pl.CostEstimate(
            flops=4 * rows * width * units * count,
            bytes_accessed=4 * width * units * count,
            transcendentals=rows * units * count,
        ),
        name="experts_keep",
    )(xn, share, wg, wu)


def experts_backward_kernel(c_ref, up_ref, gate_ref, wg_ref, wu_ref, wd_ref, *refs):
    out_ref, total_ref = refs[0], refs[-1]
    step = pl.program_id(0)
    hidden = dot_nt(c_ref[...], wd_ref[0])
    gate_grad = (hidden * gate_ref[...].astype(F32)).astype(LOW)
    up_grad = (hidden * up_ref[...].astype(F32)).astype(LOW)
    if len(refs) == 4:
        refs[1][...] = gate_grad
        refs[2][...] = up_grad
    part = dot_nt(gate_grad, wg_ref[0]) + dot_nt(up_grad, wu_ref[0])

    @pl.when(step == 0)
    def _():
        total_ref[...] = part

    @pl.when(step > 0)
    def _():
        total_ref[...] += part

    @pl.when(step == pl.num_programs(0) - 1)
    def _():
        out_ref[...] = total_ref[...].astype(LOW)


def experts_backward(c, to_up, to_gate, wg, wu, wd, keep):
    rows, width = c.shape
    count, _, units = wg.shape
    kept = pl.BlockSpec((rows, units), lambda e: (0, e))
    kept_shape = jax.ShapeDtypeStruct((rows, units * count), LOW)
    return pl.pallas_call(
        experts_backward_kernel,
        grid=(count,),
        in_specs=[
            pl.BlockSpec((rows, width), lambda e: (0, 0)),
            kept,
            kept,
            pl.BlockSpec((1, width, units), lambda e: (e, 0, 0)),
            pl.BlockSpec((1, width, units), lambda e: (e, 0, 0)),
            pl.BlockSpec((1, units, width), lambda e: (e, 0, 0)),
        ],
        out_specs=[pl.BlockSpec((rows, width), lambda e: (0, 0))] + [kept, kept] * keep,
        out_shape=[jax.ShapeDtypeStruct((rows, width), LOW)] + [kept_shape, kept_shape] * keep,
        scratch_shapes=[pltpu.VMEM((rows, width), F32)],
        compiler_params=params("arbitrary"),
        cost_estimate=pl.CostEstimate(
            flops=6 * rows * width * units * count,
            bytes_accessed=6 * width * units * count,
            transcendentals=0,
        ),
        name="experts_backward",
    )(c, to_up, to_gate, wg, wu, wd)


def attend_backward_kernel(
    z_ref, q_ref, k_ref, v_ref, da_ref, wo_ref, wq_ref, wk_ref, wv_ref,
    pc_ref, pr_ref, lc_ref, lr_ref, cos_ref, sin_ref,
    dqkv_ref, dn_ref,
):
    del z_ref
    allowed = allowed_mask(pc_ref[...], pr_ref[...], lc_ref[0], lr_ref[0])
    q, k, v = q_ref[0], k_ref[0], v_ref[0]
    rows = q.shape[0]
    dout = dot_nt(da_ref[0], wo_ref[...]).astype(LOW)
    dqs, dks, dvs = [], [], []
    for pair in range(k.shape[1] // HEAD_SIZE):
        key, value = head(k, pair), head(v, pair)
        queries = jnp.concatenate([head(q, pair * GROUP + j) for j in range(GROUP)], 0)
        douts = jnp.concatenate([head(dout, pair * GROUP + j) for j in range(GROUP)], 0)
        probs = softmax_parts(queries, key, allowed)
        dprobs = dot_nt(douts, value)
        centre = jnp.sum(probs * dprobs, -1, keepdims=True)
        dscores = (probs * (dprobs - centre) * 0.125).astype(LOW)
        dquery = dot(dscores, key)
        dqs += [dquery[j * rows : (j + 1) * rows] for j in range(GROUP)]
        dks.append(dot_tn(dscores, queries))
        dvs.append(dot_tn(probs.astype(LOW), douts))

    def turned_back(grads):
        lanes = grads.shape[-1]
        cos, sin = widen_table(cos_ref[...], lanes), widen_table(sin_ref[...], lanes)
        return (grads * cos + swap_halves(grads * sin)).astype(LOW)

    dq = turned_back(jnp.concatenate(dqs, -1))
    dk = turned_back(jnp.concatenate(dks, -1))
    dv = jnp.concatenate(dvs, -1).astype(LOW)
    dqkv_ref[0] = jnp.concatenate([dq, dk, dv], -1)
    dn = dot_nt(dq, wq_ref[...]) + dot_nt(dk, wk_ref[...]) + dot_nt(dv, wv_ref[...])
    dn_ref[0] = dn.astype(LOW)


def attend_backward(z, qkv, da, wo, wq, wk, wv, marks, cos, sin, parts):
    batches, rows, width = da.shape
    place_col, place_row, label_col, label_row = marks
    q_lanes, k_lanes = wo.shape[0] // parts, KEY_VALUE_HEADS * HEAD_SIZE // parts
    k_at = wo.shape[0] // k_lanes
    full = lambda *shape: pl.BlockSpec(shape, lambda b, z: (0,) * len(shape))
    batch = lambda *shape: pl.BlockSpec((1,) + shape, lambda b, z: (b, 0, 0))
    columns = lambda lanes: pl.BlockSpec((width, lanes), lambda b, z: (0, z[0]))
    return pl.pallas_call(
        attend_backward_kernel,
        grid_spec=pltpu.PrefetchScalarGridSpec(
            num_scalar_prefetch=1,
            grid=(batches,),
            in_specs=[
                pl.BlockSpec((1, rows, q_lanes), lambda b, z: (b, 0, z[0])),
                pl.BlockSpec((1, rows, k_lanes), lambda b, z: (b, 0, k_at + z[0])),
                pl.BlockSpec((1, rows, k_lanes), lambda b, z: (b, 0, k_at + parts + z[0])),
                batch(rows, width),
                pl.BlockSpec((q_lanes, width), lambda b, z: (z[0], 0)),
                columns(q_lanes),
                columns(k_lanes),
                columns(k_lanes),
                full(rows, 1),
                full(1, rows),
                batch(rows, 1),
                batch(1, rows),
                full(rows, cos.shape[1]),
                full(rows, cos.shape[1]),
            ],
            out_specs=[batch(rows, q_lanes + 2 * k_lanes), batch(rows, width)],
        ),
        out_shape=[
            jax.ShapeDtypeStruct((batches, rows, q_lanes + 2 * k_lanes), LOW),
            jax.ShapeDtypeStruct((batches, rows, width), LOW),
        ],
        compiler_params=params("arbitrary"),
        cost_estimate=pl.CostEstimate(
            flops=2 * batches * rows * width * 2 * (q_lanes + k_lanes) + 40 * batches * rows * rows * q_lanes,
            bytes_accessed=4 * width * (q_lanes + k_lanes) + 6 * batches * rows * width,
            transcendentals=batches * rows * rows * q_lanes // HEAD_SIZE,
        ),
        name="attend_backward",
    )(z, qkv, qkv, qkv, da, wo, wq, wk, wv, place_col, place_row, label_col, label_row, cos, sin)


def chip_block(place_ref, x, y, core):
    ring = lax.rem(place_ref[0] + x, RING)
    pair = lax.rem(place_ref[1] + y, PAIR)
    return (ring * PAIR + pair) * CORES + lax.rem(place_ref[2] + core, CORES)


def expert_grad_kernel(cut, place_ref, left_ref, right_ref, *refs):
    product_ref = refs[-1]
    rows = product_ref.shape[1]
    product = dot_tn(left_ref[...], right_ref[...]).astype(LOW)
    for i in range(RING * PAIR * CORES):
        product_ref[i] = product[i * rows : (i + 1) * rows]
    step = pl.program_id(0)
    lanes = refs[0].shape[-1]

    def place(refs, ring_first):
        for core in range(CORES):
            for x in range(RING):
                for y in range(PAIR):
                    block = product_ref[chip_block(place_ref, x, y, core)]
                    for part in range(cut):
                        at = slice(part * rows, (part + 1) * rows)
                        value = block[:, part * lanes : (part + 1) * lanes]
                        if ring_first:
                            refs[core][x, 0, y, at] = value
                        else:
                            refs[core][y, x, 0, at] = value

    @pl.when(step < pl.num_programs(0) // 2)
    def _():
        place(refs[0:2], True)

    @pl.when(step >= pl.num_programs(0) // 2)
    def _():
        place(refs[2:4], False)


def expert_grad(place, left, right, count, cut):
    rows = left.shape[0]
    left_lanes = left.shape[1] // count if cut > 1 else left.shape[1]
    right_lanes = right.shape[1] if cut > 1 else right.shape[1] // count
    owners = RING * PAIR * CORES
    high, lanes, half = left_lanes // owners, right_lanes // cut, count // 2
    ring_first = (RING, half, PAIR, high * cut, lanes)
    pair_first = (PAIR, RING, half, high * cut, lanes)
    ring_spec = pl.BlockSpec((RING, 1, PAIR, high * cut, lanes), lambda e, p: (0, jnp.minimum(e, half - 1), 0, 0, 0))
    pair_spec = pl.BlockSpec((PAIR, RING, 1, high * cut, lanes), lambda e, p: (0, 0, jnp.maximum(e - half, 0), 0, 0))
    split = lambda wide, by: pl.BlockSpec((rows, wide), (lambda e, p: (0, e)) if by else (lambda e, p: (0, 0)))
    return pl.pallas_call(
        functools.partial(expert_grad_kernel, cut),
        grid_spec=pltpu.PrefetchScalarGridSpec(
            num_scalar_prefetch=1,
            grid=(count,),
            in_specs=[split(left_lanes, cut > 1), split(right_lanes, cut == 1)],
            out_specs=[ring_spec, ring_spec, pair_spec, pair_spec],
            scratch_shapes=[pltpu.VMEM((owners, high, right_lanes), LOW)],
        ),
        out_shape=[jax.ShapeDtypeStruct(shape, LOW) for shape in (ring_first, ring_first, pair_first, pair_first)],
        compiler_params=params("arbitrary"),
        cost_estimate=pl.CostEstimate(
            flops=2 * rows * left_lanes * right_lanes * count,
            bytes_accessed=2 * left_lanes * right_lanes * count + 4 * rows * (left_lanes + right_lanes),
            transcendentals=0,
        ),
        name="expert_grad",
    )(place, left, right)


def into_grad_kernel(place_ref, left_ref, right_ref, mine_ref, other_ref, product_ref):
    half = product_ref.shape[1] // 2
    product = dot_tn(left_ref[...], right_ref[...]).astype(LOW)
    for i in range(RING * PAIR * CORES):
        product_ref[i] = product[i * 2 * half : (i + 1) * 2 * half]
    for core, ref in enumerate((mine_ref, other_ref)):
        for x in range(RING):
            for y in range(PAIR):
                block = product_ref[chip_block(place_ref, x, y, core)]
                ref[x, 0, y] = block[:half]
                ref[x, 1, y] = block[half:]


def out_of_grad_kernel(place_ref, z_ref, left_ref, right_ref, mine_ref, other_ref, product_ref):
    del z_ref
    high, lanes = mine_ref.shape[-2:]
    product = dot_tn(left_ref[...], right_ref[...]).astype(LOW)
    for i in range(RING * PAIR):
        for core in range(CORES):
            product_ref[i * CORES + core] = product[i * high : (i + 1) * high, core * 2 * lanes : (core + 1) * 2 * lanes]
    for core, ref in enumerate((mine_ref, other_ref)):
        for x in range(RING):
            for y in range(PAIR):
                block = product_ref[chip_block(place_ref, x, y, core)]
                ref[x, 0, y] = block[:, :lanes]
                ref[x, 1, y] = block[:, lanes:]


def dense_grad(place, z, left, right, parts, outward):
    rows = left.shape[0]
    owners = RING * PAIR * CORES
    if outward:
        left_lanes = left.shape[1] // parts
        high, lanes = left_lanes // (RING * PAIR), right.shape[1] // CORES // 2
        scratch = (owners, high, 2 * lanes)
    else:
        left_lanes = left.shape[1]
        high, lanes = left_lanes // owners // 2, right.shape[1]
        scratch = (owners, 2 * high, lanes)
    shape = (RING, 2, PAIR, high, lanes)
    scalars = (place, z) if outward else (place,)
    return pl.pallas_call(
        out_of_grad_kernel if outward else into_grad_kernel,
        grid_spec=pltpu.PrefetchScalarGridSpec(
            num_scalar_prefetch=len(scalars),
            grid=(1,),
            in_specs=[
                pl.BlockSpec((rows, left_lanes), lambda i, *s: (0, s[1][0] if outward else 0)),
                pl.BlockSpec((rows, right.shape[1]), lambda i, *s: (0, 0)),
            ],
            out_specs=[pl.BlockSpec(shape, lambda i, *s: (0,) * 5)] * 2,
            scratch_shapes=[pltpu.VMEM(scratch, LOW)],
        ),
        out_shape=[jax.ShapeDtypeStruct(shape, LOW)] * 2,
        compiler_params=params("arbitrary"),
        cost_estimate=pl.CostEstimate(
            flops=2 * rows * left_lanes * right.shape[1],
            bytes_accessed=2 * left_lanes * right.shape[1] + 2 * rows * (left_lanes + right.shape[1]),
            transcendentals=0,
        ),
        name="dense_grad",
    )(*scalars, left, right)


def into_layout_kernel(place_ref, z_ref, mine_ref, other_ref, wq_ref, wk_ref, wv_ref):
    parts = mine_ref.shape[0]
    half = mine_ref.shape[-2]

    def place(ref):
        for k in range(parts):
            at = lax.rem(z_ref[0] + parts - k, parts)
            start = 0
            for out in (wq_ref, wk_ref, wv_ref):
                lanes = out.shape[1] // parts
                for h in range(2):
                    columns = pl.ds(pl.multiple_of(at * lanes, 128), lanes)
                    value = ref[k, 0, 0, h, :, start : start + lanes]
                    out[h * half : (h + 1) * half, columns] = value.astype(F32)
                start += lanes

    @pl.when(pl.program_id(0) == 0)
    def _():
        place(mine_ref)

    @pl.when(pl.program_id(0) == 1)
    def _():
        place(other_ref)


def into_layout(place, z, mine, other, shapes):
    parts, _, _, _, half, lanes = mine.shape

    def row_block(core, x, y, place, z):
        ring = lax.rem(place[0] + RING - x, RING)
        pair = lax.rem(place[1] + y, PAIR)
        return ((ring * PAIR + pair) * CORES + lax.rem(place[2] + core, CORES), 0)

    block = (parts, 1, 1, 2, half, lanes)
    return pl.pallas_call(
        into_layout_kernel,
        grid_spec=pltpu.PrefetchScalarGridSpec(
            num_scalar_prefetch=2,
            grid=(CORES, RING, PAIR),
            in_specs=[
                pl.BlockSpec(block, lambda c, x, y, p, z: (0, jnp.where(c == 0, y, PAIR - 1), jnp.where(c == 0, x, RING - 1), 0, 0, 0)),
                pl.BlockSpec(block, lambda c, x, y, p, z: (0, jnp.where(c == 1, y, 0), jnp.where(c == 1, x, 0), 0, 0, 0)),
            ],
            out_specs=[pl.BlockSpec((2 * half, shape[1]), row_block) for shape in shapes],
        ),
        out_shape=[jax.ShapeDtypeStruct(shape, F32) for shape in shapes],
        compiler_params=params("arbitrary", "arbitrary", "arbitrary"),
        cost_estimate=pl.CostEstimate(flops=0, bytes_accessed=12 * mine.size, transcendentals=0),
        name="into_layout",
    )(place, z, mine, other)


def out_of_layout_kernel(place_ref, z_ref, mine_ref, other_ref, out_ref):
    parts = mine_ref.shape[0]
    lanes = mine_ref.shape[-1]
    for core, ref in enumerate((mine_ref, other_ref)):
        first = lax.rem(place_ref[2] + core, CORES) * 2 * lanes
        for k in range(parts):
            at = lax.rem(z_ref[0] + parts - k, parts)
            for h in range(2):
                columns = pl.ds(pl.multiple_of(first + h * lanes, 128), lanes)
                out_ref[at, 0, :, columns] = ref[k, 0, 0, h].astype(F32)


def out_of_layout(place, z, mine, other):
    parts, _, _, _, high, lanes = mine.shape
    width = 2 * CORES * lanes
    block = pl.BlockSpec((parts, 1, 1, 2, high, lanes), lambda x, y, p, z: (0, y, x, 0, 0, 0))

    def row_block(x, y, place, z):
        return (0, lax.rem(place[0] + RING - x, RING) * PAIR + lax.rem(place[1] + y, PAIR), 0, 0)

    out = pl.pallas_call(
        out_of_layout_kernel,
        grid_spec=pltpu.PrefetchScalarGridSpec(
            num_scalar_prefetch=2,
            grid=(RING, PAIR),
            in_specs=[block, block],
            out_specs=pl.BlockSpec((parts, 1, high, width), row_block),
        ),
        out_shape=jax.ShapeDtypeStruct((parts, RING * PAIR, high, width), F32),
        compiler_params=params("arbitrary", "arbitrary"),
        cost_estimate=pl.CostEstimate(flops=0, bytes_accessed=12 * mine.size, transcendentals=0),
        name="out_of_layout",
    )(place, z, mine, other)
    return out.reshape(-1, width)


def norm_back(grad_normed, values, gain):
    scale = lax.rsqrt(jnp.mean(values * values, -1, keepdims=True) + EPS)
    scaled = grad_normed * gain
    gain_grad = jnp.sum(grad_normed * values * scale, (0, 1))
    inner = jnp.mean(scaled * values, -1, keepdims=True)
    return (scale * scaled - values * scale * scale * scale * inner, gain_grad)


def local(
    block_input, segments, expert_ids, route_weights, attn_gain, w_query, key_projection_weight,
    value_projection_weight, w_out, ffn_gain, w_gate, w_up, w_down, out_grad,
):
    parts = lax.axis_size("expert")
    section = lax.axis_index("section")
    z = lax.axis_index("expert")
    z_at = z.reshape(1)
    dp = lax.axis_index("dp")
    dp_place = jnp.stack([dp // (PAIR * CORES), dp // CORES % PAIR, dp % CORES])
    batches, own, width = block_input.shape
    rows = parts * own
    wq, wk, wv, wo = w_query[0], key_projection_weight[0], value_projection_weight[0], w_out[0]
    local_experts, units = w_gate.shape[1], w_gate.shape[3]

    wg = lax.all_gather(w_gate[0], "dp", axis=1, tiled=True)
    wu = lax.all_gather(w_up[0], "dp", axis=1, tiled=True)
    wd = lax.all_gather(w_down[0], "dp", axis=1, tiled=True)

    start = gather_group(block_input)
    labels = gather_group(segments)
    numbers = jnp.arange(parts * local_experts, dtype=jnp.int32)
    hits = expert_ids[0][..., None] == numbers
    shares_own = jnp.sum(jnp.where(hits, route_weights[0][..., None], 0.0), 2)
    shares = gather_group(shares_own).reshape(batches * rows, parts, local_experts)
    share = lax.dynamic_index_in_dim(shares, z, 1, keepdims=False).T[..., None]
    block = jnp.arange(parts, dtype=jnp.int32)[:, None]
    place = ((z - block) % parts * own + jnp.arange(own, dtype=jnp.int32)[None, :]).reshape(rows)
    marks = (place[:, None], place[None, :], labels[:, :, None], labels[:, None, :])
    half = HEAD_SIZE // 2
    frequency = 10000.0 ** (-jnp.arange(half, dtype=F32) * 2.0 / HEAD_SIZE)
    angles = place.astype(F32)[:, None] * frequency[None, :]
    cos_half, sin_half = jnp.cos(angles), jnp.sin(angles)
    cos = jnp.concatenate([cos_half] * 4, -1)
    sin = jnp.concatenate([-sin_half, sin_half] * 2, -1)
    cos_all, sin_all = jnp.concatenate([cos] * batches, 0), jnp.concatenate([sin] * batches, 0)

    def attention(x):
        qkv, xn = project(x.reshape(batches * rows, width), attn_gain, wq, wk, wv, cos_all, sin_all)
        qkv = qkv.reshape(batches, rows, -1)
        mixed, h1, xn2 = attend(qkv, x, wo, ffn_gain, marks, parts, own)
        return qkv, xn, mixed, h1, xn2.reshape(batches * rows, width)

    _, _, _, h1, xn2 = attention(start)
    partial = experts_forward(xn2, share, wg, wu, wd).reshape(batches, rows, width)
    result = (h1 + sum_to_owners(partial, own)).astype(LOW)
    received = gather_group(to_section(result, 1))

    x = jnp.where(section == 0, start, received)
    qkv, xn, mixed, h1, xn2 = attention(x)
    hidden, to_up, to_gate = experts_keep(xn2, share, wg, wu)

    def backward(c, c_own, keep):
        partial, *kept = experts_backward(c.reshape(batches * rows, width), to_up, to_gate, wg, wu, wd, keep)
        normed_grad = sum_to_owners(partial.reshape(batches, rows, width), own)
        norm_part, ffn_grad = norm_back(normed_grad, h1, ffn_gain)
        after = c_own.astype(F32) + norm_part
        da = gather_group(after.astype(LOW))
        dqkv, dn = attend_backward(z_at, qkv, da, wo, wq, wk, wv, marks, cos, sin, parts)
        dn_own = sum_to_owners(dn, own)
        norm_part, attn_grad = norm_back(dn_own, x[:, :own].astype(F32), attn_gain)
        return after + norm_part, da, dqkv, ffn_grad, attn_grad, kept

    c_second = gather_group(out_grad)
    input_grad = backward(c_second, out_grad, False)[0]
    received_own = to_section(input_grad.astype(LOW), 0)

    partial = dot(hidden, wd.reshape(local_experts * units, width)).astype(LOW).reshape(batches, rows, width)
    layer_outputs = (h1 + sum_to_owners(partial, own)).astype(LOW)

    c_own = jnp.where(section == 1, out_grad, received_own)
    c = jnp.where(section == 1, c_second, gather_group(received_own))
    input_grad, da, dqkv, ffn_grad, attn_grad, (gate_grad, up_grad) = backward(c, c_own, True)

    flat_c = c.reshape(batches * rows, width)

    def to_owners(left, right, cut):
        mine_ring, other_ring, mine_pair, other_pair = expert_grad(dp_place, left, right, local_experts, cut)
        ring = added(mine_ring, moved(other_ring, core=1)).astype(LOW)
        pair = added(mine_pair, moved(other_pair, core=1)).astype(LOW)
        return jnp.concatenate([ring_first_sum(ring), pair_first_sum(pair)], 0)

    w_down_grad = to_owners(hidden, flat_c, width // units)
    w_gate_grad = to_owners(xn2, gate_grad, 1)
    w_up_grad = to_owners(xn2, up_grad, 1)
    w_down_grad = w_down_grad.reshape(local_experts, width // units, -1, units)
    w_down_grad = jnp.swapaxes(w_down_grad, 1, 2).reshape(local_experts, -1, width)

    mine, other = dense_grad(dp_place, z_at, mixed.reshape(batches * rows, -1), da.reshape(batches * rows, width), parts, True)
    share_out = ring_first_sum(added(mine, moved(other, core=1)).astype(LOW)).astype(LOW)
    mine = group_stack(pair_gather(ring_gather(share_out)))
    mine = jnp.reshape(mine, (parts, PAIR, RING) + share_out.shape)
    w_out_grad = out_of_layout(dp_place, z_at, mine, moved(mine, core=1))

    mine, other = dense_grad(dp_place, z_at, xn, dqkv.reshape(batches * rows, -1), parts, False)
    share_in = ring_first_sum(added(mine, moved(other, core=1)).astype(LOW)).astype(LOW)
    mine = pair_gather(group_stack(share_in))
    mine = ring_gather(jnp.moveaxis(mine, 2, 0))
    mine = jnp.transpose(mine, (3, 2, 0, 1, 4, 5))
    w_query_grad, w_key_grad, w_value_grad = into_layout(
        dp_place, z_at, mine, moved(mine, core=1), (wq.shape, wk.shape, wv.shape)
    )
    gains = sum_everywhere(jnp.stack([attn_grad, ffn_grad]))
    return (
        layer_outputs[None],
        input_grad[None],
        gains[0:1],
        w_query_grad[None],
        w_key_grad[None],
        w_value_grad[None],
        w_out_grad[None],
        gains[1:2],
        w_gate_grad[None],
        w_up_grad[None],
        w_down_grad[None],
    )


def solution(mesh):
    tokens = P(None, ("dp", "expert"), None)
    layered = P("section", None, ("dp", "expert"), None)
    vector = P("section", None)
    matrix = P("section", None, None)
    expert = P("section", "expert", "dp", None)
    return jax.shard_map(
        local,
        mesh=mesh,
        in_specs=(
            tokens, P(None, ("dp", "expert")), layered, layered, vector, matrix, matrix, matrix, matrix,
            vector, expert, expert, expert, tokens,
        ),
        out_specs=(layered, layered, vector, matrix, matrix, matrix, matrix, vector, expert, expert, expert),
        check_vma=False,
    )
```

time: 1760 us -> 869 us (0.49)
  blocking collectives: 391 us -> 0 us
  matrix products: 307 us -> 6.83 us
  waiting for transfers between devices: 658 us -> 415 us
  Pallas kernels: 0 us -> 216 us
  local copies, waits for them, and re-layouts: 214 us -> 22.1 us
  starting transfers between devices: 55.7 us -> 138 us
  other arithmetic: 106 us -> 46.8 us
    psum x1 -> x0, waiting for transfers between devices: 468 us -> none  [local(): lax.psum((dense_total[0], dense_total[1], dense_total[2], dense_total[3],...]
    ppermute x4 -> x116, waiting for transfers between devices: 15.4 us -> 349 us  [the longest x48 225 us: shifted(): lax.ppermute(block, 'expert', [(i, (i + by) % size) for i in range(size)])]
    dot_general x87 -> x1, matrix products: 307 us -> 6.83 us  [dot(): return jnp.dot(left, right, preferred_element_type=F32)]
    psum x1 -> x0, blocking collectives: 278 us -> none  [local(): lax.psum((dense_total[0], dense_total[1], dense_total[2], dense_total[3],...]
    pallas_call x0 -> x17, Pallas kernels: none -> 216 us  [the longest x2 46.7 us: attend(): pl.pallas_call(attend_kernel, grid=(batches, parts), in_specs=[pl.BlockSp...]
    ppermute x4 -> x116, starting transfers between devices: 13.3 us -> 138 us  [the longest x60 70.4 us: moved(): return lax.ppermute(block, 'dp', route)]
    all_gather x7 -> x0, blocking collectives: 73.8 us -> none  [the longest x3 32 us: layer_forward(): lax.all_gather(keys_own, 'expert', axis=0, tiled=True)]
    all_to_all x10 -> x0, waiting for transfers between devices: 61.7 us -> none  [the longest x3 39.7 us: layer_forward(): lax.all_to_all(produced[None], 'expert', split_axis=2, concat_axis=0, til...]
  transfers between devices with their start and end apart: 27 -> 119, of which waited for: 15 -> 61; matrix products, arithmetic and copies ran while one was open for 19% -> 5% of each run, Pallas kernels for 0% -> 9%
where the time goes in v1:
time: 869 us; the launch traced here: 861 us
  waiting for transfers between devices  415 us (48%)
  Pallas kernels  216 us (25%)
  starting transfers between devices  138 us (16%)
  other arithmetic  46.8 us (5%)
  local copies, waits for them, and re-layouts  22.1 us (3%)
  between operations  15.7 us (2%)
    ppermute x48, waiting for transfers between devices, shifted(): lax.ppermute(block, 'expert', [(i, (i + by) % size) for i in range(size)])  225 us
    ppermute x60, waiting for transfers between devices, moved(): return lax.ppermute(block, 'dp', route)  105 us
    ppermute x60, starting transfers between devices, moved(): return lax.ppermute(block, 'dp', route)  70.4 us
    ppermute x48, starting transfers between devices, shifted(): lax.ppermute(block, 'expert', [(i, (i + by) % size) for i in range(size)])  54.5 us
    pallas_call x2, Pallas kernels, attend(): pl.pallas_call(attend_kernel, grid=(batches, parts), in_specs=[pl.BlockSp...  46.7 us
    all_gather x1, waiting for transfers between devices, local(): wd = lax.all_gather(w_down[0], 'dp', axis=1, tiled=True)  44.8 us
    pallas_call x2, Pallas kernels, experts_backward(): pl.pallas_call(experts_backward_kernel, grid=(count,), in_specs=[pl.Block...  34.7 us
    pallas_call x3, Pallas kernels, expert_grad(): pl.pallas_call(functools.partial(expert_grad_kernel, cut), grid_spec=pltp...  27 us
  transfers between devices with their start and end apart: 119, of which 61 were waited for; matrix products, arithmetic and copies ran while one was open for 5% of the time, Pallas kernels for 9%

profile of v1, /device:TPU:1, one launch (start us, length us, event | category | flops | bytes accessed | tf_op | source)
XLA Modules:
  0.0 860.6 jit_solution(1354107380684865654)
XLA Ops:
  45.4 12.1 %project.2 = (bf16[512,2560]{1,0:T(8,128)(2,1)}, bf16[512,1536]{1,0:T(8,128)(2,1)}) custom-call(bf16[512,1536]{1,0:T(8,128)(2,1)} %bitcast.246, f32[1,1536]{1,0:T(1,128)} %gain_ref.6, bf16[1536,1536]{1,0:T(8,128)(2,1)} %bitcast.236, bf16[1536,512]{1,0:T(8,128)(2,1)} %bitcast.257, bf16[1536,512]{1,0:T(8,128)(2,1)} %bitcast.261, ...), custom_call_target="tpu_custom_call" | custom-call | flops 4026531840 | bytes 14155776 | tf_op jit(solution)/shard_map/project/pallas_call | solution.py:166
  57.5 23.3 %attend.2 = (bf16[2,256,1536]{2,1,0:T(8,128)(2,1)}, f32[2,64,1536]{2,1,0:T(8,128)}, bf16[2,256,1536]{2,1,0:T(8,128)(2,1)}) custom-call(bf16[2,256,2560]{2,1,0:T(8,128)(2,1)} %bitcast.327, bf16[2,256,2560]{2,1,0:T(8,128)(2,1)} %bitcast.328, bf16[2,256,2560]{2,1,0:T(8,128)(2,1)} %bitcast.329, s32[256,1]{1,0:T(8,128)} %add.547.pc_ref, s32[1,256]{1,0:T(1,128)} %add.431.pr_ref, ...), custom_call_target="tpu_custom_call" | custom-call | flops 5637144576 | bytes 18874368 | tf_op jit(solution)/shard_map/attend/pallas_call | solution.py:249
  80.9 19.7 %all-gather.9.cloned.1.call-done = bf16[1,4,1536,512]{3,2,1,0:T(8,128)(2,1)} async-done(((bf16[1,4,96,512]{3,2,1,0:T(8,128)(2,1)}), bf16[1,4,1536,512]{3,2,1,0:T(8,128)(2,1)}) %all-gather.9.cloned.1.call-update) | async-done | bytes 6291472 | tf_op jit(solution)/shard_map/all_gather | solution.py:748
  100.5 44.8 %all-gather.11.cloned.1.call-done = bf16[1,4,512,1536]{3,2,1,0:T(8,128)(2,1)} async-done(((bf16[1,4,32,1536]{3,2,1,0:T(8,128)(2,1)}), bf16[1,4,512,1536]{3,2,1,0:T(8,128)(2,1)}) %all-gather.11.cloned.1.call-update) | async-done | bytes 6291472 | tf_op jit(solution)/shard_map/all_gather | solution.py:749
  145.3 16.4 %experts_forward.1 = bf16[512,1536]{1,0:T(8,128)(2,1)} custom-call(bf16[512,1536]{1,0:T(8,128)(2,1)} %bitcast.333, f32[4,512,1]{2,1,0:T(8,128)} %copy.126.share_ref, bf16[4,1536,512]{2,1,0:T(8,128)(2,1)} %bitcast.312, bf16[4,1536,512]{2,1,0:T(8,128)(2,1)} %bitcast.316, bf16[4,512,1536]{2,1,0:T(8,128)(2,1)} %bitcast.320), custom_call_target="tpu_custom_call" | custom-call | flops 9663676416 | bytes 18874368 | tf_op jit(solution)/shard_map/experts_forward/pallas_call | solution.py:331
  174.8 9.6 %collective-permute-done.10 = bf16[2,64,1536]{2,1,0:T(8,128)(2,1)S(1)} collective-permute-done((bf16[2,64,1536]{2,1,0:T(8,128)(2,1)S(1)}, bf16[2,64,1536]{2,1,0:T(8,128)(2,1)S(1)}, u32[]{:S(2)}, u32[]{:S(2)}) %collective-permute-start.10) | collective-permute-done | bytes 393248 | tf_op jit(solution)/shard_map/ppermute | solution.py:38
  203.9 9.5 %collective-permute-done.19 = bf16[2,64,1536]{2,1,0:T(8,128)(2,1)S(1)} collective-permute-done((bf16[2,64,1536]{2,1,0:T(8,128)(2,1)S(1)}, bf16[2,64,1536]{2,1,0:T(8,128)(2,1)S(1)}, u32[]{:S(2)}, u32[]{:S(2)}) %collective-permute-start.19) | collective-permute-done | bytes 393248 | tf_op jit(solution)/shard_map/ppermute | solution.py:38
  233.7 11.9 %project.3 = (bf16[512,2560]{1,0:T(8,128)(2,1)}, bf16[512,1536]{1,0:T(8,128)(2,1)}) custom-call(bf16[512,1536]{1,0:T(8,128)(2,1)} %bitcast_select_fusion.1.x_ref, f32[1,1536]{1,0:T(1,128)} %gain_ref.6, bf16[1536,1536]{1,0:T(8,128)(2,1)} %bitcast.237, bf16[1536,512]{1,0:T(8,128)(2,1)} %bitcast.258, bf16[1536,512]{1,0:T(8,128)(2,1)} %bitcast.262, ...), custom_call_target="tpu_custom_call" | custom-call | flops 4026531840 | bytes 14155776 | tf_op jit(solution)/shard_map/project/pallas_call | solution.py:166
  245.7 23.4 %attend.3 = (bf16[2,256,1536]{2,1,0:T(8,128)(2,1)}, f32[2,64,1536]{2,1,0:T(8,128)}, bf16[2,256,1536]{2,1,0:T(8,128)(2,1)}) custom-call(bf16[2,256,2560]{2,1,0:T(8,128)(2,1)} %bitcast.227, bf16[2,256,2560]{2,1,0:T(8,128)(2,1)} %bitcast.228, bf16[2,256,2560]{2,1,0:T(8,128)(2,1)} %bitcast.229, s32[256,1]{1,0:T(8,128)} %add.547.pc_ref, s32[1,256]{1,0:T(1,128)} %add.431.pr_ref, ...), custom_call_target="tpu_custom_call" | custom-call | flops 5637144576 | bytes 18874368 | tf_op jit(solution)/shard_map/attend/pallas_call | solution.py:249
  269.0 12.5 %experts_keep.1 = (bf16[512,2048]{1,0:T(8,128)(2,1)}, bf16[512,2048]{1,0:T(8,128)(2,1)}, bf16[512,2048]{1,0:T(8,128)(2,1)}) custom-call(bf16[512,1536]{1,0:T(8,128)(2,1)} %bitcast.330, f32[4,512,1]{2,1,0:T(8,128)} %copy.126.share_ref, bf16[4,1536,512]{2,1,0:T(8,128)(2,1)} %bitcast.313, bf16[4,1536,512]{2,1,0:T(8,128)(2,1)} %bitcast.317), custom_call_target="tpu_custom_call" | custom-call | flops 6442450944 | bytes 12582912 | tf_op jit(solution)/shard_map/experts_keep/pallas_call | solution.py:353
  281.5 17.0 %experts_backward.2 = bf16[512,1536]{1,0:T(8,128)(2,1)} custom-call(bf16[512,1536]{1,0:T(8,128)(2,1)} %bitcast.247, bf16[512,2048]{1,0:T(8,128)(2,1)} %get-tuple-element.54.up_ref, bf16[512,2048]{1,0:T(8,128)(2,1)} %get-tuple-element.55.gate_ref, bf16[4,1536,512]{2,1,0:T(8,128)(2,1)} %bitcast.314, bf16[4,1536,512]{2,1,0:T(8,128)(2,1)} %bitcast.318, ...), custom_call_target="tpu_custom_call" | custom-call | flops 9663676416 | bytes 18874368 | tf_op jit(solution)/shard_map/experts_backward/pallas_call | solution.py:398
  312.3 9.9 %collective-permute-done.23 = bf16[2,64,1536]{2,1,0:T(8,128)(2,1)S(1)} collective-permute-done((bf16[2,64,1536]{2,1,0:T(8,128)(2,1)}, bf16[2,64,1536]{2,1,0:T(8,128)(2,1)S(1)}, u32[]{:S(2)}, u32[]{:S(2)}) %collective-permute-start.23) | collective-permute-done | bytes 393248 | tf_op jit(solution)/shard_map/ppermute | solution.py:38
  340.5 9.6 %collective-permute-done.25 = bf16[2,64,1536]{2,1,0:T(8,128)(2,1)S(1)} collective-permute-done((bf16[2,64,1536]{2,1,0:T(8,128)(2,1)S(1)}, bf16[2,64,1536]{2,1,0:T(8,128)(2,1)S(1)}, u32[]{:S(2)}, u32[]{:S(2)}) %collective-permute-start.25) | collective-permute-done | bytes 393248 | tf_op jit(solution)/shard_map/ppermute | solution.py:38
  351.4 11.4 %attend_backward.2 = (bf16[2,256,640]{2,1,0:T(8,128)(2,1)}, bf16[2,256,1536]{2,1,0:T(8,128)(2,1)}) custom-call(s32[1]{0:T(128)} %bitcast.27.z_ref, bf16[2,256,2560]{2,1,0:T(8,128)(2,1)} %bitcast.230, bf16[2,256,2560]{2,1,0:T(8,128)(2,1)} %bitcast.231, bf16[2,256,2560]{2,1,0:T(8,128)(2,1)} %bitcast.232, bf16[2,256,1536]{2,1,0:T(8,128)(2,1)} %pad_maximum_fusion.2.da_ref, ...), custom_call_target="tpu_custom_call" | custom-call | flops 3623878656 | bytes 7864320 | tf_op jit(solution)/shard_map/attend_backward/pallas_call | solution.py:467
  368.7 16.7 %collective-permute-done.30 = bf16[2,64,1536]{2,1,0:T(8,128)(2,1)} collective-permute-done((bf16[2,64,1536]{2,1,0:T(8,128)(2,1)}, bf16[2,64,1536]{2,1,0:T(8,128)(2,1)}, u32[]{:S(2)}, u32[]{:S(2)}) %collective-permute-start.30) | collective-permute-done | bytes 393248 | tf_op jit(solution)/shard_map/ppermute | solution.py:38
  391.3 11.3 %collective-permute-done.31 = bf16[2,64,1536]{2,1,0:T(8,128)(2,1)S(1)} collective-permute-done((bf16[2,64,1536]{2,1,0:T(8,128)(2,1)}, bf16[2,64,1536]{2,1,0:T(8,128)(2,1)S(1)}, u32[]{:S(2)}, u32[]{:S(2)}) %collective-permute-start.31) | collective-permute-done | bytes 393248 | tf_op jit(solution)/shard_map/ppermute | solution.py:55
  416.9 10.6 %collective-permute-done.32 = bf16[2,64,1536]{2,1,0:T(8,128)(2,1)S(1)} collective-permute-done((bf16[2,64,1536]{2,1,0:T(8,128)(2,1)S(1)}, bf16[2,64,1536]{2,1,0:T(8,128)(2,1)S(1)}, u32[]{:S(2)}, u32[]{:S(2)}) %collective-permute-start.32) | collective-permute-done | bytes 393248 | tf_op jit(solution)/shard_map/ppermute | solution.py:38
  429.2 17.7 %experts_backward.3 = (bf16[512,1536]{1,0:T(8,128)(2,1)}, bf16[512,2048]{1,0:T(8,128)(2,1)}, bf16[512,2048]{1,0:T(8,128)(2,1)}) custom-call(bf16[512,1536]{1,0:T(8,128)(2,1)} %bitcast_select_fusion.c_ref.right_ref, bf16[512,2048]{1,0:T(8,128)(2,1)} %get-tuple-element.54.up_ref, bf16[512,2048]{1,0:T(8,128)(2,1)} %get-tuple-element.55.gate_ref, ...), custom_call_target="tpu_custom_call" | custom-call | flops 9663676416 | bytes 18874368 | tf_op jit(solution)/shard_map/experts_backward/pallas_call | solution.py:398
  453.5 13.7 %collective-permute-done.37 = bf16[2,64,1536]{2,1,0:T(8,128)(2,1)S(1)} collective-permute-done((bf16[2,64,1536]{2,1,0:T(8,128)(2,1)S(1)}, bf16[2,64,1536]{2,1,0:T(8,128)(2,1)S(1)}, u32[]{:S(2)}, u32[]{:S(2)}) %collective-permute-start.37) | collective-permute-done | bytes 393248 | tf_op jit(solution)/shard_map/ppermute | solution.py:38
  469.4 15.5 %collective-permute-done.18 = bf16[2,64,1536]{2,1,0:T(8,128)(2,1)S(1)} collective-permute-done((bf16[2,64,1536]{2,1,0:T(8,128)(2,1)S(1)}, bf16[2,64,1536]{2,1,0:T(8,128)(2,1)S(1)}, u32[]{:S(2)}, u32[]{:S(2)}) %collective-permute-start.18) | collective-permute-done | bytes 393248 | tf_op jit(solution)/shard_map/ppermute | solution.py:38
  500.8 10.0 %collective-permute-done.38 = bf16[2,64,1536]{2,1,0:T(8,128)(2,1)S(1)} collective-permute-done((bf16[2,64,1536]{2,1,0:T(8,128)(2,1)}, bf16[2,64,1536]{2,1,0:T(8,128)(2,1)S(1)}, u32[]{:S(2)}, u32[]{:S(2)}) %collective-permute-start.38) | collective-permute-done | bytes 393248 | tf_op jit(solution)/shard_map/ppermute | solution.py:38
  513.1 11.4 %attend_backward.3 = (bf16[2,256,640]{2,1,0:T(8,128)(2,1)}, bf16[2,256,1536]{2,1,0:T(8,128)(2,1)}) custom-call(s32[1]{0:T(128)} %bitcast.27.z_ref, bf16[2,256,2560]{2,1,0:T(8,128)(2,1)} %bitcast.233, bf16[2,256,2560]{2,1,0:T(8,128)(2,1)} %bitcast.234, bf16[2,256,2560]{2,1,0:T(8,128)(2,1)} %bitcast.235, bf16[2,256,1536]{2,1,0:T(8,128)(2,1)} %pad_maximum_fusion.4.da_ref, ...), custom_call_target="tpu_custom_call" | custom-call | flops 3623878656 | bytes 7864320 | tf_op jit(solution)/shard_map/attend_backward/pallas_call | solution.py:467
  529.3 9.1 %expert_grad.5 = (bf16[4,2,2,96,512]{4,3,2,1,0:T(8,128)(2,1)}, bf16[4,2,2,96,512]{4,3,2,1,0:T(8,128)(2,1)}, bf16[2,4,2,96,512]{4,3,2,1,0:T(8,128)(2,1)}, bf16[2,4,2,96,512]{4,3,2,1,0:T(8,128)(2,1)}) custom-call(s32[3]{0:T(128)} %pad_add_fusion.1.place_ref, bf16[512,2048]{1,0:T(8,128)(2,1)} %get-tuple-element.53.left_ref, ...), custom_call_target="tpu_custom_call" | custom-call | flops 3221225472 | bytes 10485760 | tf_op jit(solution)/shard_map/expert_grad/pallas_call | solution.py:552
  617.4 14.8 %collective-permute-done.52 = bf16[2,2,48,640]{3,2,1,0:T(8,128)(2,1)S(1)} collective-permute-done((bf16[2,2,48,640]{3,2,1,0:T(8,128)(2,1)S(1)}, bf16[2,2,48,640]{3,2,1,0:T(8,128)(2,1)S(1)}, u32[]{:S(2)}, u32[]{:S(2)}) %collective-permute-start.52) | collective-permute-done | bytes 245792 | tf_op jit(solution)/shard_map/ppermute | solution.py:68
  676.3 17.6 %collective-permute-done.75 = bf16[4,2,48,384]{3,2,1,0:T(8,128)(2,1)S(1)} collective-permute-done((bf16[4,2,48,384]{3,2,1,0:T(8,128)(2,1)S(1)}, bf16[4,2,48,384]{3,2,1,0:T(8,128)(2,1)S(1)}, u32[]{:S(2)}, u32[]{:S(2)}) %collective-permute-start.75) | collective-permute-done | bytes 294944 | tf_op jit(solution)/shard_map/ppermute | solution.py:68
  705.1 15.2 %collective-permute-done.107 = bf16[2,96,512]{2,1,0:T(8,128)(2,1)S(1)} collective-permute-done((bf16[2,96,512]{2,1,0:T(8,128)(2,1)S(1)}, bf16[2,96,512]{2,1,0:T(8,128)(2,1)S(1)}, u32[]{:S(2)}, u32[]{:S(2)}) %collective-permute-start.107) | collective-permute-done | bytes 196640 | tf_op jit(solution)/shard_map/ppermute | solution.py:68
  724.1 9.2 %collective-permute-done.85 = bf16[2,96,512]{2,1,0:T(8,128)(2,1)S(1)} collective-permute-done((bf16[2,96,512]{2,1,0:T(8,128)(2,1)S(1)}, bf16[2,96,512]{2,1,0:T(8,128)(2,1)S(1)}, u32[]{:S(2)}, u32[]{:S(2)}) %collective-permute-start.85) | collective-permute-done | bytes 196640 | tf_op jit(solution)/shard_map/ppermute | solution.py:68
  739.5 15.9 %collective-permute-done.97 = bf16[2,96,512]{2,1,0:T(8,128)(2,1)S(1)} collective-permute-done((bf16[2,96,512]{2,1,0:T(8,128)(2,1)S(1)}, bf16[2,96,512]{2,1,0:T(8,128)(2,1)S(1)}, u32[]{:S(2)}, u32[]{:S(2)}) %collective-permute-start.97) | collective-permute-done | bytes 196640 | tf_op jit(solution)/shard_map/ppermute | solution.py:68
  755.5 13.8 %collective-permute-start.64 = (bf16[4,2,4,2,48,640]{5,4,3,2,1,0:T(8,128)(2,1)}, bf16[4,2,4,2,48,640]{5,4,3,2,1,0:T(8,128)(2,1)}, u32[]{:S(2)}, u32[]{:S(2)}) collective-permute-start(bf16[4,2,4,2,48,640]{5,4,3,2,1,0:T(8,128)(2,1)} %maximum_bitcast_fusion.mine_ref), channel_id=1, source_target_pairs={{0,4},{4,0},{8,12},{12,8},{16,20},{20,16},{24,28},{28,24},{32,36},... | collective-permute-start | bytes 11796488 | tf_op jit(solution)/shard_map/ppermute | solution.py:68
  772.3 11.2 %collective-permute-done.78 = bf16[2,4,2,48,384]{4,3,2,1,0:T(8,128)(2,1)S(1)} collective-permute-done((bf16[2,4,2,48,384]{4,3,2,1,0:T(8,128)(2,1)S(1)}, bf16[2,4,2,48,384]{4,3,2,1,0:T(8,128)(2,1)S(1)}, u32[]{:S(2)}, u32[]{:S(2)}) %collective-permute-start.78) | collective-permute-done | bytes 589856 | tf_op jit(solution)/shard_map/ppermute | solution.py:38
  786.2 14.3 %collective-permute-done.76 = bf16[2,4,2,48,384]{4,3,2,1,0:T(8,128)(2,1)S(1)} collective-permute-done((bf16[2,4,2,48,384]{4,3,2,1,0:T(8,128)(2,1)S(1)}, bf16[2,4,2,48,384]{4,3,2,1,0:T(8,128)(2,1)S(1)}, u32[]{:S(2)}, u32[]{:S(2)}) %collective-permute-start.76) | collective-permute-done | bytes 589856 | tf_op jit(solution)/shard_map/ppermute | solution.py:38
  839.2 14.4 %into_layout.1 = (f32[1536,1536]{1,0:T(8,128)}, f32[1536,512]{1,0:T(8,128)}, f32[1536,512]{1,0:T(8,128)}) custom-call(s32[3]{0:T(128)} %pad_add_fusion.1.place_ref, s32[1]{0:T(128)} %bitcast.27.z_ref, bf16[4,2,4,2,48,640]{5,4,3,2,1,0:T(8,128)(2,1)} %maximum_bitcast_fusion.mine_ref, bf16[4,2,4,2,48,640]{5,4,3,2,1,0:T(8,128)(2,1)} %collective-permute-done.64.other_ref), custom_call_target="tpu_custom_call" | custom-call | bytes 23592960 | tf_op jit(solution)/shard_map/into_layout/pallas_call | solution.py:670
  (485 shorter events, 371.4 us)
Async XLA Ops:
  7.2 73.7 %all-gather.7.cloned.1.call-start = ((), (), s32[]{:S(2)}) async-start(), calls=%async_computation | async-start | bytes 6684672 | tf_op jit(solution)/shard_map/all_gather | solution.py:747
  8.0 92.6 %all-gather.9.cloned.1.call-start = ((), (), s32[]{:S(2)}) async-start(), calls=%async_computation.1 | async-start | bytes 6684672 | tf_op jit(solution)/shard_map/all_gather | solution.py:748
  8.7 136.6 %all-gather.11.cloned.1.call-start = ((), (), s32[]{:S(2)}) async-start(), calls=%async_computation.2 | async-start | bytes 6684672 | tf_op jit(solution)/shard_map/all_gather | solution.py:749
  9.4 29.1 %collective-permute-start = (bf16[2,64,1536]{2,1,0:T(8,128)(2,1)}, bf16[2,64,1536]{2,1,0:T(8,128)(2,1)S(1)}, u32[]{:S(2)}, u32[]{:S(2)}) collective-permute-start(bf16[2,64,1536]{2,1,0:T(8,128)(2,1)} %param.14), channel_id=1, source_target_pairs={{0,1},{1,2},{2,3},{3,0},{4,5},{5,6},{6,7},{7,4},{8,9},{9,10},{10,1... | collective-permute-start | bytes 1179656 | tf_op jit(solution)/shard_map/ppermute | solution.py:38
  12.0 26.6 %collective-permute-start.1 = (bf16[2,64,1536]{2,1,0:T(8,128)(2,1)}, bf16[2,64,1536]{2,1,0:T(8,128)(2,1)S(1)}, u32[]{:S(2)}, u32[]{:S(2)}) collective-permute-start(bf16[2,64,1536]{2,1,0:T(8,128)(2,1)} %param.14), channel_id=1, source_target_pairs={{0,2},{1,3},{2,0},{3,1},{4,6},{5,7},{6,4},{7,5},{8,10},{9,11},{10,... | collective-permute-start | bytes 1179656 | tf_op jit(solution)/shard_map/ppermute | solution.py:38
  192.8 20.5 %collective-permute-start.19 = (bf16[2,64,1536]{2,1,0:T(8,128)(2,1)S(1)}, bf16[2,64,1536]{2,1,0:T(8,128)(2,1)S(1)}, u32[]{:S(2)}, u32[]{:S(2)}) collective-permute-start(bf16[2,64,1536]{2,1,0:T(8,128)(2,1)S(1)} %copy-done.6), channel_id=1, source_target_pairs={{0,1},{1,2},{2,3},{3,0},{4,5},{5,6},{6,7},{7,4},{8,9},{9,10},{10,1... | collective-permute-start | bytes 1179656 | tf_op jit(solution)/shard_map/ppermute | solution.py:38
  197.4 25.4 %collective-permute-start.13 = (bf16[2,64,1536]{2,1,0:T(8,128)(2,1)S(1)}, bf16[2,64,1536]{2,1,0:T(8,128)(2,1)S(1)}, u32[]{:S(2)}, u32[]{:S(2)}) collective-permute-start(bf16[2,64,1536]{2,1,0:T(8,128)(2,1)S(1)} %collective-permute-done.12), channel_id=1, source_target_pairs={{0,1},{1,2},{2,3},{3,0},{4,5},{5,6},{6,7},{7,4},{8,9},{9,10},{10,1... | collective-permute-start | bytes 1179656 | tf_op jit(solution)/shard_map/ppermute | solution.py:38
  329.8 20.3 %collective-permute-start.25 = (bf16[2,64,1536]{2,1,0:T(8,128)(2,1)S(1)}, bf16[2,64,1536]{2,1,0:T(8,128)(2,1)S(1)}, u32[]{:S(2)}, u32[]{:S(2)}) collective-permute-start(bf16[2,64,1536]{2,1,0:T(8,128)(2,1)S(1)} %get-tuple-element.93), channel_id=1, source_target_pairs={{0,1},{1,2},{2,3},{3,0},{4,5},{5,6},{6,7},{7,4},{8,9},{9,10},{10,1... | collective-permute-start | bytes 1179656 | tf_op jit(solution)/shard_map/ppermute | solution.py:38
  406.8 20.8 %collective-permute-start.32 = (bf16[2,64,1536]{2,1,0:T(8,128)(2,1)S(1)}, bf16[2,64,1536]{2,1,0:T(8,128)(2,1)S(1)}, u32[]{:S(2)}, u32[]{:S(2)}) collective-permute-start(bf16[2,64,1536]{2,1,0:T(8,128)(2,1)S(1)} %collective-permute-done.31), channel_id=1, source_target_pairs={{0,1},{1,2},{2,3},{3,0},{4,5},{5,6},{6,7},{7,4},{8,9},{9,10},{10,1... | collective-permute-start | bytes 1179656 | tf_op jit(solution)/shard_map/ppermute | solution.py:38
  451.0 33.9 %collective-permute-start.18 = (bf16[2,64,1536]{2,1,0:T(8,128)(2,1)S(1)}, bf16[2,64,1536]{2,1,0:T(8,128)(2,1)S(1)}, u32[]{:S(2)}, u32[]{:S(2)}) collective-permute-start(bf16[2,64,1536]{2,1,0:T(8,128)(2,1)S(1)} %get-tuple-element.126), channel_id=1, source_target_pairs={{0,1},{1,2},{2,3},{3,0},{4,5},{5,6},{6,7},{7,4},{8,9},{9,10},{10,1... | collective-permute-start | bytes 1179656 | tf_op jit(solution)/shard_map/ppermute | solution.py:38
  451.7 33.3 %collective-permute-start.17 = (bf16[2,64,1536]{2,1,0:T(8,128)(2,1)S(1)}, bf16[2,64,1536]{2,1,0:T(8,128)(2,1)S(1)}, u32[]{:S(2)}, u32[]{:S(2)}) collective-permute-start(bf16[2,64,1536]{2,1,0:T(8,128)(2,1)S(1)} %get-tuple-element.127), channel_id=1, source_target_pairs={{0,2},{1,3},{2,0},{3,1},{4,6},{5,7},{6,4},{7,5},{8,10},{9,11},{10,... | collective-permute-start | bytes 1179656 | tf_op jit(solution)/shard_map/ppermute | solution.py:38
  489.7 21.1 %collective-permute-start.38 = (bf16[2,64,1536]{2,1,0:T(8,128)(2,1)}, bf16[2,64,1536]{2,1,0:T(8,128)(2,1)S(1)}, u32[]{:S(2)}, u32[]{:S(2)}) collective-permute-start(bf16[2,64,1536]{2,1,0:T(8,128)(2,1)} %get-tuple-element.91), channel_id=1, source_target_pairs={{0,1},{1,2},{2,3},{3,0},{4,5},{5,6},{6,7},{7,4},{8,9},{9,10},{10,1... | collective-permute-start | bytes 1179656 | tf_op jit(solution)/shard_map/ppermute | solution.py:38
  557.1 39.3 %collective-permute-start.86 = (bf16[2,4,2,96,512]{4,3,2,1,0:T(8,128)(2,1)}, bf16[2,4,2,96,512]{4,3,2,1,0:T(8,128)(2,1)}, u32[]{:S(2)}, u32[]{:S(2)}) collective-permute-start(bf16[2,4,2,96,512]{4,3,2,1,0:T(8,128)(2,1)} %get-tuple-element.73), channel_id=1, source_target_pairs={{0,4},{4,0},{8,12},{12,8},{16,20},{20,16},{24,28},{28,24},{32,36},... | collective-permute-start | bytes 4718600 | tf_op jit(solution)/shard_map/ppermute | solution.py:68
  557.1 41.9 %collective-permute-start.80 = (bf16[4,2,2,96,512]{4,3,2,1,0:T(8,128)(2,1)}, bf16[4,2,2,96,512]{4,3,2,1,0:T(8,128)(2,1)S(1)}, u32[]{:S(2)}, u32[]{:S(2)}) collective-permute-start(bf16[4,2,2,96,512]{4,3,2,1,0:T(8,128)(2,1)} %get-tuple-element.71), channel_id=1, source_target_pairs={{0,4},{4,0},{8,12},{12,8},{16,20},{20,16},{24,28},{28,24},{32,36},... | collective-permute-start | bytes 4718600 | tf_op jit(solution)/shard_map/ppermute | solution.py:68
  567.1 32.7 %collective-permute-start.98 = (bf16[2,4,2,96,512]{4,3,2,1,0:T(8,128)(2,1)}, bf16[2,4,2,96,512]{4,3,2,1,0:T(8,128)(2,1)}, u32[]{:S(2)}, u32[]{:S(2)}) collective-permute-start(bf16[2,4,2,96,512]{4,3,2,1,0:T(8,128)(2,1)} %get-tuple-element.78), channel_id=1, source_target_pairs={{0,4},{4,0},{8,12},{12,8},{16,20},{20,16},{24,28},{28,24},{32,36},... | collective-permute-start | bytes 4718600 | tf_op jit(solution)/shard_map/ppermute | solution.py:68
  606.8 55.6 %collective-permute-start.82 = (bf16[2,2,96,512]{3,2,1,0:T(8,128)(2,1)S(1)}, bf16[2,2,96,512]{3,2,1,0:T(8,128)(2,1)S(1)}, u32[]{:S(2)}, u32[]{:S(2)}) collective-permute-start(bf16[2,2,96,512]{3,2,1,0:T(8,128)(2,1)S(1)} %get-tuple-element.111), channel_id=1, source_target_pairs={{0,16},{4,20},{8,24},{12,28},{16,32},{20,36},{24,40},{28,44},{32,4... | collective-permute-start | bytes 1179656 | tf_op jit(solution)/shard_map/ppermute | solution.py:68
  608.7 56.4 %collective-permute-start.81 = (bf16[2,2,96,512]{3,2,1,0:T(8,128)(2,1)S(1)}, bf16[2,2,96,512]{3,2,1,0:T(8,128)(2,1)S(1)}, u32[]{:S(2)}, u32[]{:S(2)}) collective-permute-start(bf16[2,2,96,512]{3,2,1,0:T(8,128)(2,1)S(1)} %get-tuple-element.112), channel_id=1, source_target_pairs={{0,48},{4,52},{8,56},{12,60},{16,0},{20,4},{24,8},{28,12},{32,16},... | collective-permute-start | bytes 1179656 | tf_op jit(solution)/shard_map/ppermute | solution.py:68
  610.8 55.8 %collective-permute-start.94 = (bf16[2,2,96,512]{3,2,1,0:T(8,128)(2,1)S(1)}, bf16[2,2,96,512]{3,2,1,0:T(8,128)(2,1)S(1)}, u32[]{:S(2)}, u32[]{:S(2)}) collective-permute-start(bf16[2,2,96,512]{3,2,1,0:T(8,128)(2,1)S(1)} %get-tuple-element.105), channel_id=1, source_target_pairs={{0,16},{4,20},{8,24},{12,28},{16,32},{20,36},{24,40},{28,44},{32,4... | collective-permute-start | bytes 1179656 | tf_op jit(solution)/shard_map/ppermute | solution.py:68
  666.7 104.4 %collective-permute-start.87 = (bf16[4,2,96,512]{3,2,1,0:T(8,128)(2,1)S(1)}, bf16[4,2,96,512]{3,2,1,0:T(8,128)(2,1)S(1)}, u32[]{:S(2)}, u32[]{:S(2)}) collective-permute-start(bf16[4,2,96,512]{3,2,1,0:T(8,128)(2,1)S(1)} %slice_bitcast_fusion.4), channel_id=1, source_target_pairs={{0,8},{4,12},{8,0},{12,4},{16,24},{20,28},{24,16},{28,20},{32,40},... | collective-permute-start | bytes 2359304 | tf_op jit(solution)/shard_map/ppermute | solution.py:68
  666.8 27.2 %collective-permute-start.75 = (bf16[4,2,48,384]{3,2,1,0:T(8,128)(2,1)S(1)}, bf16[4,2,48,384]{3,2,1,0:T(8,128)(2,1)S(1)}, u32[]{:S(2)}, u32[]{:S(2)}) collective-permute-start(bf16[4,2,48,384]{3,2,1,0:T(8,128)(2,1)S(1)} %get-tuple-element.169), channel_id=1, source_target_pairs={{0,8},{4,12},{8,0},{12,4},{16,24},{20,28},{24,16},{28,20},{32,40},... | collective-permute-start | bytes 884744 | tf_op jit(solution)/shard_map/ppermute | solution.py:68
  673.1 21.0 %collective-permute-start.83 = (bf16[2,96,512]{2,1,0:T(8,128)(2,1)S(1)}, bf16[2,96,512]{2,1,0:T(8,128)(2,1)S(1)}, u32[]{:S(2)}, u32[]{:S(2)}) collective-permute-start(bf16[2,96,512]{2,1,0:T(8,128)(2,1)S(1)} %get-tuple-element.109), channel_id=1, source_target_pairs={{0,16},{4,20},{8,24},{12,28},{16,32},{20,36},{24,40},{28,44},{32,4... | collective-permute-start | bytes 589832 | tf_op jit(solution)/shard_map/ppermute | solution.py:68
  673.3 23.5 %collective-permute-start.84 = (bf16[2,96,512]{2,1,0:T(8,128)(2,1)S(1)}, bf16[2,96,512]{2,1,0:T(8,128)(2,1)S(1)}, u32[]{:S(2)}, u32[]{:S(2)}) collective-permute-start(bf16[2,96,512]{2,1,0:T(8,128)(2,1)S(1)} %get-tuple-element.110), channel_id=1, source_target_pairs={{0,48},{4,52},{8,56},{12,60},{16,0},{20,4},{24,8},{28,12},{32,16},... | collective-permute-start | bytes 589832 | tf_op jit(solution)/shard_map/ppermute | solution.py:68
  676.1 45.9 %collective-permute-start.62 = (bf16[2,2,4,48,640]{4,3,0,1,2:T(8,128)(2,1)S(1)}, bf16[2,2,4,48,640]{4,3,0,1,2:T(8,128)(2,1)S(1)}, u32[]{:S(2)}, u32[]{:S(2)}) collective-permute-start(bf16[2,2,4,48,640]{4,3,0,1,2:T(8,128)(2,1)S(1)} %copy.138), channel_id=1, source_target_pairs={{0,48},{4,52},{8,56},{12,60},{16,0},{20,4},{24,8},{28,12},{32,16},... | collective-permute-start | bytes 2949128 | tf_op jit(solution)/shard_map/ppermute | solution.py:68
  696.8 25.3 %collective-permute-start.60 = (bf16[2,2,4,48,640]{4,3,1,2,0:T(8,128)(2,1)S(1)}, bf16[2,2,4,48,640]{4,3,1,2,0:T(8,128)(2,1)S(1)}, u32[]{:S(2)}, u32[]{:S(2)}) collective-permute-start(bf16[2,2,4,48,640]{4,3,1,2,0:T(8,128)(2,1)S(1)} %get-tuple-element.132), channel_id=1, source_target_pairs={{0,16},{4,20},{8,24},{12,28},{16,32},{20,36},{24,40},{28,44},{32,4... | collective-permute-start | bytes 2949128 | tf_op jit(solution)/shard_map/ppermute | solution.py:68
  699.7 20.7 %collective-permute-start.107 = (bf16[2,96,512]{2,1,0:T(8,128)(2,1)S(1)}, bf16[2,96,512]{2,1,0:T(8,128)(2,1)S(1)}, u32[]{:S(2)}, u32[]{:S(2)}) collective-permute-start(bf16[2,96,512]{2,1,0:T(8,128)(2,1)S(1)} %get-tuple-element.97), channel_id=1, source_target_pairs={{0,16},{4,20},{8,24},{12,28},{16,32},{20,36},{24,40},{28,44},{32,4... | collective-permute-start | bytes 589832 | tf_op jit(solution)/shard_map/ppermute | solution.py:68
  701.6 20.2 %collective-permute-start.108 = (bf16[2,96,512]{2,1,0:T(8,128)(2,1)S(1)}, bf16[2,96,512]{2,1,0:T(8,128)(2,1)S(1)}, u32[]{:S(2)}, u32[]{:S(2)}) collective-permute-start(bf16[2,96,512]{2,1,0:T(8,128)(2,1)S(1)} %get-tuple-element.98), channel_id=1, source_target_pairs={{0,48},{4,52},{8,56},{12,60},{16,0},{20,4},{24,8},{28,12},{32,16},... | collective-permute-start | bytes 589832 | tf_op jit(solution)/shard_map/ppermute | solution.py:68
  720.4 51.0 %collective-permute-start.99 = (bf16[4,2,96,512]{3,2,1,0:T(8,128)(2,1)S(1)}, bf16[4,2,96,512]{3,2,1,0:T(8,128)(2,1)S(1)}, u32[]{:S(2)}, u32[]{:S(2)}) collective-permute-start(bf16[4,2,96,512]{3,2,1,0:T(8,128)(2,1)S(1)} %slice_bitcast_fusion.2), channel_id=1, source_target_pairs={{0,8},{4,12},{8,0},{12,4},{16,24},{20,28},{24,16},{28,20},{32,40},... | collective-permute-start | bytes 2359304 | tf_op jit(solution)/shard_map/ppermute | solution.py:68
  733.3 67.6 %collective-permute-start.111 = (bf16[4,2,96,512]{3,2,1,0:T(8,128)(2,1)S(1)}, bf16[4,2,96,512]{3,2,1,0:T(8,128)(2,1)S(1)}, u32[]{:S(2)}, u32[]{:S(2)}) collective-permute-start(bf16[4,2,96,512]{3,2,1,0:T(8,128)(2,1)S(1)} %slice_bitcast_fusion), channel_id=1, source_target_pairs={{0,8},{4,12},{8,0},{12,4},{16,24},{20,28},{24,16},{28,20},{32,40},... | collective-permute-start | bytes 2359304 | tf_op jit(solution)/shard_map/ppermute | solution.py:68
  735.6 34.4 %collective-permute-start.109 = (bf16[2,96,512]{2,1,0:T(8,128)(2,1)S(1)}, bf16[2,96,512]{2,1,0:T(8,128)(2,1)S(1)}, u32[]{:S(2)}, u32[]{:S(2)}) collective-permute-start(bf16[2,96,512]{2,1,0:T(8,128)(2,1)S(1)} %pad_maximum_fusion.11), channel_id=1, source_target_pairs={{0,8},{4,12},{8,0},{12,4},{16,24},{20,28},{24,16},{28,20},{32,40},... | collective-permute-start | bytes 589832 | tf_op jit(solution)/shard_map/ppermute | solution.py:68
  755.5 83.8 %collective-permute-start.64 = (bf16[4,2,4,2,48,640]{5,4,3,2,1,0:T(8,128)(2,1)}, bf16[4,2,4,2,48,640]{5,4,3,2,1,0:T(8,128)(2,1)}, u32[]{:S(2)}, u32[]{:S(2)}) collective-permute-start(bf16[4,2,4,2,48,640]{5,4,3,2,1,0:T(8,128)(2,1)} %maximum_bitcast_fusion.mine_ref), channel_id=1, source_target_pairs={{0,4},{4,0},{8,12},{12,8},{16,20},{20,16},{24,28},{28,24},{32,36},... | collective-permute-start | bytes 11796488 | tf_op jit(solution)/shard_map/ppermute | solution.py:68
  771.4 29.1 %collective-permute-start.76 = (bf16[2,4,2,48,384]{4,3,2,1,0:T(8,128)(2,1)S(1)}, bf16[2,4,2,48,384]{4,3,2,1,0:T(8,128)(2,1)S(1)}, u32[]{:S(2)}, u32[]{:S(2)}) collective-permute-start(bf16[2,4,2,48,384]{4,3,2,1,0:T(8,128)(2,1)S(1)} %get-tuple-element.159), channel_id=1, source_target_pairs={{0,1},{1,2},{2,3},{3,0},{4,5},{5,6},{6,7},{7,4},{8,9},{9,10},{10,1... | collective-permute-start | bytes 1769480 | tf_op jit(solution)/shard_map/ppermute | solution.py:38
  800.9 30.0 %collective-permute-start.79 = (bf16[4,2,4,2,48,384]{5,4,3,2,1,0:T(8,128)(2,1)S(1)}, bf16[4,2,4,2,48,384]{5,4,3,2,1,0:T(8,128)(2,1)}, u32[]{:S(2)}, u32[]{:S(2)}) collective-permute-start(bf16[4,2,4,2,48,384]{5,4,3,2,1,0:T(8,128)(2,1)S(1)} %pad_maximum_fusion.mine_ref), channel_id=1, source_target_pairs={{0,4},{4,0},{8,12},{12,8},{16,20},{20,16},{24,28},{28,24},{32,36},... | collective-permute-start | bytes 7077896 | tf_op jit(solution)/shard_map/ppermute | solution.py:68
  (138 other events, 1593.5 us)
Sparse Core Ops, SparseCore 0:
  9.7 45.9 all-gather.6
  57.3 43.1 all-gather.8
  102.2 43.0 all-gather.10

commit v2 on v1

v2 whole, which is shorter than its diff:
```python
import functools

import jax
import jax.numpy as jnp
from jax import lax
from jax.experimental import pallas as pl
from jax.experimental.pallas import tpu as pltpu
from jax.sharding import PartitionSpec as P

QUERY_HEADS = 24
KEY_VALUE_HEADS = 8
HEAD_SIZE = 64
GROUP = QUERY_HEADS // KEY_VALUE_HEADS
EPS = 1e-06
LOW = jnp.bfloat16
F32 = jnp.float32
MIB = 1024 * 1024
TINY = pl.CostEstimate(flops=1, bytes_accessed=1, transcendentals=0)


def params(*semantics, mib=30):
    return pltpu.CompilerParams(dimension_semantics=semantics, vmem_limit_bytes=mib * MIB)


def dot(left, right):
    return jnp.dot(left, right, preferred_element_type=F32)


def dot_nt(left, right):
    return lax.dot_general(left, right, (((1,), (1,)), ((), ())), preferred_element_type=F32)


def dot_tn(left, right):
    return lax.dot_general(left, right, (((0,), (0,)), ((), ())), preferred_element_type=F32)


def shifted(block, by):
    size = lax.axis_size("expert")
    return lax.ppermute(block, "expert", [(i, (i + by) % size) for i in range(size)])


def spread_group(block):
    return [block] + [shifted(block, j) for j in range(1, lax.axis_size("expert"))]


def gather_group(block):
    return jnp.concatenate(spread_group(block), 1)


def sum_to_owners(blocks):
    size = len(blocks)
    return added(blocks[0], *[shifted(blocks[j], size - j) for j in range(1, size)])


def to_section(block, target):
    return lax.ppermute(block, "section", [(1 - target, target)])


RING, PAIR, CORES = 4, 2, 2


def moved(block, x=0, y=0, core=0):
    route = []
    for i in range(RING):
        for j in range(PAIR):
            for k in range(CORES):
                target = ((i + x) % RING * PAIR + (j + y) % PAIR) * CORES + (k + core) % CORES
                route.append(((i * PAIR + j) * CORES + k, target))
    return lax.ppermute(block, "dp", route)


def added(*terms):
    total = terms[0].astype(F32)
    for term in terms[1:]:
        total = total + term.astype(F32)
    return total


def ring_step(blocks):
    return moved(blocks[:, 3:5], x=1), moved(blocks[:, 5:7], x=-1)


def ring_next(blocks, step):
    from_below, from_above = step
    below = moved(added(blocks[:, 2], from_below[:, 1]).astype(LOW), x=1)
    above = moved(added(blocks[:, 7], from_above[:, 0]).astype(LOW), x=-1)
    return below, above


def ring_end(blocks, step, last):
    first = added(blocks[:, 0], step[1][:, 1], last[0])
    return jnp.stack([first, added(blocks[:, 1], step[0][:, 0], last[1])])


def ring_gather_step(block):
    return moved(block, x=1), moved(block, x=-1)


def ring_gather_next(step):
    return moved(step[0][0], x=1), moved(step[1][1], x=-1)


def group_gather_step(block):
    return shifted(block, 1), shifted(block, 3)


def group_gather_next(step):
    return shifted(step[0][0], 1), shifted(step[1][1], 3)


def ring_stack(block, step, last):
    return jnp.stack([block, step[0], jnp.stack(last), step[1]])


def by_lanes(block):
    lanes = block.shape[-1] // 2
    return jnp.stack([block[..., :lanes], block[..., lanes:]])


def exchanged(values, axis, bit):
    return lax.ppermute(values, axis, [(i, i ^ bit) for i in range(lax.axis_size(axis))])


def hold(*values):
    return lax.optimization_barrier(values)


def swap_halves(values):
    half = HEAD_SIZE // 2
    lanes = values.shape[-1]
    lane = lax.broadcasted_iota(jnp.int32, values.shape, values.ndim - 1)
    ahead = pltpu.roll(values, lanes - half, values.ndim - 1)
    behind = pltpu.roll(values, half, values.ndim - 1)
    return jnp.where(lane % HEAD_SIZE < half, ahead, behind)


def widen_table(table, lanes):
    return jnp.concatenate([table] * (lanes // table.shape[-1]), -1)


def project_kernel(query_steps, x_ref, gain_ref, wq_ref, wk_ref, wv_ref, cos_ref, sin_ref, out_ref, xn_ref):
    step = pl.program_id(0)

    @pl.when(step == 0)
    def _():
        wide = x_ref[...].astype(F32)
        scale = lax.rsqrt(jnp.mean(wide * wide, -1, keepdims=True) + EPS)
        xn_ref[...] = (wide * scale * gain_ref[...]).astype(LOW)

    def turned(weight):
        product = dot(xn_ref[...], weight)
        lanes = product.shape[-1]
        cos, sin = widen_table(cos_ref[...], lanes), widen_table(sin_ref[...], lanes)
        return (product * cos + swap_halves(product) * sin).astype(LOW)

    @pl.when(step < query_steps)
    def _():
        out_ref[...] = turned(wq_ref[...])

    @pl.when(step == query_steps)
    def _():
        out_ref[...] = turned(wk_ref[...])

    @pl.when(step == query_steps + 1)
    def _():
        out_ref[...] = dot(xn_ref[...], wv_ref[...]).astype(LOW)


def project(x, gain, wq, wk, wv, cos, sin):
    rows, width = x.shape
    lanes = wk.shape[1]
    query_steps = wq.shape[1] // lanes
    whole = lambda *shape: pl.BlockSpec(shape, lambda i: (0,) * len(shape))
    return pl.pallas_call(
        functools.partial(project_kernel, query_steps),
        grid=(query_steps + 2,),
        in_specs=[
            whole(rows, width),
            whole(1, width),
            pl.BlockSpec((width, lanes), lambda i: (0, jnp.minimum(i, query_steps - 1))),
            whole(width, lanes),
            whole(width, lanes),
            whole(rows, cos.shape[1]),
            whole(rows, cos.shape[1]),
        ],
        out_specs=[pl.BlockSpec((rows, lanes), lambda i: (0, i)), whole(rows, width)],
        out_shape=[
            jax.ShapeDtypeStruct((rows, lanes * (query_steps + 2)), LOW),
            jax.ShapeDtypeStruct((rows, width), LOW),
        ],
        compiler_params=params("arbitrary"),
        cost_estimate=TINY,
        name="project",
    )(x, gain, wq, wk, wv, cos, sin)


def head(values, index):
    return values[:, index * HEAD_SIZE : (index + 1) * HEAD_SIZE]


def softmax_parts(stacked_q, key, bias):
    scores = dot_nt(stacked_q, key) * 0.125 + bias
    raised = jnp.exp(scores - jnp.max(scores, -1, keepdims=True))
    return raised * (1.0 / jnp.sum(raised, -1, keepdims=True))


def attend_kernel(q_ref, k_ref, v_ref, bias_ref, o_ref):
    bias = bias_ref[0]
    q, k, v = q_ref[0] * jnp.asarray(0.125, LOW), k_ref[0], v_ref[0]
    mixed = []
    for pair in range(k.shape[1] // HEAD_SIZE):
        key, value = head(k, pair), head(v, pair)
        for j in range(GROUP):
            scores = dot_nt(head(q, pair * GROUP + j), key) + bias
            raised = jnp.exp(scores - jnp.max(scores, -1, keepdims=True))
            total = jnp.sum(raised, -1, keepdims=True)
            mixed.append(dot(raised.astype(LOW), value) * (1.0 / total))
    o_ref[0] = jnp.concatenate(mixed, -1).astype(LOW)


def attend(qkv, bias, parts):
    batches, rows, lanes = qkv.shape
    k_lanes = KEY_VALUE_HEADS * HEAD_SIZE // parts
    q_lanes = k_lanes * GROUP
    k_at = parts * GROUP
    return pl.pallas_call(
        attend_kernel,
        grid=(batches, parts),
        in_specs=[
            pl.BlockSpec((1, rows, q_lanes), lambda b, c: (b, 0, c)),
            pl.BlockSpec((1, rows, k_lanes), lambda b, c: (b, 0, k_at + c)),
            pl.BlockSpec((1, rows, k_lanes), lambda b, c: (b, 0, k_at + parts + c)),
            pl.BlockSpec((1, rows, rows), lambda b, c: (b, 0, 0)),
        ],
        out_specs=pl.BlockSpec((1, rows, q_lanes), lambda b, c: (b, 0, c)),
        out_shape=jax.ShapeDtypeStruct((batches, rows, q_lanes * parts), LOW),
        compiler_params=params("arbitrary", "arbitrary"),
        cost_estimate=TINY,
        name="attend",
    )(qkv, qkv, qkv, bias)


def join_kernel(o_ref, x_ref, wo_ref, gain_ref, h1_ref, xn2_ref):
    total = x_ref[0].astype(F32) + dot(o_ref[0], wo_ref[...])
    scale = lax.rsqrt(jnp.mean(total * total, -1, keepdims=True) + EPS)
    h1_ref[0] = total[: h1_ref.shape[1]]
    xn2_ref[0] = (total * scale * gain_ref[...]).astype(LOW)


def join(o, x, wo, gain, own):
    batches, rows, width = x.shape
    batch = lambda *shape: pl.BlockSpec((1,) + shape, lambda b: (b, 0, 0))
    whole = lambda *shape: pl.BlockSpec(shape, lambda b: (0, 0))
    return pl.pallas_call(
        join_kernel,
        grid=(batches,),
        in_specs=[batch(rows, wo.shape[0]), batch(rows, width), whole(*wo.shape), whole(1, width)],
        out_specs=[batch(own, width), batch(rows, width)],
        out_shape=[
            jax.ShapeDtypeStruct((batches, own, width), F32),
            jax.ShapeDtypeStruct((batches, rows, width), LOW),
        ],
        compiler_params=params("arbitrary"),
        cost_estimate=TINY,
        name="join",
    )(o, x, wo, gain)


def expert_hidden(xn_ref, share_ref, wg_ref, wu_ref):
    gate, up = dot(xn_ref[...], wg_ref[0]), dot(xn_ref[...], wu_ref[0])
    share = share_ref[0]
    sigma = jax.nn.sigmoid(gate)
    silu = gate * sigma
    return gate, up, share, sigma, silu


def accumulate(total_ref, part):
    step = pl.program_id(0)

    @pl.when(step == 0)
    def _():
        total_ref[...] = part

    @pl.when(step > 0)
    def _():
        total_ref[...] += part


def hand_out(total_ref, out_refs):
    @pl.when(pl.program_id(0) == pl.num_programs(0) - 1)
    def _():
        batches, own, _ = out_refs[0].shape
        for b in range(batches):
            for j, ref in enumerate(out_refs):
                at = (b * len(out_refs) + j) * own
                ref[b] = total_ref[at : at + own].astype(LOW)


def experts_forward_kernel(place_ref, xn_ref, share_ref, *refs):
    pieces, out_refs = refs[:12], refs[12:-4]
    wg_ref, wu_ref, wd_ref, total_ref = refs[-4:]
    step = pl.program_id(0)
    high = wg_ref.shape[1] // (RING * PAIR * CORES)
    low = wd_ref.shape[1] // (RING * PAIR * CORES)

    def lay(block, x, y, core):
        ring = lax.rem(place_ref[0] + RING - x, RING)
        pair = lax.rem(place_ref[1] + y, PAIR)
        at = (ring * PAIR + pair) * CORES + lax.rem(place_ref[2] + core, CORES)
        rows = pl.ds(pl.multiple_of(at * high, high), high)
        wg_ref[0, rows] = block[0]
        wu_ref[0, rows] = block[1]
        outer = [block[2][k * low : (k + 1) * low] for k in range(high // low)]
        wd_ref[0, pl.ds(pl.multiple_of(at * low, low), low)] = jnp.concatenate(outer, -1)

    @pl.when(step < 2)
    def _():
        for core in range(CORES):
            for ref, xs in zip(pieces[core * 6 : core * 6 + 2], ((0, 1, 3), (2,))):
                for i, x in enumerate(xs):
                    for y in range(PAIR):
                        lay([ref[i, 0, y, k] for k in range(3)], x, y, core)

    @pl.when(step >= 2)
    def _():
        for core in range(CORES):
            for n, ref in enumerate(pieces[core * 6 + 2 : core * 6 + 6]):
                for i, x in enumerate((0, 1, 3) if n % 2 == 0 else (2,)):
                    lay([ref[i, 0, k] for k in range(3)], x, n // 2, core)

    _, up, share, _, silu = expert_hidden(xn_ref, share_ref, wg_ref, wu_ref)
    accumulate(total_ref, dot((silu * up * share).astype(LOW), wd_ref[0]))
    hand_out(total_ref, out_refs)


def experts_forward(place, xn, share, pieces, batches, parts):
    rows, width = xn.shape
    count = share.shape[0]
    high, units = pieces[0].shape[-2:]
    specs = []
    for piece in pieces:
        shape = (piece.shape[0], 1) + piece.shape[2:]
        near = len(shape) == 6
        index = lambda e, p, near=near, n=len(shape) - 2: (0, jnp.minimum(e, 1) if near else jnp.maximum(e - 2, 0)) + (0,) * n
        specs.append(pl.BlockSpec(shape, index))
    block = (batches, rows // batches // parts, width)
    matrix = lambda *shape: pl.BlockSpec((1,) + shape, lambda e, p: (e, 0, 0))
    return pl.pallas_call(
        experts_forward_kernel,
        grid_spec=pltpu.PrefetchScalarGridSpec(
            num_scalar_prefetch=1,
            grid=(count,),
            in_specs=[
                pl.BlockSpec((rows, width), lambda e, p: (0, 0)),
                pl.BlockSpec((1, rows, 1), lambda e, p: (e, 0, 0)),
            ]
            + specs,
            out_specs=[pl.BlockSpec(block, lambda e, p: (0, 0, 0))] * parts
            + [matrix(width, units), matrix(width, units), matrix(units, width)],
            scratch_shapes=[pltpu.VMEM((rows, width), F32)],
        ),
        out_shape=[jax.ShapeDtypeStruct(block, LOW)] * parts
        + [jax.ShapeDtypeStruct((count,) + shape, LOW) for shape in ((width, units), (width, units), (units, width))],
        compiler_params=params("arbitrary", mib=44),
        cost_estimate=TINY,
        name="experts_forward",
    )(place, xn, share, *pieces)


def experts_turn_kernel(xn_ref, share_ref, c_ref, wg_ref, wu_ref, wd_ref, hidden_ref, to_up_ref, to_gate_ref, *refs):
    gate, up, share, sigma, silu = expert_hidden(xn_ref, share_ref, wg_ref, wu_ref)
    shared = silu * share
    hidden_ref[...] = (shared * up).astype(LOW)
    to_up = shared.astype(LOW)
    to_gate = (share * up * sigma * (1.0 + gate * (1.0 - sigma))).astype(LOW)
    to_up_ref[...] = to_up
    to_gate_ref[...] = to_gate
    grads = dot_nt(c_ref[...], wd_ref[0])
    gate_grad = (grads * to_gate.astype(F32)).astype(LOW)
    up_grad = (grads * to_up.astype(F32)).astype(LOW)
    accumulate(refs[-1], dot_nt(gate_grad, wg_ref[0]) + dot_nt(up_grad, wu_ref[0]))
    hand_out(refs[-1], refs[:-1])


def experts_turn(xn, share, c, wg, wu, wd, batches, parts):
    rows, width = xn.shape
    count, _, units = wg.shape
    kept = pl.BlockSpec((rows, units), lambda e: (0, e))
    block = (batches, rows // batches // parts, width)
    return pl.pallas_call(
        experts_turn_kernel,
        grid=(count,),
        in_specs=[
            pl.BlockSpec((rows, width), lambda e: (0, 0)),
            pl.BlockSpec((1, rows, 1), lambda e: (e, 0, 0)),
            pl.BlockSpec((rows, width), lambda e: (0, 0)),
            pl.BlockSpec((1, width, units), lambda e: (e, 0, 0)),
            pl.BlockSpec((1, width, units), lambda e: (e, 0, 0)),
            pl.BlockSpec((1, units, width), lambda e: (e, 0, 0)),
        ],
        out_specs=[kept] * 3 + [pl.BlockSpec(block, lambda e: (0, 0, 0))] * parts,
        out_shape=[jax.ShapeDtypeStruct((rows, units * count), LOW)] * 3 + [jax.ShapeDtypeStruct(block, LOW)] * parts,
        scratch_shapes=[pltpu.VMEM((rows, width), F32)],
        compiler_params=params("arbitrary", mib=36),
        cost_estimate=TINY,
        name="experts_turn",
    )(xn, share, c, wg, wu, wd)


def experts_backward_kernel(c_ref, up_ref, gate_ref, wg_ref, wu_ref, wd_ref, *refs):
    total_ref = refs[-1]
    hidden = dot_nt(c_ref[...], wd_ref[0])
    gate_grad = (hidden * gate_ref[...].astype(F32)).astype(LOW)
    up_grad = (hidden * up_ref[...].astype(F32)).astype(LOW)
    refs[-2][0] = gate_grad
    refs[-2][1] = up_grad
    accumulate(total_ref, dot_nt(gate_grad, wg_ref[0]) + dot_nt(up_grad, wu_ref[0]))
    hand_out(total_ref, refs[:-2])


def experts_backward(c, to_up, to_gate, wg, wu, wd, batches, parts):
    rows, width = c.shape
    count, _, units = wg.shape
    kept = pl.BlockSpec((rows, units), lambda e: (0, e))
    block = (batches, rows // batches // parts, width)
    return pl.pallas_call(
        experts_backward_kernel,
        grid=(count,),
        in_specs=[
            pl.BlockSpec((rows, width), lambda e: (0, 0)),
            kept,
            kept,
            pl.BlockSpec((1, width, units), lambda e: (e, 0, 0)),
            pl.BlockSpec((1, width, units), lambda e: (e, 0, 0)),
            pl.BlockSpec((1, units, width), lambda e: (e, 0, 0)),
        ],
        out_specs=[pl.BlockSpec(block, lambda e: (0, 0, 0))] * parts
        + [pl.BlockSpec((2, rows, units), lambda e: (0, 0, e))],
        out_shape=[jax.ShapeDtypeStruct(block, LOW)] * parts
        + [jax.ShapeDtypeStruct((2, rows, units * count), LOW)],
        scratch_shapes=[pltpu.VMEM((rows, width), F32)],
        compiler_params=params("arbitrary"),
        cost_estimate=TINY,
        name="experts_backward",
    )(c, to_up, to_gate, wg, wu, wd)


def head_grads(queries, key, value, douts, bias):
    probs = softmax_parts(queries, key, bias)
    dprobs = dot_nt(douts, value)
    centre = jnp.sum(probs * dprobs, -1, keepdims=True)
    dscores = (probs * (dprobs - centre) * 0.125).astype(LOW)
    return dot(dscores, key), dot_tn(dscores, queries), dot_tn(probs.astype(LOW), douts)


def stacked_heads(values, pair):
    return jnp.concatenate([head(values, pair * GROUP + j) for j in range(GROUP)], 0)


def chunk_grads(q, k, v, dout, bias):
    rows = q.shape[0]
    bias = jnp.concatenate([bias] * GROUP, 0)
    dqs, dks, dvs = [], [], []
    for pair in range(k.shape[1] // HEAD_SIZE):
        dquery, dkey, dvalue = head_grads(stacked_heads(q, pair), head(k, pair), head(v, pair), stacked_heads(dout, pair), bias)
        dqs += [dquery[j * rows : (j + 1) * rows] for j in range(GROUP)]
        dks.append(dkey)
        dvs.append(dvalue)
    return jnp.concatenate(dqs, -1), jnp.concatenate(dks, -1), jnp.concatenate(dvs, -1).astype(LOW)


def turned_back(grads, cos, sin):
    lanes = grads.shape[-1]
    return (grads * widen_table(cos, lanes) + swap_halves(grads * widen_table(sin, lanes))).astype(LOW)


def attend_backward_kernel(
    z_ref, q_ref, k_ref, v_ref, da_ref, wo_ref, wq_ref, wk_ref, wv_ref, bias_ref, cos_ref, sin_ref, dqkv_ref, dn_ref
):
    dout = dot_nt(da_ref[0], wo_ref[...]).astype(LOW)
    dq, dk, dv = chunk_grads(q_ref[0], k_ref[0], v_ref[0], dout, bias_ref[0])
    dq, dk = turned_back(dq, cos_ref[...], sin_ref[...]), turned_back(dk, cos_ref[...], sin_ref[...])
    dqkv_ref[0] = jnp.concatenate([dq, dk, dv], -1)
    dn = dot_nt(dq, wq_ref[...]) + dot_nt(dk, wk_ref[...]) + dot_nt(dv, wv_ref[...])
    parts, _, own, _ = dn_ref.shape
    for j in range(parts):
        dn_ref[lax.rem(z_ref[0] + parts - j, parts), 0] = dn[j * own : (j + 1) * own].astype(LOW)


def attend_backward(z, qkv, da, wo, wq, wk, wv, bias, cos, sin, parts):
    batches, rows, width = da.shape
    q_lanes, k_lanes = wo.shape[0] // parts, KEY_VALUE_HEADS * HEAD_SIZE // parts
    k_at = wo.shape[0] // k_lanes
    full = lambda *shape: pl.BlockSpec(shape, lambda b, z: (0,) * len(shape))
    batch = lambda *shape: pl.BlockSpec((1,) + shape, lambda b, z: (b, 0, 0))
    columns = lambda lanes: pl.BlockSpec((width, lanes), lambda b, z: (0, z[0]))
    return pl.pallas_call(
        attend_backward_kernel,
        grid_spec=pltpu.PrefetchScalarGridSpec(
            num_scalar_prefetch=1,
            grid=(batches,),
            in_specs=[
                pl.BlockSpec((1, rows, q_lanes), lambda b, z: (b, 0, z[0])),
                pl.BlockSpec((1, rows, k_lanes), lambda b, z: (b, 0, k_at + z[0])),
                pl.BlockSpec((1, rows, k_lanes), lambda b, z: (b, 0, k_at + parts + z[0])),
                batch(rows, width),
                pl.BlockSpec((q_lanes, width), lambda b, z: (z[0], 0)),
                columns(q_lanes),
                columns(k_lanes),
                columns(k_lanes),
                batch(rows, rows),
                full(rows, cos.shape[1]),
                full(rows, cos.shape[1]),
            ],
            out_specs=[
                batch(rows, q_lanes + 2 * k_lanes),
                pl.BlockSpec((parts, 1, rows // parts, width), lambda b, z: (0, b, 0, 0)),
            ],
        ),
        out_shape=[
            jax.ShapeDtypeStruct((batches, rows, q_lanes + 2 * k_lanes), LOW),
            jax.ShapeDtypeStruct((parts, batches, rows // parts, width), LOW),
        ],
        compiler_params=params("arbitrary"),
        cost_estimate=TINY,
        name="attend_backward",
    )(z, qkv, qkv, qkv, da, wo, wq, wk, wv, bias, cos, sin)


def own_backward_kernel(q_ref, k_ref, v_ref, da_ref, wo_ref, bias_ref, cos_ref, sin_ref, dq_ref, *out_refs):
    batches, own, _ = q_ref.shape
    da = jnp.concatenate([da_ref[b] for b in range(batches)], 0)
    dout = dot_nt(da, wo_ref[...]).astype(LOW)
    lanes = k_ref.shape[-1]
    at = pl.multiple_of(pl.program_id(0) * lanes, lanes)
    middle = out_refs[0].shape[-1] // 2
    for b in range(batches):
        dq, dk, dv = chunk_grads(q_ref[b], k_ref[b], v_ref[b], dout[b * own : (b + 1) * own], bias_ref[b])
        dq_ref[b] = turned_back(dq, cos_ref[:own], sin_ref[:own])
        dk = turned_back(dk, cos_ref[...], sin_ref[...])
        for j, ref in enumerate(out_refs):
            ref[b, :, pl.ds(at, lanes)] = dk[j * own : (j + 1) * own]
            ref[b, :, pl.ds(middle + at, lanes)] = dv[j * own : (j + 1) * own]


def own_backward(qkv, da, wo, bias, cos, sin, parts):
    batches, own, width = da.shape
    rows = qkv.shape[1]
    k_lanes = KEY_VALUE_HEADS * HEAD_SIZE // parts
    q_lanes = k_lanes * GROUP
    k_at = parts * GROUP
    full = lambda *shape: pl.BlockSpec(shape, lambda c: (0,) * len(shape))
    block = (batches, own, 2 * k_lanes * parts)
    return pl.pallas_call(
        own_backward_kernel,
        grid=(parts,),
        in_specs=[
            pl.BlockSpec((batches, own, q_lanes), lambda c: (0, 0, c)),
            pl.BlockSpec((batches, rows, k_lanes), lambda c: (0, 0, k_at + c)),
            pl.BlockSpec((batches, rows, k_lanes), lambda c: (0, 0, k_at + parts + c)),
            full(batches, own, width),
            pl.BlockSpec((q_lanes, width), lambda c: (c, 0)),
            full(batches, own, rows),
            full(rows, cos.shape[1]),
            full(rows, cos.shape[1]),
        ],
        out_specs=[pl.BlockSpec((batches, own, q_lanes), lambda c: (0, 0, c))] + [full(*block)] * parts,
        out_shape=[jax.ShapeDtypeStruct((batches, own, q_lanes * parts), LOW)] + [jax.ShapeDtypeStruct(block, LOW)] * parts,
        compiler_params=params("arbitrary"),
        cost_estimate=TINY,
        name="own_backward",
    )(qkv, qkv, qkv, da, wo, bias, cos, sin)


def chip_block(place_ref, x, y, core):
    ring = lax.rem(place_ref[0] + x, RING)
    pair = lax.rem(place_ref[1] + y, PAIR)
    return (ring * PAIR + pair) * CORES + lax.rem(place_ref[2] + core, CORES)


def expert_grad_kernel(cut, place_ref, left_ref, right_ref, mine_ref, other_ref, turned_ref):
    rows = mine_ref.shape[-2] // cut
    lanes = mine_ref.shape[-1]
    step = pl.program_id(1)
    if cut == 1:

        @pl.when((pl.program_id(0) == 0) & (step == 0))
        def _():
            turned_ref[...] = left_ref[...].T

        product = dot(turned_ref[...], right_ref[0]).astype(LOW)
    else:
        product = dot_tn(left_ref[...], right_ref[0]).astype(LOW)
    half = lax.rem(step, 2)

    def place(refs, ring_first):
        for i in range(RING):
            x = lax.rem(i + RING - place_ref[0], RING)
            for j in range(PAIR):
                y = lax.rem(j + PAIR - place_ref[1], PAIR)
                index = (x * 2 + half) * PAIR + y if ring_first else (y * RING + x) * 2 + half
                for core in range(CORES):
                    at = ((i * PAIR + j) * CORES + core) * rows
                    for part in range(cut):
                        value = product[at : at + rows, part * lanes : (part + 1) * lanes]
                        refs[core][0, 0, index, part * rows : (part + 1) * rows] = value

    for core in range(CORES):
        for ring_first in (True, False):

            @pl.when((place_ref[2] == core) & ((step < 2) == ring_first))
            def _(core=core, ring_first=ring_first):
                place((mine_ref, other_ref) if core == 0 else (other_ref, mine_ref), ring_first)


def expert_grad(place, left, right, count, cut):
    number, rows, _ = right.shape
    left_lanes = left.shape[1] // count if cut > 1 else left.shape[1]
    right_lanes = right.shape[2] if cut > 1 else right.shape[2] // count
    owners = RING * PAIR * CORES
    high, lanes = left_lanes // owners, right_lanes // cut
    shape = (2, owners, high * cut, lanes)
    out = pl.BlockSpec((1, 1) + shape[1:], lambda r, e, p: (r, e // 2, 0, 0, 0))
    left_spec = pl.BlockSpec((rows, left_lanes), lambda r, e, p: (0, e if cut > 1 else 0))
    right_spec = pl.BlockSpec((1, rows, right_lanes), lambda r, e, p: (r, 0, 0 if cut > 1 else e))
    return pl.pallas_call(
        functools.partial(expert_grad_kernel, cut),
        grid_spec=pltpu.PrefetchScalarGridSpec(
            num_scalar_prefetch=1,
            grid=(number, count),
            in_specs=[left_spec, right_spec],
            out_specs=[out, out],
            scratch_shapes=[pltpu.VMEM((left_lanes, rows) if cut == 1 else (16, 128), LOW)],
        ),
        out_shape=[jax.ShapeDtypeStruct((number,) + shape, LOW)] * 2,
        compiler_params=params("arbitrary", "arbitrary"),
        name="expert_grad",
    )(place, left, right)


def dense_grad_kernel(
    place_ref, z_ref, mixed_ref, da_ref, xn_ref, dqkv_ref, mine_ref, other_ref, into_ref, out_of_ref
):
    del z_ref
    high = mine_ref.shape[-2]
    lanes, wide = out_of_ref.shape[-1], dqkv_ref.shape[1]
    into = dot_tn(xn_ref[...], dqkv_ref[...]).astype(LOW)
    out_of = dot_tn(mixed_ref[...], da_ref[...]).astype(LOW)
    for chip in range(RING * PAIR):
        for core in range(CORES):
            owner = chip * CORES + core
            for half in range(2):
                at = (owner * 2 + half) * high
                into_ref[owner, half] = into[at : at + high]
                at = (half * CORES + core) * lanes
                out_of_ref[owner, half] = out_of[chip * high : (chip + 1) * high, at : at + lanes]
    for core, ref in enumerate((mine_ref, other_ref)):
        for x in range(RING):
            for y in range(PAIR):
                owner = chip_block(place_ref, x, y, core)
                for half in range(2):
                    ref[0, x * 2 + half, y, :, :wide] = into_ref[owner, half]
                    ref[0, x * 2 + half, y, :, wide:] = out_of_ref[owner, half]


def dense_grad(place, z, mixed, da, xn, dqkv, parts):
    rows, width = xn.shape
    owners = RING * PAIR * CORES
    q_lanes, wide = mixed.shape[1] // parts, dqkv.shape[1]
    high, lanes = width // owners // 2, width // CORES // 2
    shape = (1, 2 * RING, PAIR, high, wide + lanes)
    whole = lambda columns: pl.BlockSpec((rows, columns), lambda i, p, z: (0, 0))
    return pl.pallas_call(
        dense_grad_kernel,
        grid_spec=pltpu.PrefetchScalarGridSpec(
            num_scalar_prefetch=2,
            grid=(1,),
            in_specs=[
                pl.BlockSpec((rows, q_lanes), lambda i, p, z: (0, z[0])),
                whole(width),
                whole(width),
                whole(wide),
            ],
            out_specs=[pl.BlockSpec(shape, lambda i, p, z: (0,) * 5)] * 2,
            scratch_shapes=[pltpu.VMEM((owners, 2, high, wide), LOW), pltpu.VMEM((owners, 2, high, lanes), LOW)],
        ),
        out_shape=[jax.ShapeDtypeStruct(shape, LOW)] * 2,
        compiler_params=params("arbitrary"),
        cost_estimate=TINY,
        name="dense_grad",
    )(place, z, mixed, da, xn, dqkv)


def dense_layout_kernel(by_x, place_ref, z_ref, mine_ref, other_ref, *refs):
    outs = refs[-4:]
    parts = mine_ref.shape[3] if by_x else mine_ref.shape[0]
    wide = mine_ref.shape[-1]
    for core, ref in enumerate((mine_ref, other_ref)):
        to_core = lax.rem(place_ref[2] + core, CORES)
        for y in range(PAIR):
            to_y = lax.rem(place_ref[1] + y, PAIR)
            for k in range(parts):
                at = lax.rem(z_ref[0] + parts - k, parts)
                start = 0
                for out in outs:
                    to_rows = out is outs[3]
                    lanes = out.shape[-1] // (CORES if to_rows else parts)
                    by, begin = divmod(start, wide)
                    index = (0, by, y, k) if by_x else (k, by, y, 0)
                    value = ref[index + (slice(None), slice(begin, begin + lanes))].astype(F32)
                    if to_rows:
                        out[at, 0, to_y, :, pl.ds(pl.multiple_of(to_core * lanes, 128), lanes)] = value
                    else:
                        out[0, to_y, to_core, 0, :, pl.ds(pl.multiple_of(at * lanes, 128), lanes)] = value
                    start += lanes


def dense_layout(place, z, half, mine, other, shapes, before):
    by_x = half == 0
    high, lanes = mine.shape[-2:]
    parts = mine.shape[3] if by_x else mine.shape[0]
    if by_x:
        source = pl.BlockSpec((1, 2, PAIR, parts, high, lanes), lambda x, p, z: (x, 0, 0, 0, 0, 0))
    else:
        source = pl.BlockSpec((parts, 2, PAIR, 1, high, lanes), lambda x, p, z: (0, 0, 0, x, 0, 0))
    ring = lambda x, p: lax.rem(p[0] + RING - x, RING)
    width = shapes[3][1]
    shapes = [(RING, PAIR, CORES, 2, high, shape[1]) for shape in shapes[:3]] + [(parts, RING, PAIR, high, width)]
    out_specs = [
        pl.BlockSpec((1, PAIR, CORES, 1, high, shape[-1]), lambda x, p, z: (ring(x, p), 0, 0, half, 0, 0)) for shape in shapes[:3]
    ] + [pl.BlockSpec((parts, 1, PAIR, high, width // 2), lambda x, p, z: (0, ring(x, p), 0, 0, half))]
    return pl.pallas_call(
        functools.partial(dense_layout_kernel, by_x),
        grid_spec=pltpu.PrefetchScalarGridSpec(
            num_scalar_prefetch=2,
            grid=(RING,),
            in_specs=[source, source] + [pl.BlockSpec(memory_space=pl.ANY)] * len(before),
            out_specs=out_specs,
        ),
        out_shape=[jax.ShapeDtypeStruct(shape, F32) for shape in shapes],
        input_output_aliases={4 + i: i for i in range(len(before))},
        compiler_params=params("arbitrary"),
        cost_estimate=pl.CostEstimate(flops=0, bytes_accessed=24 * mine.size, transcendentals=0),
        name="dense_layout",
    )(place, z, mine, other, *before)


def norm_back(grad_normed, values, gain):
    scale = lax.rsqrt(jnp.mean(values * values, -1, keepdims=True) + EPS)
    scaled = grad_normed * gain
    gain_grad = jnp.sum(grad_normed * values * scale, (0, 1))
    inner = jnp.mean(scaled * values, -1, keepdims=True)
    return (scale * scaled - values * scale * scale * scale * inner, gain_grad)


def local(
    block_input, segments, expert_ids, route_weights, attn_gain, w_query, key_projection_weight,
    value_projection_weight, w_out, ffn_gain, w_gate, w_up, w_down, out_grad,
):
    parts = lax.axis_size("expert")
    section = lax.axis_index("section")
    z = lax.axis_index("expert")
    z_at = z.reshape(1)
    dp = lax.axis_index("dp")
    dp_place = jnp.stack([dp // (PAIR * CORES), dp // CORES % PAIR, dp % CORES])
    batches, own, width = block_input.shape
    rows = parts * own
    wq, wk, wv, wo = w_query[0], key_projection_weight[0], value_projection_weight[0], w_out[0]
    local_experts, units = w_gate.shape[1], w_gate.shape[3]

    outer = w_down[0].reshape(local_experts, -1, width // units, units)
    outer = jnp.swapaxes(outer, 1, 2).reshape(w_gate[0].shape)
    shard = jnp.stack([w_gate[0], w_up[0], outer], 1)
    near, far = shard[:2], shard[2:]
    numbers = jnp.arange(parts * local_experts, dtype=jnp.int32)
    hits = expert_ids[0][..., None] == numbers
    shares = jnp.sum(jnp.where(hits, route_weights[0][..., None], 0.0), 2)
    shares = jnp.concatenate([shares, segments.astype(F32)[..., None]], -1)
    start = spread_group(block_input)
    near_y = moved(near, y=1)
    far_1 = ring_gather_step(far)
    shares = spread_group(shares)
    start, near_y, far_1, shares = hold(start, near_y, far_1, shares)

    start = jnp.concatenate(start, 1)
    shares = jnp.concatenate(shares, 1)
    labels = shares[..., -1]
    shares = shares[..., :-1].reshape(batches * rows, parts, local_experts)
    share = lax.dynamic_index_in_dim(shares, z, 1, keepdims=False).T[..., None]
    block = jnp.arange(parts, dtype=jnp.int32)[:, None]
    place = ((z - block) % parts * own + jnp.arange(own, dtype=jnp.int32)[None, :]).reshape(rows)
    allowed = (place[None, None, :] <= place[None, :, None]) & (labels[:, None, :] == labels[:, :, None])
    bias = jnp.where(allowed, 0.0, -1e30).astype(F32)
    half = HEAD_SIZE // 2
    frequency = 10000.0 ** (-jnp.arange(half, dtype=F32) * 2.0 / HEAD_SIZE)
    angles = place.astype(F32)[:, None] * frequency[None, :]
    cos_half, sin_half = jnp.cos(angles), jnp.sin(angles)
    cos = jnp.concatenate([cos_half] * 4, -1)
    sin = jnp.concatenate([-sin_half, sin_half] * 2, -1)
    cos_all, sin_all = jnp.concatenate([cos] * batches, 0), jnp.concatenate([sin] * batches, 0)

    def attention_in(x):
        qkv, xn = project(x.reshape(batches * rows, width), attn_gain, wq, wk, wv, cos_all, sin_all)
        return qkv.reshape(batches, rows, -1), xn

    def attention_out(qkv, x):
        mixed = attend(qkv, bias, parts)
        h1, xn2 = join(mixed, x, wo, ffn_gain, own)
        return mixed.reshape(batches * rows, -1), h1, xn2.reshape(batches * rows, width)

    near = jnp.stack([near, near_y], 1)
    near_1 = ring_gather_step(near)
    far_2 = ring_gather_next(far_1)
    far_a = jnp.stack([far, *far_1])
    far_ya = moved(far_a, y=1)
    qkv, _ = attention_in(start)
    _, h1, xn2 = attention_out(qkv, start)

    xn2, near_1, far_2, far_ya = hold(xn2, near_1, far_2, far_ya)
    near_a = jnp.stack([near, *near_1])
    near_b = ring_gather_next(near_1)
    far_b = jnp.stack(far_2)[None]
    far_yb = moved(far_b, y=1)
    others = [moved(piece, core=1) for piece in (near_a, far_a, far_b, far_ya)]

    near_b, far_yb, others = hold(near_b, far_yb, others)
    near_b = jnp.stack(near_b)[None]
    others = [others[0], moved(near_b, core=1), *others[1:], moved(far_yb, core=1)]
    pieces = [near_a, near_b, far_a, far_b, far_ya, far_yb, *others]
    *blocks, wg, wu, wd = experts_forward(dp_place, xn2, share, pieces, batches, parts)
    c_second = lax.all_gather(out_grad, "expert")
    c_second = jnp.concatenate([lax.dynamic_index_in_dim(c_second, (z + parts - j) % parts, 0, False) for j in range(parts)], 1)
    result = (h1 + sum_to_owners(blocks)).astype(LOW)
    received = gather_group(to_section(result, 1))

    x = jnp.where(section == 0, start, received)
    qkv, xn = attention_in(x)
    mixed, h1, xn2 = attention_out(qkv, x)
    flat_second = c_second.reshape(batches * rows, width)
    hidden, to_up, to_gate, *blocks = experts_turn(xn2, share, flat_second, wg, wu, wd, batches, parts)

    def after_experts(blocks, c_own):
        norm_part, ffn_grad = norm_back(sum_to_owners(blocks), h1, ffn_gain)
        return c_own.astype(F32) + norm_part, ffn_grad

    def after_attention(after, dn_own):
        norm_part, attn_grad = norm_back(dn_own, x[:, :own].astype(F32), attn_gain)
        return after + norm_part, attn_grad

    outputs = dot(hidden, wd.reshape(local_experts * units, width)).astype(LOW).reshape(batches, parts, own, width)
    outputs = jnp.flip(jnp.moveaxis(outputs, 1, 0), 0)
    outputs = lax.dynamic_slice_in_dim(jnp.concatenate([outputs, outputs], 0), (2 * parts - 1 - z) % parts, parts, 0)
    after, _ = after_experts(blocks, out_grad)
    after, outputs = hold(after, outputs)
    dq, *blocks = own_backward(qkv, after.astype(LOW), wo, bias, cos, sin, parts)
    dn_own = dot_nt(dq.reshape(batches * own, -1), wq)
    dkv = sum_to_owners(blocks).astype(LOW).reshape(batches * own, -1)
    dn_own = dn_own + dot_nt(dkv[:, : wk.shape[1]], wk) + dot_nt(dkv[:, wk.shape[1] :], wv)
    input_grad, _ = after_attention(after, dn_own.reshape(batches, own, width))
    received_own = to_section(input_grad.astype(LOW), 0)

    c_own = jnp.where(section == 1, out_grad, received_own)
    c = jnp.where(section == 1, c_second, gather_group(received_own))
    flat_c = c.reshape(batches * rows, width)
    *blocks, hidden_grads = experts_backward(flat_c, to_up, to_gate, wg, wu, wd, batches, parts)
    after, ffn_grad = after_experts(blocks, c_own)
    both = [
        expert_grad(dp_place, xn2, hidden_grads, local_experts, 1),
        expert_grad(dp_place, hidden, flat_c[None], local_experts, width // units),
    ]
    after, both = hold(after, both)
    both = [(mine, moved(other, core=1)) for mine, other in both]
    da = gather_group(after.astype(LOW))
    by_ring, by_pair = (
        jnp.concatenate([added(mine[:, kind], other[:, kind]).astype(LOW) for mine, other in both], 0) for kind in range(2)
    )
    by_ring = by_ring.reshape((-1, 2 * RING, PAIR) + by_ring.shape[2:])
    by_pair = by_pair.reshape((-1, PAIR, 2 * RING) + by_pair.shape[2:])
    da, by_ring, by_pair = hold(da, by_ring, by_pair)

    ring_1 = ring_step(by_ring)
    pair_1 = [moved(by_pair[:, 1, :RING], y=1), moved(by_pair[:, 1, RING:], y=1)]
    dqkv, dn = attend_backward(z_at, qkv, da, wo, wq, wk, wv, bias, cos, sin, parts)
    mine, other = dense_grad(
        dp_place, z_at, mixed, da.reshape(batches * rows, width), xn, dqkv.reshape(batches * rows, -1), parts
    )
    dn_own = lax.psum_scatter(dn, "expert", scatter_dimension=0, tiled=True)[0].astype(F32)

    mine, other, ring_1, pair_1[0] = hold(mine, other, ring_1, pair_1[0])
    dense = added(mine, moved(other, core=1)).astype(LOW)

    (dense,) = hold(dense)
    dense_1 = ring_step(dense)

    dense_1, dn_own = hold(dense_1, dn_own)
    dense_2 = ring_next(dense, dense_1)
    ring_2 = ring_next(by_ring, ring_1)
    input_grad, attn_grad = after_attention(after, dn_own)
    gains = jnp.stack([attn_grad, ffn_grad])
    gains = gains + exchanged(gains, "expert", 1)

    dense_2, gains, ring_2 = hold(dense_2, gains, ring_2)
    dense = ring_end(dense, dense_1, dense_2)[:, 0]
    dense_3 = moved(dense[:, 1].astype(LOW), y=1)
    gains = gains + exchanged(gains, "expert", 2)
    ring_sums = ring_end(by_ring, ring_1, ring_2)

    dense_3, gains, ring_sums, pair_1 = hold(dense_3, gains, ring_sums, pair_1)
    owned = added(dense[:, 0], dense_3).astype(LOW)
    first, second = owned[0], by_lanes(owned[1])
    first_1 = [shifted(first, k) for k in range(1, parts)]
    second_1 = [moved(second, x=k) for k in range(1, RING)]
    pair_sums = added(by_pair[:, 0], jnp.concatenate(pair_1, 1)).astype(LOW)

    first_1, second_1, pair_sums = hold(first_1, second_1, pair_sums)
    first = jnp.stack([first] + first_1)
    first_2 = moved(first, y=1)
    second = jnp.stack([second] + second_1)
    second_2 = moved(second, y=1)
    pair_2 = ring_step(pair_sums)
    gains = gains + exchanged(gains, "dp", 1)

    first_2, second_2, gains, pair_2 = hold(first_2, second_2, gains, pair_2)
    first = by_lanes(jnp.stack([first, first_2]))
    first_3 = ring_gather_step(first)
    second = jnp.moveaxis(jnp.stack([second, second_2]), 2, 0)
    second_3 = group_gather_step(second)
    ring_away = moved(ring_sums[:, :, 1].astype(LOW), y=1)
    gains = gains + exchanged(gains, "dp", 2)

    first_3, second_3, ring_away, gains = hold(first_3, second_3, ring_away, gains)
    first_4 = ring_gather_next(first_3)
    second_4 = group_gather_next(second_3)
    pair_3 = ring_next(pair_sums, pair_2)
    ring_sums = added(ring_sums[:, :, 0], ring_away)

    first_4, second_4, pair_3, ring_sums = hold(first_4, second_4, pair_3, ring_sums)
    first = ring_stack(first, first_3, first_4)
    first_other = moved(first, core=1)
    pair_sums = ring_end(pair_sums, pair_2, pair_3)
    gains = gains + exchanged(gains, "dp", 4)

    second = ring_stack(second, second_3, second_4)
    second, first_other, gains, pair_sums = hold(second, first_other, gains, pair_sums)
    second_other = moved(second, core=1)
    shapes = (wq.shape, wk.shape, wv.shape, wo.shape)
    laid = dense_layout(dp_place, z_at, 0, first, first_other, shapes, ())
    gains = gains + exchanged(gains, "dp", 8)
    w_gate_grad, w_up_grad, w_down_grad = (jnp.concatenate([ring_sums[:, i], pair_sums[:, i]], 0) for i in range(3))
    w_down_grad = w_down_grad.reshape(local_experts, width // units, -1, units)
    w_down_grad = jnp.swapaxes(w_down_grad, 1, 2).reshape(local_experts, -1, width)

    second_other, laid = hold(second_other, laid)
    laid = dense_layout(dp_place, z_at, 1, second, second_other, shapes, laid)
    w_query_grad, w_key_grad, w_value_grad, w_out_grad = (
        grad.reshape(weight.shape) for grad, weight in zip(laid, (wq, wk, wv, wo))
    )

    outputs, dqkv = hold(outputs, dqkv)
    outputs = lax.psum_scatter(outputs, "expert", scatter_dimension=0, tiled=True)[0]
    layer_outputs = (h1 + outputs.astype(F32)).astype(LOW)
    return (
        layer_outputs[None],
        input_grad[None],
        gains[0:1],
        w_query_grad[None],
        w_key_grad[None],
        w_value_grad[None],
        w_out_grad[None],
        gains[1:2],
        w_gate_grad[None],
        w_up_grad[None],
        w_down_grad[None],
    )


def solution(mesh):
    tokens = P(None, ("dp", "expert"), None)
    layered = P("section", None, ("dp", "expert"), None)
    vector = P("section", None)
    matrix = P("section", None, None)
    expert = P("section", "expert", "dp", None)
    return jax.shard_map(
        local,
        mesh=mesh,
        in_specs=(
            tokens, P(None, ("dp", "expert")), layered, layered, vector, matrix, matrix, matrix, matrix,
            vector, expert, expert, expert, tokens,
        ),
        out_specs=(layered, layered, vector, matrix, matrix, matrix, matrix, vector, expert, expert, expert),
        check_vma=False,
    )
```

time: 869 us -> 647 us (0.74)
  waiting for transfers between devices: 415 us -> 218 us
  Pallas kernels: 216 us -> 159 us
  local copies, waits for them, and re-layouts: 22.1 us -> 62.5 us
  starting transfers between devices: 138 us -> 115 us
  other arithmetic: 46.8 us -> 60.1 us
    ppermute x48 -> x34, waiting for transfers between devices: 225 us -> 94.7 us  [shifted(): lax.ppermute(block, 'expert', [(i, (i + by) % size) for i in range(size)])]
    all_gather x3 -> x1, waiting for transfers between devices: 64.5 us -> 0.01 us  [local(): c_second = lax.all_gather(out_grad, 'expert')]
    unnamed x108 -> x284, local copies, waits for them, and re-layouts: 5.14 us -> 36.9 us
    pallas_call x2, Pallas kernels: 46.7 us -> 19.2 us  [attend(): pl.pallas_call(attend_kernel, grid=(batches, parts), in_specs=[pl.BlockSp...]
    pallas_call x6 -> x8, Pallas kernels: 60.7 us -> 82.4 us  [the longest x1 23.2 us: experts_turn(): pl.pallas_call(experts_turn_kernel, grid=(count,), in_specs=[pl.BlockSpec...]
    pallas_call x2 -> x1, Pallas kernels: 34.7 us -> 14.2 us  [experts_backward(): pl.pallas_call(experts_backward_kernel, grid=(count,), in_specs=[pl.Block...]
    ppermute x60 -> x47, starting transfers between devices: 70.4 us -> 54.7 us  [moved(): return lax.ppermute(block, 'dp', route)]
    ppermute x60 -> x47, waiting for transfers between devices: 105 us -> 89.6 us  [moved(): return lax.ppermute(block, 'dp', route)]
  transfers between devices with their start and end apart: 119 -> 92, of which waited for: 61 -> 48; matrix products, arithmetic and copies ran while one was open for 5% -> 11% of each run, Pallas kernels for 9% -> 12%
where the time goes in v2:
time: 647 us; the launch traced here: 640 us
  waiting for transfers between devices  218 us (34%)
  Pallas kernels  159 us (25%)
  starting transfers between devices  115 us (18%)
  local copies, waits for them, and re-layouts  62.5 us (10%)
  other arithmetic  60.1 us (9%)
  between operations  16.3 us (3%)
  matrix products  9.09 us (1%)
    ppermute x34, waiting for transfers between devices, shifted(): lax.ppermute(block, 'expert', [(i, (i + by) % size) for i in range(size)])  94.7 us
    ppermute x47, waiting for transfers between devices, moved(): return lax.ppermute(block, 'dp', route)  89.6 us
    ppermute x47, starting transfers between devices, moved(): return lax.ppermute(block, 'dp', route)  54.7 us
    ppermute x34, starting transfers between devices, shifted(): lax.ppermute(block, 'expert', [(i, (i + by) % size) for i in range(size)])  40.9 us
    unnamed x284, local copies, waits for them, and re-layouts  36.9 us
    pallas_call x1, Pallas kernels, experts_turn(): pl.pallas_call(experts_turn_kernel, grid=(count,), in_specs=[pl.BlockSpec...  23.2 us
    pallas_call x1, Pallas kernels, experts_forward(): pl.pallas_call(experts_forward_kernel, grid_spec=pltpu.PrefetchScalarGrid...  20.1 us
    pallas_call x2, Pallas kernels, attend(): pl.pallas_call(attend_kernel, grid=(batches, parts), in_specs=[pl.BlockSp...  19.2 us
  transfers between devices with their start and end apart: 92, of which 48 were waited for; matrix products, arithmetic and copies ran while one was open for 11% of the time, Pallas kernels for 12%

profile of v2, /device:TPU:1, one launch (start us, length us, event | category | flops | bytes accessed | tf_op | source)
XLA Modules:
  0.0 639.8 jit_solution(9496173958248054623)
XLA Ops:
  43.2 9.2 %project.2 = (bf16[512,2560]{1,0:T(8,128)(2,1)S(1)}, bf16[512,1536]{1,0:T(8,128)(2,1)}) custom-call(bf16[512,1536]{1,0:T(8,128)(2,1)S(1)} %bitcast.307, f32[1,1536]{1,0:T(1,128)S(1)} %copy-done.52, bf16[1536,1536]{1,0:T(8,128)(2,1)S(1)} %bitcast.288, bf16[1536,512]{1,0:T(8,128)(2,1)S(1)} %bitcast.308, bf16[1536,512]{1,0:T(8,128)(2,1)S(1)} %bitcast.311, ...), custom_call_target="tpu_custom_call" | custom-call | flops 1 | bytes 1 | tf_op jit(solution)/shard_map/project/pallas_call | solution.py:174
  52.6 9.6 %attend.2.o_ref = bf16[2,256,1536]{2,1,0:T(8,128)(2,1)S(1)} custom-call(bf16[2,256,2560]{2,1,0:T(8,128)(2,1)S(1)} %bitcast.316, bf16[2,256,2560]{2,1,0:T(8,128)(2,1)S(1)} %bitcast.317, bf16[2,256,2560]{2,1,0:T(8,128)(2,1)S(1)} %bitcast.318, f32[2,256,256]{2,1,0:T(8,128)S(1)} %and_select_fusion.bias_ref), custom_call_target="tpu_custom_call" | custom-call | flops 1 | bytes 1 | tf_op jit(solution)/shard_map/attend/pallas_call | solution.py:226
  83.8 5.8 collective-permute-done.18.refs_8_
  90.0 7.1 %collective-permute-done.15 = bf16[2,3,96,512]{3,2,1,0:T(8,128)(2,1)S(1)} collective-permute-done((bf16[2,3,96,512]{3,2,1,0:T(8,128)(2,1)S(1)}, bf16[2,3,96,512]{3,2,1,0:T(8,128)(2,1)S(1)}, u32[]{:S(2)}, u32[]{:S(2)}) %collective-permute-start.15) | collective-permute-done | bytes 589856 | tf_op jit(solution)/shard_map/ppermute | solution.py:69
  99.1 12.1 %collective-permute-done.16.refs_5_ = bf16[1,2,3,96,512]{4,3,2,1,0:T(8,128)(2,1)} collective-permute-done((bf16[1,2,3,96,512]{4,3,2,1,0:T(8,128)(2,1)S(1)}, bf16[1,2,3,96,512]{4,3,2,1,0:T(8,128)(2,1)}, u32[]{:S(2)}, u32[]{:S(2)}) %collective-permute-start.16) | collective-permute-done | bytes 589856 | tf_op jit(solution)/shard_map/ppermute | solution.py:69
  125.2 20.1 %experts_forward.1 = (bf16[2,64,1536]{2,1,0:T(8,128)(2,1)S(1)}, bf16[2,64,1536]{2,1,0:T(8,128)(2,1)S(1)}, bf16[2,64,1536]{2,1,0:T(8,128)(2,1)S(1)}, bf16[2,64,15...) custom-call(s32[3]{0:T(128)S(1)} %pad_add_fusion.place_ref, ...), custom_call_target="tpu_custom_call" | custom-call | flops 1 | bytes 1 | tf_op jit(solution)/shard_map/experts_forward/pallas_call | solution.py:348
  148.2 7.8 %collective-permute-done.23 = bf16[2,64,1536]{2,1,0:T(8,128)(2,1)S(1)} collective-permute-done((bf16[2,64,1536]{2,1,0:T(8,128)(2,1)S(1)}, bf16[2,64,1536]{2,1,0:T(8,128)(2,1)S(1)}, u32[]{:S(2)}, u32[]{:S(2)}) %collective-permute-start.23) | collective-permute-done | bytes 393248 | tf_op jit(solution)/shard_map/ppermute | solution.py:39
  159.1 9.0 %collective-permute-done.25 = bf16[2,64,1536]{2,1,0:T(8,128)(2,1)S(1)} collective-permute-done((bf16[2,64,1536]{2,1,0:T(8,128)(2,1)S(1)}, bf16[2,64,1536]{2,1,0:T(8,128)(2,1)S(1)}, u32[]{:S(2)}, u32[]{:S(2)}) %collective-permute-start.25) | collective-permute-done | bytes 393248 | tf_op jit(solution)/shard_map/ppermute | solution.py:39
  176.2 5.9 collective-permute-done.26
  186.8 7.0 %collective-permute-done.27 = bf16[2,64,1536]{2,1,0:T(8,128)(2,1)S(1)} collective-permute-done((bf16[2,64,1536]{2,1,0:T(8,128)(2,1)S(1)}, bf16[2,64,1536]{2,1,0:T(8,128)(2,1)S(1)}, u32[]{:S(2)}, u32[]{:S(2)}) %collective-permute-start.27) | collective-permute-done | bytes 393248 | tf_op jit(solution)/shard_map/ppermute | solution.py:39
  202.9 8.1 %project.3 = (bf16[512,2560]{1,0:T(8,128)(2,1)S(1)}, bf16[512,1536]{1,0:T(8,128)(2,1)S(1)}) custom-call(bf16[512,1536]{1,0:T(8,128)(2,1)S(1)} %bitcast_select_fusion.1.x_ref, f32[1,1536]{1,0:T(1,128)S(1)} %copy-done.52, bf16[1536,1536]{1,0:T(8,128)(2,1)S(1)} %bitcast.291, bf16[1536,512]{1,0:T(8,128)(2,1)S(1)} %bitcast.309, bf16[1536,512]{1,0:T(8,128)(2,1)S(1)} %bitcast.312, ...), custom_call_target="tpu_custom_call" | custom-call | flops 1 | bytes 1 | tf_op jit(solution)/shard_map/project/pallas_call | solution.py:174
  211.0 9.6 %attend.3.o_ref = bf16[2,256,1536]{2,1,0:T(8,128)(2,1)S(1)} custom-call(bf16[2,256,2560]{2,1,0:T(8,128)(2,1)S(1)} %bitcast.277, bf16[2,256,2560]{2,1,0:T(8,128)(2,1)S(1)} %bitcast.278, bf16[2,256,2560]{2,1,0:T(8,128)(2,1)S(1)} %bitcast.279, f32[2,256,256]{2,1,0:T(8,128)S(1)} %and_select_fusion.bias_ref), custom_call_target="tpu_custom_call" | custom-call | flops 1 | bytes 1 | tf_op jit(solution)/shard_map/attend/pallas_call | solution.py:226
  225.1 23.2 %experts_turn.1 = (bf16[512,2048]{1,0:T(8,128)(2,1)S(1)}, bf16[512,2048]{1,0:T(8,128)(2,1)S(1)}, bf16[512,2048]{1,0:T(8,128)(2,1)S(1)}, bf16[2,64,1536]{2,1,0:T(...) custom-call(bf16[512,1536]{1,0:T(8,128)(2,1)S(1)} %bitcast.322, ...), custom_call_target="tpu_custom_call" | custom-call | flops 1 | bytes 1 | tf_op jit(solution)/shard_map/experts_turn/pallas_call | solution.py:390
  253.8 6.2 convolution_convert_fusion
  267.1 6.7 %collective-permute-done.32 = bf16[2,64,1536]{2,1,0:T(8,128)(2,1)} collective-permute-done((bf16[2,64,1536]{2,1,0:T(8,128)(2,1)}, bf16[2,64,1536]{2,1,0:T(8,128)(2,1)}, u32[]{:S(2)}, u32[]{:S(2)}) %collective-permute-start.32) | collective-permute-done | bytes 393248 | tf_op jit(solution)/shard_map/ppermute | solution.py:39
  279.9 13.1 %own_backward.1 = (bf16[2,64,1536]{2,1,0:T(8,128)(2,1)S(1)}, bf16[2,64,1024]{2,1,0:T(8,128)(2,1)S(1)}, bf16[2,64,1024]{2,1,0:T(8,128)(2,1)S(1)}, bf16[2,64,1024]...) custom-call(bf16[2,256,2560]{2,1,0:T(8,128)(2,1)S(1)} %bitcast.280, bf16[2,256,2560]{2,1,0:T(8,128)(2,1)S(1)} %bitcast.281, ...), custom_call_target="tpu_custom_call" | custom-call | flops 1 | bytes 1 | tf_op jit(solution)/shard_map/own_backward/pallas_call | solution.py:554
  301.4 7.0 %collective-permute-done.35 = bf16[2,64,1024]{2,1,0:T(8,128)(2,1)S(1)} collective-permute-done((bf16[2,64,1024]{2,1,0:T(8,128)(2,1)S(1)}, bf16[2,64,1024]{2,1,0:T(8,128)(2,1)S(1)}, u32[]{:S(2)}, u32[]{:S(2)}) %collective-permute-start.35) | collective-permute-done | bytes 262176 | tf_op jit(solution)/shard_map/ppermute | solution.py:39
  313.3 12.4 %collective-permute-done.36 = bf16[2,64,1536]{2,1,0:T(8,128)(2,1)} collective-permute-done((bf16[2,64,1536]{2,1,0:T(8,128)(2,1)S(1)}, bf16[2,64,1536]{2,1,0:T(8,128)(2,1)}, u32[]{:S(2)}, u32[]{:S(2)}) %collective-permute-start.36) | collective-permute-done | bytes 393248 | tf_op jit(solution)/shard_map/ppermute | solution.py:56
  329.7 8.4 %collective-permute-done.37 = bf16[2,64,1536]{2,1,0:T(8,128)(2,1)} collective-permute-done((bf16[2,64,1536]{2,1,0:T(8,128)(2,1)}, bf16[2,64,1536]{2,1,0:T(8,128)(2,1)}, u32[]{:S(2)}, u32[]{:S(2)}) %collective-permute-start.37) | collective-permute-done | bytes 393248 | tf_op jit(solution)/shard_map/ppermute | solution.py:39
  351.3 14.2 %experts_backward.1 = (bf16[2,64,1536]{2,1,0:T(8,128)(2,1)S(1)}, bf16[2,64,1536]{2,1,0:T(8,128)(2,1)S(1)}, bf16[2,64,1536]{2,1,0:T(8,128)(2,1)S(1)}, bf16[2,64,1...) custom-call(bf16[512,1536]{1,0:T(8,128)(2,1)S(1)} %bitcast_select_fusion.c_ref, bf16[512,2048]{1,0:T(8,128)(2,1)S(1)} %copy-done.32, ...), custom_call_target="tpu_custom_call" | custom-call | flops 1 | bytes 1 | tf_op jit(solution)/shard_map/experts_backward/pallas_call | solution.py:426
  376.6 12.1 %expert_grad.2 = (bf16[2,2,16,96,512]{4,3,2,1,0:T(8,128)(2,1)S(1)}, bf16[2,2,16,96,512]{4,3,2,1,0:T(8,128)(2,1)}) custom-call(s32[3]{0:T(128)S(1)} %copy-done.55, bf16[512,1536]{1,0:T(8,128)(2,1)S(1)} %bitcast.323, bf16[2,512,2048]{2,1,0:T(8,128)(2,1)S(1)} %get-tuple-element.200.right_ref), custom_call_target="tpu_custom_call" | custom-call | tf_op jit(solution)/shard_map/expert_grad/pallas_call | solution.py:626
  398.8 6.7 %collective-permute-done.45 = bf16[2,64,1536]{2,1,0:T(8,128)(2,1)S(1)} collective-permute-done((bf16[2,64,1536]{2,1,0:T(8,128)(2,1)S(1)}, bf16[2,64,1536]{2,1,0:T(8,128)(2,1)S(1)}, u32[]{:S(2)}, u32[]{:S(2)}) %collective-permute-start.45) | collective-permute-done | bytes 393248 | tf_op jit(solution)/shard_map/ppermute | solution.py:39
  408.4 9.5 %collective-permute-done.43 = bf16[2,64,1536]{2,1,0:T(8,128)(2,1)S(1)} collective-permute-done((bf16[2,64,1536]{2,1,0:T(8,128)(2,1)S(1)}, bf16[2,64,1536]{2,1,0:T(8,128)(2,1)S(1)}, u32[]{:S(2)}, u32[]{:S(2)}) %collective-permute-start.43) | collective-permute-done | bytes 393248 | tf_op jit(solution)/shard_map/ppermute | solution.py:39
  436.5 8.3 %attend_backward.1 = (bf16[2,256,640]{2,1,0:T(8,128)(2,1)S(1)}, bf16[4,2,64,1536]{3,2,1,0:T(8,128)(2,1)S(1)}) custom-call(s32[1]{0:T(128)} %bitcast.53.z_ref, bf16[2,256,2560]{2,1,0:T(8,128)(2,1)S(1)} %bitcast.283, bf16[2,256,2560]{2,1,0:T(8,128)(2,1)S(1)} %bitcast.284, bf16[2,256,2560]{2,1,0:T(8,128)(2,1)S(1)} %bitcast.285, ...), custom_call_target="tpu_custom_call" | custom-call | flops 1 | bytes 1 | tf_op jit(solution)/shard_map/attend_backward/pallas_call | solution.py:497
  477.4 16.3 %collective-permute-done.53 = bf16[1,2,2,48,1024]{4,3,2,1,0:T(8,128)(2,1)} collective-permute-done((bf16[1,2,2,48,1024]{4,3,2,1,0:T(8,128)(2,1)}, bf16[1,2,2,48,1024]{4,3,2,1,0:T(8,128)(2,1)}, u32[]{:S(2)}, u32[]{:S(2)}) %collective-permute-start.53) | collective-permute-done | bytes 393248 | tf_op jit(solution)/shard_map/ppermute | solution.py:69
  525.9 7.6 %collective-permute-start.70 = (f32[2,1536]{1,0:T(2,128)S(1)}, f32[2,1536]{1,0:T(2,128)S(1)}, u32[]{:S(2)}, u32[]{:S(2)}) collective-permute-start(f32[2,1536]{1,0:T(2,128)S(1)} %add.411), channel_id=1, source_target_pairs={{0,4},{4,0},{8,12},{12,8},{16,20},{20,16},{24,28},{28,24},{32,36},... | collective-permute-start | bytes 36872 | tf_op jit(solution)/shard_map/ppermute | solution.py:121
  545.3 8.2 %collective-permute-done.77 = bf16[2,3,96,512]{3,2,0,1:T(8,128)(2,1)S(1)} collective-permute-done((bf16[2,3,96,512]{3,2,0,1:T(8,128)(2,1)S(1)}, bf16[2,3,96,512]{3,2,0,1:T(8,128)(2,1)S(1)}, u32[]{:S(2)}, u32[]{:S(2)}) %collective-permute-start.77) | collective-permute-done | bytes 589856 | tf_op jit(solution)/shard_map/ppermute | solution.py:69
  564.1 6.4 collective-permute-done.83
  573.3 10.4 %collective-permute-start.85 = (bf16[4,2,2,4,48,512]{5,4,3,2,1,0:T(8,128)(2,1)}, bf16[4,2,2,4,48,512]{5,4,3,2,1,0:T(8,128)(2,1)}, u32[]{:S(2)}, u32[]{:S(2)}) collective-permute-start(bf16[4,2,2,4,48,512]{5,4,3,2,1,0:T(8,128)(2,1)} %pad_maximum_fusion.4.mine_ref), channel_id=1, source_target_pairs={{0,4},{4,0},{8,12},{12,8},{16,20},{20,16},{24,28},{28,24},{32,36},... | collective-permute-start | bytes 9437192 | tf_op jit(solution)/shard_map/ppermute | solution.py:69
  594.9 9.5 %reduce-scatter.3.cloned.1.call-done = bf16[1,2,64,1536]{3,2,1,0:T(8,128)(2,1)} async-done(((bf16[4,2,64,1536]{3,2,1,0:T(8,128)(2,1)}), bf16[1,2,64,1536]{3,2,1,0:T(8,128)(2,1)}) %reduce-scatter.3.cloned.1.call-update) | async-done | bytes 393232 | tf_op jit(solution)/shard_map/reduce_scatter | solution.py:960
  615.5 8.4 %dense_layout.2 = (f32[4,2,2,2,48,1536]{5,4,3,2,1,0:T(8,128)}, f32[4,2,2,2,48,512]{5,4,3,2,1,0:T(8,128)}, f32[4,2,2,2,48,512]{5,4,3,2,1,0:T(8,128)}, f32[4,4,2,48,1536]{4,3,2,1,0:T(8,128)}) custom-call(s32[3]{0:T(128)S(1)} %copy-done.55, s32[1]{0:T(128)} %bitcast.53.z_ref, bf16[4,2,2,4,48,512]{5,4,3,2,1,0:T(8,128)(2,1)} %pad_maximum_fusion.4.mine_ref, ...), custom_call_target="tpu_custom_call" | custom-call | bytes 37748736 | tf_op jit(solution)/shard_map/dense_layout/pallas_call | solution.py:732
  624.6 8.5 %dense_layout.3 = (f32[4,2,2,2,48,1536]{5,4,3,2,1,0:T(8,128)}, f32[4,2,2,2,48,512]{5,4,3,2,1,0:T(8,128)}, f32[4,2,2,2,48,512]{5,4,3,2,1,0:T(8,128)}, f32[4,4,2,48,1536]{4,3,2,1,0:T(8,128)}) custom-call(s32[3]{0:T(128)S(1)} %copy-done.55, s32[1]{0:T(128)} %bitcast.53.z_ref, ...), custom_call_target="tpu_custom_call", output_to_operand_aliasing={{0}: (4, {}), {1}: (5, {}), {2}: (6, {}), {3}: (7, {})} | custom-call | bytes 37748736 | tf_op jit(solution)/shard_map/dense_layout/pallas_call | solution.py:732
  (596 shorter events, 309.4 us)
Async XLA Ops:
  7.2 174.9 %all-gather.3.cloned.1.call-start = ((), (), s32[]{:S(2)}) async-start(), calls=%async_computation.4 | async-start | bytes 1966080 | tf_op jit(solution)/shard_map/all_gather | solution.py:831
  37.9 34.1 %collective-permute-start.10 = (bf16[2,2,3,96,512]{4,3,2,0,1:T(8,128)(2,1)S(1)}, bf16[2,2,3,96,512]{4,3,2,0,1:T(8,128)(2,1)S(1)}, u32[]{:S(2)}, u32[]{:S(2)}) collective-permute-start(bf16[2,2,3,96,512]{4,3,2,0,1:T(8,128)(2,1)S(1)} %get-tuple-element.322), channel_id=1, source_target_pairs={{0,48},{4,52},{8,56},{12,60},{16,0},{20,4},{24,8},{28,12},{32,16},... | collective-permute-start | bytes 3538952 | tf_op jit(solution)/shard_map/ppermute | solution.py:69
  39.6 37.0 %collective-permute-start.13 = (bf16[3,2,3,96,512]{4,3,2,1,0:T(8,128)(2,1)S(1)}, bf16[3,2,3,96,512]{4,3,2,1,0:T(8,128)(2,1)S(1)}, u32[]{:S(2)}, u32[]{:S(2)}) collective-permute-start(bf16[3,2,3,96,512]{4,3,2,1,0:T(8,128)(2,1)S(1)} %pad_maximum_fusion.6.refs_2_), channel_id=1, source_target_pairs={{0,8},{4,12},{8,0},{12,4},{16,24},{20,28},{24,16},{28,20},{32,40},... | collective-permute-start | bytes 5308424 | tf_op jit(solution)/shard_map/ppermute | solution.py:69
  40.9 28.1 %collective-permute-start.12 = (bf16[3,96,512]{2,1,0:T(8,128)(2,1)S(1)}, bf16[3,96,512]{2,1,0:T(8,128)(2,1)S(1)}, u32[]{:S(2)}, u32[]{:S(2)}) collective-permute-start(bf16[3,96,512]{2,1,0:T(8,128)(2,1)S(1)} %slice_bitcast_fusion.13), channel_id=1, source_target_pairs={{0,48},{4,52},{8,56},{12,60},{16,0},{20,4},{24,8},{28,12},{32,16},... | collective-permute-start | bytes 884744 | tf_op jit(solution)/shard_map/ppermute | solution.py:69
  41.1 28.0 %collective-permute-start.11 = (bf16[3,96,512]{2,1,0:T(8,128)(2,1)S(1)}, bf16[3,96,512]{2,1,0:T(8,128)(2,1)S(1)}, u32[]{:S(2)}, u32[]{:S(2)}) collective-permute-start(bf16[3,96,512]{2,1,0:T(8,128)(2,1)S(1)} %slice_bitcast_fusion.14), channel_id=1, source_target_pairs={{0,16},{4,20},{8,24},{12,28},{16,32},{20,36},{24,40},{28,44},{32,4... | collective-permute-start | bytes 884744 | tf_op jit(solution)/shard_map/ppermute | solution.py:69
  42.6 29.4 %collective-permute-start.9 = (bf16[2,2,3,96,512]{4,3,2,1,0:T(8,128)(2,1)S(1)}, bf16[2,2,3,96,512]{4,3,2,1,0:T(8,128)(2,1)S(1)}, u32[]{:S(2)}, u32[]{:S(2)}) collective-permute-start(bf16[2,2,3,96,512]{4,3,2,1,0:T(8,128)(2,1)S(1)} %copy.143), channel_id=1, source_target_pairs={{0,16},{4,20},{8,24},{12,28},{16,32},{20,36},{24,40},{28,44},{32,4... | collective-permute-start | bytes 3538952 | tf_op jit(solution)/shard_map/ppermute | solution.py:69
  77.0 34.2 %collective-permute-start.17 = (bf16[3,2,2,3,96,512]{5,4,3,1,2,0:T(8,128)(2,1)S(1)}, bf16[3,2,2,3,96,512]{5,4,3,1,2,0:T(8,128)(2,1)S(1)}, u32[]{:S(2)}, u32[]{:S(2)}) collective-permute-start(bf16[3,2,2,3,96,512]{5,4,3,1,2,0:T(8,128)(2,1)S(1)} %pad_maximum_fusion.2), channel_id=1, source_target_pairs={{0,4},{4,0},{8,12},{12,8},{16,20},{20,16},{24,28},{28,24},{32,36},... | collective-permute-start | bytes 10616840 | tf_op jit(solution)/shard_map/ppermute | solution.py:69
  81.3 29.9 %collective-permute-start.20 = (bf16[3,2,3,96,512]{4,3,2,1,0:T(8,128)(2,1)S(1)}, bf16[3,2,3,96,512]{4,3,2,1,0:T(8,128)(2,1)S(1)}, u32[]{:S(2)}, u32[]{:S(2)}) collective-permute-start(bf16[3,2,3,96,512]{4,3,2,1,0:T(8,128)(2,1)S(1)} %collective-permute-done.13.refs_4_), channel_id=1, source_target_pairs={{0,4},{4,0},{8,12},{12,8},{16,20},{20,16},{24,28},{28,24},{32,36},... | collective-permute-start | bytes 5308424 | tf_op jit(solution)/shard_map/ppermute | solution.py:69
  116.4 359.8 %reduce-scatter.5.cloned.1.call-start = ((), (), s32[]{:S(2)}) async-start(), calls=%async_computation.3 | async-start | bytes 1966080 | tf_op jit(solution)/shard_map/reduce_scatter | solution.py:887
  147.6 20.4 %collective-permute-start.25 = (bf16[2,64,1536]{2,1,0:T(8,128)(2,1)S(1)}, bf16[2,64,1536]{2,1,0:T(8,128)(2,1)S(1)}, u32[]{:S(2)}, u32[]{:S(2)}) collective-permute-start(bf16[2,64,1536]{2,1,0:T(8,128)(2,1)S(1)} %get-tuple-element.175), channel_id=1, source_target_pairs={{0,1},{1,2},{2,3},{3,0},{4,5},{5,6},{6,7},{7,4},{8,9},{9,10},{10,1... | collective-permute-start | bytes 1179656 | tf_op jit(solution)/shard_map/ppermute | solution.py:39
  248.3 18.8 %collective-permute-start.30 = (bf16[2,64,1536]{2,1,0:T(8,128)(2,1)}, bf16[2,64,1536]{2,1,0:T(8,128)(2,1)}, u32[]{:S(2)}, u32[]{:S(2)}) collective-permute-start(bf16[2,64,1536]{2,1,0:T(8,128)(2,1)} %get-tuple-element.183), channel_id=1, source_target_pairs={{0,3},{1,0},{2,1},{3,2},{4,7},{5,4},{6,5},{7,6},{8,11},{9,8},{10,9... | collective-permute-start | bytes 1179656 | tf_op jit(solution)/shard_map/ppermute | solution.py:39
  253.7 20.2 %collective-permute-start.32 = (bf16[2,64,1536]{2,1,0:T(8,128)(2,1)}, bf16[2,64,1536]{2,1,0:T(8,128)(2,1)}, u32[]{:S(2)}, u32[]{:S(2)}) collective-permute-start(bf16[2,64,1536]{2,1,0:T(8,128)(2,1)} %get-tuple-element.185), channel_id=1, source_target_pairs={{0,1},{1,2},{2,3},{3,0},{4,5},{5,6},{6,7},{7,4},{8,9},{9,10},{10,1... | collective-permute-start | bytes 1179656 | tf_op jit(solution)/shard_map/ppermute | solution.py:39
  325.8 17.7 %collective-permute-start.39 = (bf16[2,64,1536]{2,1,0:T(8,128)(2,1)}, bf16[2,64,1536]{2,1,0:T(8,128)(2,1)S(1)}, u32[]{:S(2)}, u32[]{:S(2)}) collective-permute-start(bf16[2,64,1536]{2,1,0:T(8,128)(2,1)} %collective-permute-done.36), channel_id=1, source_target_pairs={{0,3},{1,0},{2,1},{3,2},{4,7},{5,4},{6,5},{7,6},{8,11},{9,8},{10,9... | collective-permute-start | bytes 1179656 | tf_op jit(solution)/shard_map/ppermute | solution.py:39
  365.5 23.2 %collective-permute-start.40 = (bf16[2,64,1536]{2,1,0:T(8,128)(2,1)S(1)}, bf16[2,64,1536]{2,1,0:T(8,128)(2,1)S(1)}, u32[]{:S(2)}, u32[]{:S(2)}) collective-permute-start(bf16[2,64,1536]{2,1,0:T(8,128)(2,1)S(1)} %get-tuple-element.197), channel_id=1, source_target_pairs={{0,3},{1,0},{2,1},{3,2},{4,7},{5,4},{6,5},{7,6},{8,11},{9,8},{10,9... | collective-permute-start | bytes 1179656 | tf_op jit(solution)/shard_map/ppermute | solution.py:39
  368.3 20.4 %collective-permute-start.41 = (bf16[2,64,1536]{2,1,0:T(8,128)(2,1)S(1)}, bf16[2,64,1536]{2,1,0:T(8,128)(2,1)S(1)}, u32[]{:S(2)}, u32[]{:S(2)}) collective-permute-start(bf16[2,64,1536]{2,1,0:T(8,128)(2,1)S(1)} %get-tuple-element.198), channel_id=1, source_target_pairs={{0,2},{1,3},{2,0},{3,1},{4,6},{5,7},{6,4},{7,5},{8,10},{9,11},{10,... | collective-permute-start | bytes 1179656 | tf_op jit(solution)/shard_map/ppermute | solution.py:39
  369.4 19.8 %collective-permute-start.42 = (bf16[2,64,1536]{2,1,0:T(8,128)(2,1)S(1)}, bf16[2,64,1536]{2,1,0:T(8,128)(2,1)S(1)}, u32[]{:S(2)}, u32[]{:S(2)}) collective-permute-start(bf16[2,64,1536]{2,1,0:T(8,128)(2,1)S(1)} %get-tuple-element.199), channel_id=1, source_target_pairs={{0,1},{1,2},{2,3},{3,0},{4,5},{5,6},{6,7},{7,4},{8,9},{9,10},{10,1... | collective-permute-start | bytes 1179656 | tf_op jit(solution)/shard_map/ppermute | solution.py:39
  391.7 27.6 %collective-permute-start.46 = (bf16[2,2,16,96,512]{4,3,2,1,0:T(8,128)(2,1)}, bf16[2,2,16,96,512]{4,3,2,1,0:T(8,128)(2,1)}, u32[]{:S(2)}, u32[]{:S(2)}) collective-permute-start(bf16[2,2,16,96,512]{4,3,2,1,0:T(8,128)(2,1)} %get-tuple-element.207), channel_id=1, source_target_pairs={{0,4},{4,0},{8,12},{12,8},{16,20},{20,16},{24,28},{28,24},{32,36},... | collective-permute-start | bytes 18874376 | tf_op jit(solution)/shard_map/ppermute | solution.py:69
  394.1 23.9 %collective-permute-start.47 = (bf16[1,2,16,96,512]{4,3,2,1,0:T(8,128)(2,1)S(1)}, bf16[1,2,16,96,512]{4,3,2,1,0:T(8,128)(2,1)S(1)}, u32[]{:S(2)}, u32[]{:S(2)}) collective-permute-start(bf16[1,2,16,96,512]{4,3,2,1,0:T(8,128)(2,1)S(1)} %get-tuple-element.209), channel_id=1, source_target_pairs={{0,4},{4,0},{8,12},{12,8},{16,20},{20,16},{24,28},{28,24},{32,36},... | collective-permute-start | bytes 9437192 | tf_op jit(solution)/shard_map/ppermute | solution.py:69
  398.1 19.8 %collective-permute-start.43 = (bf16[2,64,1536]{2,1,0:T(8,128)(2,1)S(1)}, bf16[2,64,1536]{2,1,0:T(8,128)(2,1)S(1)}, u32[]{:S(2)}, u32[]{:S(2)}) collective-permute-start(bf16[2,64,1536]{2,1,0:T(8,128)(2,1)S(1)} %convert_element_type.511), channel_id=1, source_target_pairs={{0,1},{1,2},{2,3},{3,0},{4,5},{5,6},{6,7},{7,4},{8,9},{9,10},{10,1... | collective-permute-start | bytes 1179656 | tf_op jit(solution)/shard_map/ppermute | solution.py:39
  430.2 27.4 %collective-permute-start.50 = (bf16[3,4,96,512]{3,2,0,1:T(8,128)(2,1)}, bf16[3,4,96,512]{3,2,0,1:T(8,128)(2,1)}, u32[]{:S(2)}, u32[]{:S(2)}) collective-permute-start(bf16[3,4,96,512]{3,2,0,1:T(8,128)(2,1)} %get-tuple-element.292), channel_id=1, source_target_pairs={{0,8},{4,12},{8,0},{12,4},{16,24},{20,28},{24,16},{28,20},{32,40},... | collective-permute-start | bytes 3538952 | tf_op jit(solution)/shard_map/ppermute | solution.py:69
  434.5 27.0 %collective-permute-start.49 = (bf16[3,2,2,96,512]{4,3,0,2,1:T(8,128)(2,1)}, bf16[3,2,2,96,512]{4,3,0,2,1:T(8,128)(2,1)}, u32[]{:S(2)}, u32[]{:S(2)}) collective-permute-start(bf16[3,2,2,96,512]{4,3,0,2,1:T(8,128)(2,1)} %get-tuple-element.297), channel_id=1, source_target_pairs={{0,48},{4,52},{8,56},{12,60},{16,0},{20,4},{24,8},{28,12},{32,16},... | collective-permute-start | bytes 3538952 | tf_op jit(solution)/shard_map/ppermute | solution.py:69
  436.4 27.9 %collective-permute-start.48 = (bf16[3,2,2,96,512]{4,3,0,2,1:T(8,128)(2,1)}, bf16[3,2,2,96,512]{4,3,0,2,1:T(8,128)(2,1)}, u32[]{:S(2)}, u32[]{:S(2)}) collective-permute-start(bf16[3,2,2,96,512]{4,3,0,2,1:T(8,128)(2,1)} %get-tuple-element.298), channel_id=1, source_target_pairs={{0,16},{4,20},{8,24},{12,28},{16,32},{20,36},{24,40},{28,44},{32,4... | collective-permute-start | bytes 3538952 | tf_op jit(solution)/shard_map/ppermute | solution.py:69
  446.9 157.5 %reduce-scatter.3.cloned.1.call-start = ((), (), s32[]{:S(2)}) async-start(), calls=%async_computation.2 | async-start | bytes 1966080 | tf_op jit(solution)/shard_map/reduce_scatter | solution.py:960
  466.4 43.9 %collective-permute-start.61 = (bf16[3,4,96,512]{3,2,0,1:T(8,128)(2,1)}, bf16[3,4,96,512]{3,2,0,1:T(8,128)(2,1)}, u32[]{:S(2)}, u32[]{:S(2)}) collective-permute-start(bf16[3,4,96,512]{3,2,0,1:T(8,128)(2,1)} %get-tuple-element.291), channel_id=1, source_target_pairs={{0,8},{4,12},{8,0},{12,4},{16,24},{20,28},{24,16},{28,20},{32,40},... | collective-permute-start | bytes 3538952 | tf_op jit(solution)/shard_map/ppermute | solution.py:69
  470.3 28.2 %collective-permute-start.58 = (bf16[3,2,96,512]{3,2,0,1:T(8,128)(2,1)}, bf16[3,2,96,512]{3,2,0,1:T(8,128)(2,1)}, u32[]{:S(2)}, u32[]{:S(2)}) collective-permute-start(bf16[3,2,96,512]{3,2,0,1:T(8,128)(2,1)} %get-tuple-element.295), channel_id=1, source_target_pairs={{0,48},{4,52},{8,56},{12,60},{16,0},{20,4},{24,8},{28,12},{32,16},... | collective-permute-start | bytes 1769480 | tf_op jit(solution)/shard_map/ppermute | solution.py:69
  470.3 28.2 %collective-permute-start.57 = (bf16[3,2,96,512]{3,2,0,1:T(8,128)(2,1)}, bf16[3,2,96,512]{3,2,0,1:T(8,128)(2,1)}, u32[]{:S(2)}, u32[]{:S(2)}) collective-permute-start(bf16[3,2,96,512]{3,2,0,1:T(8,128)(2,1)} %get-tuple-element.296), channel_id=1, source_target_pairs={{0,16},{4,20},{8,24},{12,28},{16,32},{20,36},{24,40},{28,44},{32,4... | collective-permute-start | bytes 1769480 | tf_op jit(solution)/shard_map/ppermute | solution.py:69
  474.7 19.0 %collective-permute-start.53 = (bf16[1,2,2,48,1024]{4,3,2,1,0:T(8,128)(2,1)}, bf16[1,2,2,48,1024]{4,3,2,1,0:T(8,128)(2,1)}, u32[]{:S(2)}, u32[]{:S(2)}) collective-permute-start(bf16[1,2,2,48,1024]{4,3,2,1,0:T(8,128)(2,1)} %get-tuple-element.309), channel_id=1, source_target_pairs={{0,48},{4,52},{8,56},{12,60},{16,0},{20,4},{24,8},{28,12},{32,16},... | collective-permute-start | bytes 1179656 | tf_op jit(solution)/shard_map/ppermute | solution.py:69
  476.0 18.8 %collective-permute-start.52 = (bf16[1,2,2,48,1024]{4,3,2,1,0:T(8,128)(2,1)}, bf16[1,2,2,48,1024]{4,3,2,1,0:T(8,128)(2,1)}, u32[]{:S(2)}, u32[]{:S(2)}) collective-permute-start(bf16[1,2,2,48,1024]{4,3,2,1,0:T(8,128)(2,1)} %get-tuple-element.310), channel_id=1, source_target_pairs={{0,16},{4,20},{8,24},{12,28},{16,32},{20,36},{24,40},{28,44},{32,4... | collective-permute-start | bytes 1179656 | tf_op jit(solution)/shard_map/ppermute | solution.py:69
  537.3 18.6 %collective-permute-start.75 = (bf16[2,2,4,48,512]{4,3,2,1,0:T(8,128)(2,1)S(1)}, bf16[2,2,4,48,512]{4,3,2,1,0:T(8,128)(2,1)S(1)}, u32[]{:S(2)}, u32[]{:S(2)}) collective-permute-start(bf16[2,2,4,48,512]{4,3,2,1,0:T(8,128)(2,1)S(1)} %get-tuple-element.330), channel_id=1, source_target_pairs={{0,1},{1,2},{2,3},{3,0},{4,5},{5,6},{6,7},{7,4},{8,9},{9,10},{10,1... | collective-permute-start | bytes 2359304 | tf_op jit(solution)/shard_map/ppermute | solution.py:39
  537.3 18.6 %collective-permute-start.76 = (bf16[2,2,4,48,512]{4,3,2,1,0:T(8,128)(2,1)S(1)}, bf16[2,2,4,48,512]{4,3,2,1,0:T(8,128)(2,1)S(1)}, u32[]{:S(2)}, u32[]{:S(2)}) collective-permute-start(bf16[2,2,4,48,512]{4,3,2,1,0:T(8,128)(2,1)S(1)} %get-tuple-element.330), channel_id=1, source_target_pairs={{0,3},{1,0},{2,1},{3,2},{4,7},{5,4},{6,5},{7,6},{8,11},{9,8},{10,9... | collective-permute-start | bytes 2359304 | tf_op jit(solution)/shard_map/ppermute | solution.py:39
  573.3 20.4 %collective-permute-start.85 = (bf16[4,2,2,4,48,512]{5,4,3,2,1,0:T(8,128)(2,1)}, bf16[4,2,2,4,48,512]{5,4,3,2,1,0:T(8,128)(2,1)}, u32[]{:S(2)}, u32[]{:S(2)}) collective-permute-start(bf16[4,2,2,4,48,512]{5,4,3,2,1,0:T(8,128)(2,1)} %pad_maximum_fusion.4.mine_ref), channel_id=1, source_target_pairs={{0,4},{4,0},{8,12},{12,8},{16,20},{20,16},{24,28},{28,24},{32,36},... | collective-permute-start | bytes 9437192 | tf_op jit(solution)/shard_map/ppermute | solution.py:69
  593.7 30.9 %collective-permute-start.88 = (bf16[4,2,2,4,48,512]{5,4,3,2,1,0:T(8,128)(2,1)}, bf16[4,2,2,4,48,512]{5,4,3,2,1,0:T(8,128)(2,1)}, u32[]{:S(2)}, u32[]{:S(2)}) collective-permute-start(bf16[4,2,2,4,48,512]{5,4,3,2,1,0:T(8,128)(2,1)} %pad_maximum_fusion.3.mine_ref), channel_id=1, source_target_pairs={{0,4},{4,0},{8,12},{12,8},{16,20},{20,16},{24,28},{28,24},{32,36},... | collective-permute-start | bytes 9437192 | tf_op jit(solution)/shard_map/ppermute | solution.py:69
  (197 other events, 2147.9 us)
Sparse Core Ops, SparseCore 0:
  116.5 25.9 all-gather.2
  447.0 23.2 reduce-scatter.4
  583.9 20.4 reduce-scatter.2

commit v3 on v2

--- a/solution.py
+++ b/solution.py
@@ -15,7 +15,6 @@
 LOW = jnp.bfloat16
 F32 = jnp.float32
 MIB = 1024 * 1024
-TINY = pl.CostEstimate(flops=1, bytes_accessed=1, transcendentals=0)
 
 
 def params(*semantics, mib=30):
@@ -47,9 +46,9 @@
     return jnp.concatenate(spread_group(block), 1)
 
 
-def sum_to_owners(blocks):
+def owners_step(blocks):
     size = len(blocks)
-    return added(blocks[0], *[shifted(blocks[j], size - j) for j in range(1, size)])
+    return [blocks[0]] + [shifted(blocks[j], size - j) for j in range(1, size)]
 
 
 def to_section(block, target):
@@ -123,6 +122,10 @@
 
 def hold(*values):
     return lax.optimization_barrier(values)
+
+
+def once(values, *earlier):
+    return hold(values, *earlier)[0]
 
 
 def swap_halves(values):
@@ -189,7 +192,6 @@
             jax.ShapeDtypeStruct((rows, width), LOW),
         ],
         compiler_params=params("arbitrary"),
-        cost_estimate=TINY,
         name="project",
     )(x, gain, wq, wk, wv, cos, sin)
 
@@ -235,7 +237,6 @@
         out_specs=pl.BlockSpec((1, rows, q_lanes), lambda b, c: (b, 0, c)),
         out_shape=jax.ShapeDtypeStruct((batches, rows, q_lanes * parts), LOW),
         compiler_params=params("arbitrary", "arbitrary"),
-        cost_estimate=TINY,
         name="attend",
     )(qkv, qkv, qkv, bias)
 
@@ -261,7 +262,6 @@
             jax.ShapeDtypeStruct((batches, rows, width), LOW),
         ],
         compiler_params=params("arbitrary"),
-        cost_estimate=TINY,
         name="join",
     )(o, x, wo, gain)
 
@@ -316,34 +316,38 @@
     @pl.when(step < 2)
     def _():
         for core in range(CORES):
-            for ref, xs in zip(pieces[core * 6 : core * 6 + 2], ((0, 1, 3), (2,))):
-                for i, x in enumerate(xs):
-                    for y in range(PAIR):
-                        lay([ref[i, 0, y, k] for k in range(3)], x, y, core)
+            near_a, near_b = pieces[core * 6 : core * 6 + 2]
+            for y in range(PAIR):
+                for i, x in enumerate((0, 1, 3)):
+                    lay([near_a[i, y, 0, k] for k in range(3)], x, y, core)
+                lay([near_b[0, y, k] for k in range(3)], 2, y, core)
 
     @pl.when(step >= 2)
     def _():
         for core in range(CORES):
             for n, ref in enumerate(pieces[core * 6 + 2 : core * 6 + 6]):
                 for i, x in enumerate((0, 1, 3) if n % 2 == 0 else (2,)):
-                    lay([ref[i, 0, k] for k in range(3)], x, n // 2, core)
+                    lay([ref[(i, 0, k) if n % 2 == 0 else (0, k)] for k in range(3)], x, n // 2, core)
 
     _, up, share, _, silu = expert_hidden(xn_ref, share_ref, wg_ref, wu_ref)
     accumulate(total_ref, dot((silu * up * share).astype(LOW), wd_ref[0]))
     hand_out(total_ref, out_refs)
 
 
-def experts_forward(place, xn, share, pieces, batches, parts):
+def experts_forward(place, xn, share, pieces, batches, own, parts):
     rows, width = xn.shape
     count = share.shape[0]
     high, units = pieces[0].shape[-2:]
-    specs = []
-    for piece in pieces:
-        shape = (piece.shape[0], 1) + piece.shape[2:]
-        near = len(shape) == 6
-        index = lambda e, p, near=near, n=len(shape) - 2: (0, jnp.minimum(e, 1) if near else jnp.maximum(e - 2, 0)) + (0,) * n
-        specs.append(pl.BlockSpec(shape, index))
-    block = (batches, rows // batches // parts, width)
+    tile = (3, high, units)
+    near, far = (lambda e: jnp.minimum(e, 1)), (lambda e: jnp.maximum(e - 2, 0))
+    specs = [
+        pl.BlockSpec((3, PAIR, 1) + tile, lambda e, p: (0, 0, near(e), 0, 0, 0)),
+        pl.BlockSpec((1, PAIR) + tile, lambda e, p: (near(e), 0, 0, 0, 0)),
+        pl.BlockSpec((3, 1) + tile, lambda e, p: (0, far(e), 0, 0, 0)),
+        pl.BlockSpec((1,) + tile, lambda e, p: (far(e), 0, 0, 0)),
+    ]
+    specs = (specs + specs[2:]) * CORES
+    block = (1, own, width)
     matrix = lambda *shape: pl.BlockSpec((1,) + shape, lambda e, p: (e, 0, 0))
     return pl.pallas_call(
         experts_forward_kernel,
@@ -355,19 +359,27 @@
                 pl.BlockSpec((1, rows, 1), lambda e, p: (e, 0, 0)),
             ]
             + specs,
-            out_specs=[pl.BlockSpec(block, lambda e, p: (0, 0, 0))] * parts
+            out_specs=[pl.BlockSpec(block, lambda e, p: (0, 0, 0))] * parts * batches
             + [matrix(width, units), matrix(width, units), matrix(units, width)],
             scratch_shapes=[pltpu.VMEM((rows, width), F32)],
         ),
-        out_shape=[jax.ShapeDtypeStruct(block, LOW)] * parts
+        out_shape=[jax.ShapeDtypeStruct(block, LOW)] * parts * batches
         + [jax.ShapeDtypeStruct((count,) + shape, LOW) for shape in ((width, units), (width, units), (units, width))],
         compiler_params=params("arbitrary", mib=44),
-        cost_estimate=TINY,
         name="experts_forward",
     )(place, xn, share, *pieces)
 
 
-def experts_turn_kernel(xn_ref, share_ref, c_ref, wg_ref, wu_ref, wd_ref, hidden_ref, to_up_ref, to_gate_ref, *refs):
+def expert_specs(rows, width, units, batch):
+    return [
+        pl.BlockSpec((1, rows, 1), lambda e: (e, batch, 0)),
+        pl.BlockSpec((1, width, units), lambda e: (e, 0, 0)),
+        pl.BlockSpec((1, width, units), lambda e: (e, 0, 0)),
+        pl.BlockSpec((1, units, width), lambda e: (e, 0, 0)),
+    ]
+
+
+def experts_turn_kernel(xn_ref, c_ref, share_ref, wg_ref, wu_ref, wd_ref, hidden_ref, to_up_ref, to_gate_ref, *refs):
     gate, up, share, sigma, silu = expert_hidden(xn_ref, share_ref, wg_ref, wu_ref)
     shared = silu * share
     hidden_ref[...] = (shared * up).astype(LOW)
@@ -382,67 +394,69 @@
     hand_out(refs[-1], refs[:-1])
 
 
-def experts_turn(xn, share, c, wg, wu, wd, batches, parts):
+def experts_turn(xn, c, share, wg, wu, wd, batch, own, parts):
     rows, width = xn.shape
     count, _, units = wg.shape
     kept = pl.BlockSpec((rows, units), lambda e: (0, e))
-    block = (batches, rows // batches // parts, width)
+    block = (1, own, width)
     return pl.pallas_call(
         experts_turn_kernel,
         grid=(count,),
         in_specs=[
             pl.BlockSpec((rows, width), lambda e: (0, 0)),
-            pl.BlockSpec((1, rows, 1), lambda e: (e, 0, 0)),
-            pl.BlockSpec((rows, width), lambda e: (0, 0)),
-            pl.BlockSpec((1, width, units), lambda e: (e, 0, 0)),
-            pl.BlockSpec((1, width, units), lambda e: (e, 0, 0)),
-            pl.BlockSpec((1, units, width), lambda e: (e, 0, 0)),
-        ],
+            pl.BlockSpec((rows, width), lambda e: (batch, 0)),
+        ]
+        + expert_specs(rows, width, units, batch),
         out_specs=[kept] * 3 + [pl.BlockSpec(block, lambda e: (0, 0, 0))] * parts,
         out_shape=[jax.ShapeDtypeStruct((rows, units * count), LOW)] * 3 + [jax.ShapeDtypeStruct(block, LOW)] * parts,
         scratch_shapes=[pltpu.VMEM((rows, width), F32)],
-        compiler_params=params("arbitrary", mib=36),
-        cost_estimate=TINY,
+        compiler_params=params("arbitrary", mib=56),
         name="experts_turn",
-    )(xn, share, c, wg, wu, wd)
-
-
-def experts_backward_kernel(c_ref, up_ref, gate_ref, wg_ref, wu_ref, wd_ref, *refs):
-    total_ref = refs[-1]
+    )(xn, c, share, wg, wu, wd)
+
+
+def experts_backward_kernel(batches, *refs):
+    c_refs, up_refs, gate_refs = (refs[i * batches : (i + 1) * batches] for i in range(3))
+    wg_ref, wu_ref, wd_ref, *out_refs = refs[3 * batches : -3]
+    kept_ref, total_ref, c_ref = refs[-3:]
+
+    @pl.when(pl.program_id(0) == 0)
+    def _():
+        c_ref[...] = jnp.concatenate([ref[...] for ref in c_refs], 0)
+
     hidden = dot_nt(c_ref[...], wd_ref[0])
-    gate_grad = (hidden * gate_ref[...].astype(F32)).astype(LOW)
-    up_grad = (hidden * up_ref[...].astype(F32)).astype(LOW)
-    refs[-2][0] = gate_grad
-    refs[-2][1] = up_grad
+    gate_grad = (hidden * jnp.concatenate([ref[...] for ref in gate_refs], 0).astype(F32)).astype(LOW)
+    up_grad = (hidden * jnp.concatenate([ref[...] for ref in up_refs], 0).astype(F32)).astype(LOW)
+    kept_ref[0] = gate_grad
+    kept_ref[1] = up_grad
     accumulate(total_ref, dot_nt(gate_grad, wg_ref[0]) + dot_nt(up_grad, wu_ref[0]))
-    hand_out(total_ref, refs[:-2])
-
-
-def experts_backward(c, to_up, to_gate, wg, wu, wd, batches, parts):
-    rows, width = c.shape
+    hand_out(total_ref, out_refs)
+
+
+def experts_backward(c, to_up, to_gate, wg, wu, wd, own, parts):
+    batches = len(c)
+    rows, width = c[0].shape
     count, _, units = wg.shape
     kept = pl.BlockSpec((rows, units), lambda e: (0, e))
-    block = (batches, rows // batches // parts, width)
-    return pl.pallas_call(
-        experts_backward_kernel,
+    block = (batches, own, width)
+    return pl.pallas_call(
+        functools.partial(experts_backward_kernel, batches),
         grid=(count,),
-        in_specs=[
-            pl.BlockSpec((rows, width), lambda e: (0, 0)),
-            kept,
-            kept,
+        in_specs=[pl.BlockSpec((rows, width), lambda e: (0, 0))] * batches
+        + [kept] * 2 * batches
+        + [
             pl.BlockSpec((1, width, units), lambda e: (e, 0, 0)),
             pl.BlockSpec((1, width, units), lambda e: (e, 0, 0)),
             pl.BlockSpec((1, units, width), lambda e: (e, 0, 0)),
         ],
         out_specs=[pl.BlockSpec(block, lambda e: (0, 0, 0))] * parts
-        + [pl.BlockSpec((2, rows, units), lambda e: (0, 0, e))],
+        + [pl.BlockSpec((2, batches * rows, units), lambda e: (0, 0, e))],
         out_shape=[jax.ShapeDtypeStruct(block, LOW)] * parts
-        + [jax.ShapeDtypeStruct((2, rows, units * count), LOW)],
-        scratch_shapes=[pltpu.VMEM((rows, width), F32)],
-        compiler_params=params("arbitrary"),
-        cost_estimate=TINY,
+        + [jax.ShapeDtypeStruct((2, batches * rows, units * count), LOW)],
+        scratch_shapes=[pltpu.VMEM((batches * rows, width), F32), pltpu.VMEM((batches * rows, width), LOW)],
+        compiler_params=params("arbitrary", mib=34),
         name="experts_backward",
-    )(c, to_up, to_gate, wg, wu, wd)
+    )(*c, *to_up, *to_gate, wg, wu, wd)
 
 
 def head_grads(queries, key, value, douts, bias):
@@ -474,36 +488,47 @@
     return (grads * widen_table(cos, lanes) + swap_halves(grads * widen_table(sin, lanes))).astype(LOW)
 
 
-def attend_backward_kernel(
-    z_ref, q_ref, k_ref, v_ref, da_ref, wo_ref, wq_ref, wk_ref, wv_ref, bias_ref, cos_ref, sin_ref, dqkv_ref, dn_ref
-):
-    dout = dot_nt(da_ref[0], wo_ref[...]).astype(LOW)
-    dq, dk, dv = chunk_grads(q_ref[0], k_ref[0], v_ref[0], dout, bias_ref[0])
-    dq, dk = turned_back(dq, cos_ref[...], sin_ref[...]), turned_back(dk, cos_ref[...], sin_ref[...])
-    dqkv_ref[0] = jnp.concatenate([dq, dk, dv], -1)
-    dn = dot_nt(dq, wq_ref[...]) + dot_nt(dk, wk_ref[...]) + dot_nt(dv, wv_ref[...])
-    parts, _, own, _ = dn_ref.shape
-    for j in range(parts):
-        dn_ref[lax.rem(z_ref[0] + parts - j, parts), 0] = dn[j * own : (j + 1) * own].astype(LOW)
+def attend_backward_kernel(batches, parts, z_ref, *refs):
+    q_refs, k_refs, v_refs = (refs[i * batches : (i + 1) * batches] for i in range(3))
+    da_refs = refs[3 * batches : 3 * batches + parts]
+    wo_ref, wq_ref, wk_ref, wv_ref, bias_ref, cos_ref, sin_ref, dqkv_ref, dn_ref = refs[3 * batches + parts :]
+
+    def turn(q_ref, k_ref, v_ref):
+        da = jnp.concatenate([ref[0] for ref in da_refs], 0)
+        dout = dot_nt(da, wo_ref[...]).astype(LOW)
+        dq, dk, dv = chunk_grads(q_ref[0], k_ref[0], v_ref[0], dout, bias_ref[0])
+        dq, dk = turned_back(dq, cos_ref[...], sin_ref[...]), turned_back(dk, cos_ref[...], sin_ref[...])
+        dqkv_ref[...] = jnp.concatenate([dq, dk, dv], -1)
+        dn = dot_nt(dq, wq_ref[...]) + dot_nt(dk, wk_ref[...]) + dot_nt(dv, wv_ref[...])
+        own = dn_ref.shape[2]
+        for j in range(parts):
+            dn_ref[lax.rem(z_ref[0] + parts - j, parts), 0] = dn[j * own : (j + 1) * own].astype(LOW)
+
+    for b in range(batches):
+
+        @pl.when(pl.program_id(0) == b)
+        def _(b=b):
+            turn(q_refs[b], k_refs[b], v_refs[b])
 
 
 def attend_backward(z, qkv, da, wo, wq, wk, wv, bias, cos, sin, parts):
-    batches, rows, width = da.shape
+    batches, rows = len(qkv), qkv[0].shape[1]
+    _, own, width = da[0].shape
     q_lanes, k_lanes = wo.shape[0] // parts, KEY_VALUE_HEADS * HEAD_SIZE // parts
     k_at = wo.shape[0] // k_lanes
     full = lambda *shape: pl.BlockSpec(shape, lambda b, z: (0,) * len(shape))
     batch = lambda *shape: pl.BlockSpec((1,) + shape, lambda b, z: (b, 0, 0))
     columns = lambda lanes: pl.BlockSpec((width, lanes), lambda b, z: (0, z[0]))
     return pl.pallas_call(
-        attend_backward_kernel,
+        functools.partial(attend_backward_kernel, batches, parts),
         grid_spec=pltpu.PrefetchScalarGridSpec(
             num_scalar_prefetch=1,
             grid=(batches,),
-            in_specs=[
-                pl.BlockSpec((1, rows, q_lanes), lambda b, z: (b, 0, z[0])),
-                pl.BlockSpec((1, rows, k_lanes), lambda b, z: (b, 0, k_at + z[0])),
-                pl.BlockSpec((1, rows, k_lanes), lambda b, z: (b, 0, k_at + parts + z[0])),
-                batch(rows, width),
+            in_specs=[pl.BlockSpec((1, rows, q_lanes), lambda b, z: (0, 0, z[0]))] * batches
+            + [pl.BlockSpec((1, rows, k_lanes), lambda b, z: (0, 0, k_at + z[0]))] * batches
+            + [pl.BlockSpec((1, rows, k_lanes), lambda b, z: (0, 0, k_at + parts + z[0]))] * batches
+            + [batch(own, width)] * parts
+            + [
                 pl.BlockSpec((q_lanes, width), lambda b, z: (z[0], 0)),
                 columns(q_lanes),
                 columns(k_lanes),
@@ -513,18 +538,17 @@
                 full(rows, cos.shape[1]),
             ],
             out_specs=[
-                batch(rows, q_lanes + 2 * k_lanes),
-                pl.BlockSpec((parts, 1, rows // parts, width), lambda b, z: (0, b, 0, 0)),
+                pl.BlockSpec((rows, q_lanes + 2 * k_lanes), lambda b, z: (b, 0)),
+                pl.BlockSpec((parts, 1, own, width), lambda b, z: (0, b, 0, 0)),
             ],
         ),
         out_shape=[
-            jax.ShapeDtypeStruct((batches, rows, q_lanes + 2 * k_lanes), LOW),
-            jax.ShapeDtypeStruct((parts, batches, rows // parts, width), LOW),
+            jax.ShapeDtypeStruct((batches * rows, q_lanes + 2 * k_lanes), LOW),
+            jax.ShapeDtypeStruct((parts, batches, own, width), LOW),
         ],
-        compiler_params=params("arbitrary"),
-        cost_estimate=TINY,
+        compiler_params=params("arbitrary", mib=56),
         name="attend_backward",
-    )(z, qkv, qkv, qkv, da, wo, wq, wk, wv, bias, cos, sin)
+    )(z, *qkv, *qkv, *qkv, *da, wo, wq, wk, wv, bias, cos, sin)
 
 
 def own_backward_kernel(q_ref, k_ref, v_ref, da_ref, wo_ref, bias_ref, cos_ref, sin_ref, dq_ref, *out_refs):
@@ -567,7 +591,6 @@
         out_specs=[pl.BlockSpec((batches, own, q_lanes), lambda c: (0, 0, c))] + [full(*block)] * parts,
         out_shape=[jax.ShapeDtypeStruct((batches, own, q_lanes * parts), LOW)] + [jax.ShapeDtypeStruct(block, LOW)] * parts,
         compiler_params=params("arbitrary"),
-        cost_estimate=TINY,
         name="own_backward",
     )(qkv, qkv, qkv, da, wo, bias, cos, sin)
 
@@ -578,7 +601,10 @@
     return (ring * PAIR + pair) * CORES + lax.rem(place_ref[2] + core, CORES)
 
 
-def expert_grad_kernel(cut, place_ref, left_ref, right_ref, mine_ref, other_ref, turned_ref):
+def expert_grad_kernel(cut, batches, place_ref, *refs):
+    left_refs, right_refs = refs[:batches], refs[batches:-3]
+    mine_ref, other_ref, turned_ref = refs[-3:]
+    tokens = left_refs[0].shape[0]
     rows = mine_ref.shape[-2] // cut
     lanes = mine_ref.shape[-1]
     step = pl.program_id(1)
@@ -586,11 +612,13 @@
 
         @pl.when((pl.program_id(0) == 0) & (step == 0))
         def _():
-            turned_ref[...] = left_ref[...].T
-
-        product = dot(turned_ref[...], right_ref[0]).astype(LOW)
+            for i, ref in enumerate(left_refs):
+                turned_ref[:, i * tokens : (i + 1) * tokens] = ref[...].T
+
+        product = dot(turned_ref[...], right_refs[0][0]).astype(LOW)
     else:
-        product = dot_tn(left_ref[...], right_ref[0]).astype(LOW)
+        products = [dot_tn(left[...], right[0]) for left, right in zip(left_refs, right_refs)]
+        product = sum(products[1:], products[0]).astype(LOW)
     half = lax.rem(step, 2)
 
     def place(refs, ring_first):
@@ -613,39 +641,88 @@
                 place((mine_ref, other_ref) if core == 0 else (other_ref, mine_ref), ring_first)
 
 
-def expert_grad(place, left, right, count, cut):
-    number, rows, _ = right.shape
-    left_lanes = left.shape[1] // count if cut > 1 else left.shape[1]
-    right_lanes = right.shape[2] if cut > 1 else right.shape[2] // count
+def expert_grad(place, lefts, rights, count, cut):
+    number, right_rows, right_lanes = rights[0].shape
+    rows, left_lanes = lefts[0].shape
+    if cut > 1:
+        left_lanes = left_lanes // count
+    else:
+        right_lanes = right_lanes // count
     owners = RING * PAIR * CORES
     high, lanes = left_lanes // owners, right_lanes // cut
     shape = (2, owners, high * cut, lanes)
     out = pl.BlockSpec((1, 1) + shape[1:], lambda r, e, p: (r, e // 2, 0, 0, 0))
     left_spec = pl.BlockSpec((rows, left_lanes), lambda r, e, p: (0, e if cut > 1 else 0))
-    right_spec = pl.BlockSpec((1, rows, right_lanes), lambda r, e, p: (r, 0, 0 if cut > 1 else e))
-    return pl.pallas_call(
-        functools.partial(expert_grad_kernel, cut),
+    right_spec = pl.BlockSpec((1, right_rows, right_lanes), lambda r, e, p: (r, 0, 0 if cut > 1 else e))
+    batches = len(lefts)
+    return pl.pallas_call(
+        functools.partial(expert_grad_kernel, cut, batches),
         grid_spec=pltpu.PrefetchScalarGridSpec(
             num_scalar_prefetch=1,
             grid=(number, count),
-            in_specs=[left_spec, right_spec],
+            in_specs=[left_spec] * batches + [right_spec] * len(rights),
             out_specs=[out, out],
-            scratch_shapes=[pltpu.VMEM((left_lanes, rows) if cut == 1 else (16, 128), LOW)],
+            scratch_shapes=[pltpu.VMEM((left_lanes, rows * batches) if cut == 1 else (16, 128), LOW)],
         ),
         out_shape=[jax.ShapeDtypeStruct((number,) + shape, LOW)] * 2,
         compiler_params=params("arbitrary", "arbitrary"),
         name="expert_grad",
-    )(place, left, right)
-
-
-def dense_grad_kernel(
-    place_ref, z_ref, mixed_ref, da_ref, xn_ref, dqkv_ref, mine_ref, other_ref, into_ref, out_of_ref
+    )(place, *lefts, *rights)
+
+
+def chip_sum_kernel(
+    mine_inner, other_inner, mine_outer, other_outer, keep_ring, to_above, to_below, keep_pair, to_pair, to_pair_next
 ):
+    matrix, kind = pl.program_id(0), pl.program_id(1)
+    ring = {index: (keep_ring, at) for at, index in enumerate((0, 1, 2, 7))}
+    ring.update({3: (to_above, 0), 4: (to_above, 1), 5: (to_below, 0), 6: (to_below, 1)})
+
+    def add(mine, other, ring_first):
+        for index in range(2 * RING * PAIR):
+            value = (mine[0, 0, index].astype(F32) + other[0, 0, index].astype(F32)).astype(LOW)
+            if ring_first:
+                ref, at = ring[index // PAIR]
+                ref[0, at, index % PAIR] = value
+            elif index < 2 * RING:
+                keep_pair[0, index] = value
+            else:
+                (to_pair if index < 3 * RING else to_pair_next)[0, index % RING] = value
+
+    for inner in (True, False):
+        for ring_first in (True, False):
+
+            @pl.when(((matrix < 2) == inner) & ((kind == 0) == ring_first))
+            def _(inner=inner, ring_first=ring_first):
+                add(*((mine_inner, other_inner) if inner else (mine_outer, other_outer)), ring_first)
+
+
+def chip_sum(inner, outer):
+    tile = inner[0].shape[3:]
+    block = (1, 1, 2 * RING * PAIR) + tile
+    inner_spec = pl.BlockSpec(block, lambda m, k: (jnp.minimum(m, 1), jnp.where(m < 2, k, 1), 0, 0, 0))
+    outer_spec = pl.BlockSpec(block, lambda m, k: (0, jnp.where(m < 2, 0, k), 0, 0, 0))
+    shapes = [(4, PAIR), (2, PAIR), (2, PAIR), (2 * RING,), (RING,), (RING,)]
+    return pl.pallas_call(
+        chip_sum_kernel,
+        grid=(3, 2),
+        in_specs=[inner_spec, inner_spec, outer_spec, outer_spec],
+        out_specs=[pl.BlockSpec((1,) + shape + tile, lambda m, k, n=len(shape) + 2: (m,) + (0,) * n) for shape in shapes],
+        out_shape=[jax.ShapeDtypeStruct((3,) + shape + tile, LOW) for shape in shapes],
+        compiler_params=params("arbitrary", "arbitrary", mib=56),
+        name="chip_sum",
+    )(*inner, *outer)
+
+
+def dense_grad_kernel(batches, parts, place_ref, z_ref, *refs):
     del z_ref
+    mixed_refs, xn_refs, da_refs = refs[:batches], refs[batches : 2 * batches], refs[2 * batches : 2 * batches + parts]
+    dqkv_ref, mine_ref, other_ref, into_ref, out_of_ref = refs[2 * batches + parts :]
+    rows = xn_refs[0].shape[0]
     high = mine_ref.shape[-2]
     lanes, wide = out_of_ref.shape[-1], dqkv_ref.shape[1]
-    into = dot_tn(xn_ref[...], dqkv_ref[...]).astype(LOW)
-    out_of = dot_tn(mixed_ref[...], da_ref[...]).astype(LOW)
+    into = sum(dot_tn(ref[...], dqkv_ref[b * rows : (b + 1) * rows]) for b, ref in enumerate(xn_refs)).astype(LOW)
+    da = [jnp.concatenate([ref[b] for ref in da_refs], 0) for b in range(batches)]
+    out_of = sum(dot_tn(ref[...], da[b]) for b, ref in enumerate(mixed_refs)).astype(LOW)
     for chip in range(RING * PAIR):
         for core in range(CORES):
             owner = chip * CORES + core
@@ -664,31 +741,29 @@
 
 
 def dense_grad(place, z, mixed, da, xn, dqkv, parts):
-    rows, width = xn.shape
+    batches = len(xn)
+    rows, width = xn[0].shape
     owners = RING * PAIR * CORES
-    q_lanes, wide = mixed.shape[1] // parts, dqkv.shape[1]
+    q_lanes, wide = mixed[0].shape[1] // parts, dqkv.shape[1]
     high, lanes = width // owners // 2, width // CORES // 2
     shape = (1, 2 * RING, PAIR, high, wide + lanes)
-    whole = lambda columns: pl.BlockSpec((rows, columns), lambda i, p, z: (0, 0))
-    return pl.pallas_call(
-        dense_grad_kernel,
+    whole = lambda *shape: pl.BlockSpec(shape, lambda i, p, z: (0,) * len(shape))
+    return pl.pallas_call(
+        functools.partial(dense_grad_kernel, batches, parts),
         grid_spec=pltpu.PrefetchScalarGridSpec(
             num_scalar_prefetch=2,
             grid=(1,),
-            in_specs=[
-                pl.BlockSpec((rows, q_lanes), lambda i, p, z: (0, z[0])),
-                whole(width),
-                whole(width),
-                whole(wide),
-            ],
+            in_specs=[pl.BlockSpec((rows, q_lanes), lambda i, p, z: (0, z[0]))] * batches
+            + [whole(rows, width)] * batches
+            + [whole(*da[0].shape)] * parts
+            + [whole(*dqkv.shape)],
             out_specs=[pl.BlockSpec(shape, lambda i, p, z: (0,) * 5)] * 2,
             scratch_shapes=[pltpu.VMEM((owners, 2, high, wide), LOW), pltpu.VMEM((owners, 2, high, lanes), LOW)],
         ),
         out_shape=[jax.ShapeDtypeStruct(shape, LOW)] * 2,
-        compiler_params=params("arbitrary"),
-        cost_estimate=TINY,
+        compiler_params=params("arbitrary", mib=56),
         name="dense_grad",
-    )(place, z, mixed, da, xn, dqkv)
+    )(place, z, *mixed, *xn, *da, dqkv)
 
 
 def dense_layout_kernel(by_x, place_ref, z_ref, mine_ref, other_ref, *refs):
@@ -799,120 +874,141 @@
     sin = jnp.concatenate([-sin_half, sin_half] * 2, -1)
     cos_all, sin_all = jnp.concatenate([cos] * batches, 0), jnp.concatenate([sin] * batches, 0)
 
-    def attention_in(x):
-        qkv, xn = project(x.reshape(batches * rows, width), attn_gain, wq, wk, wv, cos_all, sin_all)
-        return qkv.reshape(batches, rows, -1), xn
-
-    def attention_out(qkv, x):
+    def attention_in(x, cos, sin):
+        qkv, xn = project(x.reshape(-1, width), attn_gain, wq, wk, wv, cos, sin)
+        return qkv.reshape(-1, rows, qkv.shape[1]), xn
+
+    def attention_out(qkv, bias, x):
         mixed = attend(qkv, bias, parts)
         h1, xn2 = join(mixed, x, wo, ffn_gain, own)
-        return mixed.reshape(batches * rows, -1), h1, xn2.reshape(batches * rows, width)
-
-    near = jnp.stack([near, near_y], 1)
+        return mixed.reshape(-1, wo.shape[0]), h1, xn2.reshape(-1, width)
+
+    near = jnp.stack([near, near_y])
     near_1 = ring_gather_step(near)
     far_2 = ring_gather_next(far_1)
     far_a = jnp.stack([far, *far_1])
     far_ya = moved(far_a, y=1)
-    qkv, _ = attention_in(start)
-    _, h1, xn2 = attention_out(qkv, start)
+    qkv, _ = attention_in(start, cos_all, sin_all)
+    _, h1, xn2 = attention_out(qkv, bias, start)
 
     xn2, near_1, far_2, far_ya = hold(xn2, near_1, far_2, far_ya)
+    near_b = moved(near_1[0][:, 0], x=1), moved(near_1[1][:, 1], x=-1)
+    far_b = jnp.stack(far_2)
+    far_yb = moved(far_b, y=1)
     near_a = jnp.stack([near, *near_1])
-    near_b = ring_gather_next(near_1)
-    far_b = jnp.stack(far_2)[None]
-    far_yb = moved(far_b, y=1)
-    others = [moved(piece, core=1) for piece in (near_a, far_a, far_b, far_ya)]
+    others = [moved(piece, core=1) for piece in (near_a, far_a)]
 
     near_b, far_yb, others = hold(near_b, far_yb, others)
-    near_b = jnp.stack(near_b)[None]
-    others = [others[0], moved(near_b, core=1), *others[1:], moved(far_yb, core=1)]
-    pieces = [near_a, near_b, far_a, far_b, far_ya, far_yb, *others]
-    *blocks, wg, wu, wd = experts_forward(dp_place, xn2, share, pieces, batches, parts)
+    near_b = jnp.stack(near_b)
+    pieces = [near_a, near_b, far_a, far_b, far_ya, far_yb]
+    pieces += [others[0], moved(near_b, core=1), others[1], *[moved(piece, core=1) for piece in (far_b, far_ya, far_yb)]]
+    *blocks, wg, wu, wd = experts_forward(dp_place, xn2, share, pieces, batches, own, parts)
+    blocks = [blocks[b * parts : (b + 1) * parts] for b in range(batches)]
     c_second = lax.all_gather(out_grad, "expert")
     c_second = jnp.concatenate([lax.dynamic_index_in_dim(c_second, (z + parts - j) % parts, 0, False) for j in range(parts)], 1)
-    result = (h1 + sum_to_owners(blocks)).astype(LOW)
-    received = gather_group(to_section(result, 1))
-
-    x = jnp.where(section == 0, start, received)
-    qkv, xn = attention_in(x)
-    mixed, h1, xn2 = attention_out(qkv, x)
     flat_second = c_second.reshape(batches * rows, width)
-    hidden, to_up, to_gate, *blocks = experts_turn(xn2, share, flat_second, wg, wu, wd, batches, parts)
-
-    def after_experts(blocks, c_own):
-        norm_part, ffn_grad = norm_back(sum_to_owners(blocks), h1, ffn_gain)
-        return c_own.astype(F32) + norm_part, ffn_grad
-
-    def after_attention(after, dn_own):
-        norm_part, attn_grad = norm_back(dn_own, x[:, :own].astype(F32), attn_gain)
-        return after + norm_part, attn_grad
-
-    outputs = dot(hidden, wd.reshape(local_experts * units, width)).astype(LOW).reshape(batches, parts, own, width)
-    outputs = jnp.flip(jnp.moveaxis(outputs, 1, 0), 0)
-    outputs = lax.dynamic_slice_in_dim(jnp.concatenate([outputs, outputs], 0), (2 * parts - 1 - z) % parts, parts, 0)
-    after, _ = after_experts(blocks, out_grad)
-    after, outputs = hold(after, outputs)
-    dq, *blocks = own_backward(qkv, after.astype(LOW), wo, bias, cos, sin, parts)
-    dn_own = dot_nt(dq.reshape(batches * own, -1), wq)
-    dkv = sum_to_owners(blocks).astype(LOW).reshape(batches * own, -1)
-    dn_own = dn_own + dot_nt(dkv[:, : wk.shape[1]], wk) + dot_nt(dkv[:, wk.shape[1] :], wv)
-    input_grad, _ = after_attention(after, dn_own.reshape(batches, own, width))
-    received_own = to_section(input_grad.astype(LOW), 0)
-
-    c_own = jnp.where(section == 1, out_grad, received_own)
-    c = jnp.where(section == 1, c_second, gather_group(received_own))
-    flat_c = c.reshape(batches * rows, width)
-    *blocks, hidden_grads = experts_backward(flat_c, to_up, to_gate, wg, wu, wd, batches, parts)
-    after, ffn_grad = after_experts(blocks, c_own)
+    received = []
+    result = None
+    for b in range(batches):
+        came = owners_step(blocks[b])
+        if b > 0:
+            came = once(came, result)
+        result = (h1[b : b + 1] + added(*came)).astype(LOW)
+        received.append(spread_group(to_section(result, 1)))
+
+    biases = [bias[b : b + 1] for b in range(batches)]
+    x, qkv, xn, mixed, h1, xn2, hidden, to_up, to_gate, blocks = ([None] * batches for _ in range(10))
+    for b in range(batches):
+        if b > 0:
+            received[b] = once(received[b], hidden[b - 1])
+        x[b] = jnp.where(section == 0, start[b : b + 1], jnp.concatenate(received[b], 1))
+        qkv[b], xn[b] = attention_in(x[b], cos, sin)
+        mixed[b], h1[b], xn2[b] = attention_out(qkv[b], biases[b], x[b])
+        hidden[b], to_up[b], to_gate[b], *blocks[b] = experts_turn(xn2[b], flat_second, share, wg, wu, wd, b, own, parts)
+    x_own = jnp.concatenate([rows_of[:, :own] for rows_of in x], 0).astype(F32)
+
+    after, dq, kv_came = ([None] * batches for _ in range(3))
+    for b in range(batches):
+        came = owners_step(blocks[b])
+        if b > 0:
+            came = once(came, dq[b - 1])
+        after[b] = out_grad[b : b + 1].astype(F32) + norm_back(added(*came), h1[b], ffn_gain)[0]
+        dq[b], *kv_blocks = own_backward(qkv[b], after[b].astype(LOW), wo, biases[b], cos, sin, parts)
+        kv_came[b] = owners_step(kv_blocks)
+    kv_came[0] = once(kv_came[0], dq[-1])
+    received_own = []
+    for b in range(batches):
+        if b > 0:
+            kv_came[b] = once(kv_came[b], input_grad)
+        dkv = added(*kv_came[b]).astype(LOW).reshape(own, -1)
+        dn_own = dot_nt(dq[b].reshape(own, -1), wq)
+        dn_own = dn_own + dot_nt(dkv[:, : wk.shape[1]], wk) + dot_nt(dkv[:, wk.shape[1] :], wv)
+        input_grad = after[b] + norm_back(dn_own[None], x_own[b : b + 1], attn_gain)[0]
+        received_own.append(to_section(input_grad.astype(LOW), 0))
+
+    c_own = jnp.where(section == 1, out_grad, jnp.concatenate(received_own, 0))
+    c = [jnp.where(section == 1, c_second[b : b + 1], gather_group(received_own[b])).reshape(rows, width) for b in range(batches)]
+    *blocks, hidden_grads = experts_backward(c, to_up, to_gate, wg, wu, wd, own, parts)
+    norm_part, ffn_grad = norm_back(added(*owners_step(blocks)), jnp.concatenate(h1, 0), ffn_gain)
+    after = c_own.astype(F32) + norm_part
     both = [
-        expert_grad(dp_place, xn2, hidden_grads, local_experts, 1),
-        expert_grad(dp_place, hidden, flat_c[None], local_experts, width // units),
+        expert_grad(dp_place, xn2, [hidden_grads], local_experts, 1),
+        expert_grad(dp_place, hidden, [block[None] for block in c], local_experts, width // units),
     ]
     after, both = hold(after, both)
-    both = [(mine, moved(other, core=1)) for mine, other in both]
-    da = gather_group(after.astype(LOW))
-    by_ring, by_pair = (
-        jnp.concatenate([added(mine[:, kind], other[:, kind]).astype(LOW) for mine, other in both], 0) for kind in range(2)
-    )
-    by_ring = by_ring.reshape((-1, 2 * RING, PAIR) + by_ring.shape[2:])
-    by_pair = by_pair.reshape((-1, PAIR, 2 * RING) + by_pair.shape[2:])
-    da, by_ring, by_pair = hold(da, by_ring, by_pair)
-
-    ring_1 = ring_step(by_ring)
-    pair_1 = [moved(by_pair[:, 1, :RING], y=1), moved(by_pair[:, 1, RING:], y=1)]
+    inner, outer = [(mine, moved(other, core=1)) for mine, other in both]
+    da = spread_group(after.astype(LOW))
+    keep_ring, to_above, to_below, keep_pair, *to_pair = chip_sum(inner, outer)
+    da, to_above, to_below, to_pair = hold(da, to_above, to_below, to_pair)
+
+    ring_1 = moved(to_above, x=1), moved(to_below, x=-1)
+    pair_1 = [moved(block, y=1) for block in to_pair]
     dqkv, dn = attend_backward(z_at, qkv, da, wo, wq, wk, wv, bias, cos, sin, parts)
-    mine, other = dense_grad(
-        dp_place, z_at, mixed, da.reshape(batches * rows, width), xn, dqkv.reshape(batches * rows, -1), parts
-    )
+    mine, other = dense_grad(dp_place, z_at, mixed, da, xn, dqkv, parts)
     dn_own = lax.psum_scatter(dn, "expert", scatter_dimension=0, tiled=True)[0].astype(F32)
 
     mine, other, ring_1, pair_1[0] = hold(mine, other, ring_1, pair_1[0])
-    dense = added(mine, moved(other, core=1)).astype(LOW)
+    other = moved(other, core=1)
+    outputs = jnp.stack([dot(units_of, wd.reshape(local_experts * units, width)).astype(LOW) for units_of in once(hidden, mine)])
+    other = once(other, outputs)
+    dense = added(mine, other).astype(LOW)
 
     (dense,) = hold(dense)
     dense_1 = ring_step(dense)
-
-    dense_1, dn_own = hold(dense_1, dn_own)
+    outputs = outputs.reshape(batches, parts, own, width)
+    outputs = jnp.stack([lax.dynamic_index_in_dim(outputs, (z + parts - i) % parts, 1, False) for i in range(parts)])
+
+    dense_1, outputs, dn_own = hold(dense_1, outputs, dn_own)
+    outputs = lax.psum_scatter(outputs, "expert", scatter_dimension=0, tiled=True)[0]
     dense_2 = ring_next(dense, dense_1)
-    ring_2 = ring_next(by_ring, ring_1)
-    input_grad, attn_grad = after_attention(after, dn_own)
+    norm_part, attn_grad = norm_back(dn_own, x_own, attn_gain)
+    input_grad = after + norm_part
     gains = jnp.stack([attn_grad, ffn_grad])
     gains = gains + exchanged(gains, "expert", 1)
+    ring_2 = (
+        moved(added(keep_ring[:, 2], ring_1[0][:, 1]).astype(LOW), x=1),
+        moved(added(keep_ring[:, 3], ring_1[1][:, 0]).astype(LOW), x=-1),
+    )
 
     dense_2, gains, ring_2 = hold(dense_2, gains, ring_2)
     dense = ring_end(dense, dense_1, dense_2)[:, 0]
     dense_3 = moved(dense[:, 1].astype(LOW), y=1)
     gains = gains + exchanged(gains, "expert", 2)
-    ring_sums = ring_end(by_ring, ring_1, ring_2)
-
-    dense_3, gains, ring_sums, pair_1 = hold(dense_3, gains, ring_sums, pair_1)
+    ring_sums = jnp.stack(
+        [
+            added(keep_ring[:, 0], ring_1[1][:, 1], ring_2[0]),
+            added(keep_ring[:, 1], ring_1[0][:, 0], ring_2[1]),
+        ]
+    )
+
+    dense_3, gains, ring_sums = hold(dense_3, gains, ring_sums)
     owned = added(dense[:, 0], dense_3).astype(LOW)
     first, second = owned[0], by_lanes(owned[1])
     first_1 = [shifted(first, k) for k in range(1, parts)]
     second_1 = [moved(second, x=k) for k in range(1, RING)]
-    pair_sums = added(by_pair[:, 0], jnp.concatenate(pair_1, 1)).astype(LOW)
-
-    first_1, second_1, pair_sums = hold(first_1, second_1, pair_sums)
+
+    first_1, second_1, pair_1 = hold(first_1, second_1, pair_1)
+    pair_sums = added(keep_pair, jnp.concatenate(pair_1, 1)).astype(LOW)
     first = jnp.stack([first] + first_1)
     first_2 = moved(first, y=1)
     second = jnp.stack([second] + second_1)
@@ -928,7 +1024,7 @@
     ring_away = moved(ring_sums[:, :, 1].astype(LOW), y=1)
     gains = gains + exchanged(gains, "dp", 2)
 
-    first_3, second_3, ring_away, gains = hold(first_3, second_3, ring_away, gains)
+    first_3, second_3, ring_away, gains, outputs = hold(first_3, second_3, ring_away, gains, outputs)
     first_4 = ring_gather_next(first_3)
     second_4 = group_gather_next(second_3)
     pair_3 = ring_next(pair_sums, pair_2)
@@ -956,9 +1052,7 @@
         grad.reshape(weight.shape) for grad, weight in zip(laid, (wq, wk, wv, wo))
     )
 
-    outputs, dqkv = hold(outputs, dqkv)
-    outputs = lax.psum_scatter(outputs, "expert", scatter_dimension=0, tiled=True)[0]
-    layer_outputs = (h1 + outputs.astype(F32)).astype(LOW)
+    layer_outputs = (jnp.concatenate(h1, 0) + outputs.astype(F32)).astype(LOW)
     return (
         layer_outputs[None],
         input_grad[None],

time: 647 us -> 597 us (0.923)
  waiting for transfers between devices: 218 us -> 128 us
  Pallas kernels: 159 us -> 186 us
  starting transfers between devices: 115 us -> 141 us
  local copies, waits for them, and re-layouts: 62.5 us -> 48.9 us
    ppermute x34 -> x49, waiting for transfers between devices: 94.7 us -> 37.1 us  [shifted(): lax.ppermute(block, 'expert', [(i, (i + by) % size) for i in range(size)])]
    pallas_call x5 -> x6, Pallas kernels: 42.9 us -> 62.1 us  [the longest x2 16.2 us: expert_grad(): pl.pallas_call(functools.partial(expert_grad_kernel, cut, batches), grid_...]
    ppermute x2 -> x4, waiting for transfers between devices: 18.3 us -> 5.63 us  [to_section(): return lax.ppermute(block, 'section', [(1 - target, target)])]
    ppermute x47, starting transfers between devices: 54.7 us -> 65.1 us  [moved(): return lax.ppermute(block, 'dp', route)]
    ppermute x47, waiting for transfers between devices: 89.6 us -> 79.4 us  [moved(): return lax.ppermute(block, 'dp', route)]
    ppermute x34 -> x49, starting transfers between devices: 40.9 us -> 50.9 us  [shifted(): lax.ppermute(block, 'expert', [(i, (i + by) % size) for i in range(size)])]
    reduce_scatter x1, waiting for transfers between devices: 9.47 us -> 0.02 us  [local(): lax.psum_scatter(outputs, 'expert', scatter_dimension=0, tiled=True)[0]]
    unnamed x284 -> x290, local copies, waits for them, and re-layouts: 36.9 us -> 30.1 us
  transfers between devices with their start and end apart: 92 -> 109, of which waited for: 48 -> 42; matrix products, arithmetic and copies ran while one was open for 11% -> 13% of each run, Pallas kernels for 12% -> 28%
where the time goes in v3:
time: 597 us; the launch traced here: 590 us
  Pallas kernels  186 us (31%)
  starting transfers between devices  141 us (24%)
  waiting for transfers between devices  128 us (21%)
  other arithmetic  57.2 us (10%)
  local copies, waits for them, and re-layouts  48.9 us (8%)
  between operations  16.5 us (3%)
  matrix products  12.2 us (2%)
    ppermute x47, waiting for transfers between devices, moved(): return lax.ppermute(block, 'dp', route)  79.4 us
    ppermute x47, starting transfers between devices, moved(): return lax.ppermute(block, 'dp', route)  65.1 us
    ppermute x49, starting transfers between devices, shifted(): lax.ppermute(block, 'expert', [(i, (i + by) % size) for i in range(size)])  50.9 us
    ppermute x49, waiting for transfers between devices, shifted(): lax.ppermute(block, 'expert', [(i, (i + by) % size) for i in range(size)])  37.1 us
    unnamed x290, local copies, waits for them, and re-layouts  30.1 us
    pallas_call x2, Pallas kernels, experts_turn(): pl.pallas_call(experts_turn_kernel, grid=(count,), in_specs=[pl.BlockSpec...  29.8 us
    pallas_call x1, Pallas kernels, experts_forward(): pl.pallas_call(experts_forward_kernel, grid_spec=pltpu.PrefetchScalarGrid...  20.5 us
    pallas_call x3, Pallas kernels, attend(): pl.pallas_call(attend_kernel, grid=(batches, parts), in_specs=[pl.BlockSp...  19.2 us
  transfers between devices with their start and end apart: 109, of which 42 were waited for; matrix products, arithmetic and copies ran while one was open for 13% of the time, Pallas kernels for 28%

profile of v3, /device:TPU:1, one launch (start us, length us, event | category | flops | bytes accessed | tf_op | source)
XLA Modules:
  0.0 589.9 jit_solution(3400411579079697071)
XLA Ops:
  47.0 9.2 %project.3 = (bf16[512,2560]{1,0:T(8,128)(2,1)S(1)}, bf16[512,1536]{1,0:T(8,128)(2,1)}) custom-call(bf16[512,1536]{1,0:T(8,128)(2,1)S(1)} %bitcast.363, f32[1,1536]{1,0:T(1,128)S(1)} %copy-done.49, bf16[1536,1536]{1,0:T(8,128)(2,1)S(1)} %bitcast.317, bf16[1536,512]{1,0:T(8,128)(2,1)S(1)} %bitcast.353, bf16[1536,512]{1,0:T(8,128)(2,1)S(1)} %bitcast.357, ...), custom_call_target="tpu_custom_call" | custom-call | tf_op jit(solution)/shard_map/project/pallas_call | solution.py:177
  56.4 9.6 %attend.3.o_ref = bf16[2,256,1536]{2,1,0:T(8,128)(2,1)S(1)} custom-call(bf16[2,256,2560]{2,1,0:T(8,128)(2,1)S(1)} %bitcast.360, bf16[2,256,2560]{2,1,0:T(8,128)(2,1)S(1)} %bitcast.361, bf16[2,256,2560]{2,1,0:T(8,128)(2,1)S(1)} %bitcast.362, f32[2,256,256]{2,1,0:T(8,128)S(1)} %and_select_fusion.bias_ref.refs_14_), custom_call_target="tpu_custom_call" | custom-call | tf_op jit(solution)/shard_map/attend/pallas_call | solution.py:228
  69.4 5.3 collective-permute-done.9
  94.8 5.8 collective-permute-done.15
  111.7 20.5 %experts_forward.1 = (bf16[1,64,1536]{2,1,0:T(8,128)(2,1)S(1)}, bf16[1,64,1536]{2,1,0:T(8,128)(2,1)}, bf16[1,64,1536]{2,1,0:T(8,128)(2,1)}, bf16[1,64,1536]{2,1,...) custom-call(s32[3]{0:T(128)S(1)} %pad_add_fusion.place_ref, ...), custom_call_target="tpu_custom_call" | custom-call | tf_op jit(solution)/shard_map/experts_forward/pallas_call | solution.py:352
  144.0 5.2 collective-permute-done.25
  149.4 4.9 collective-permute-start.26
  157.2 5.5 collective-permute-start.33
  170.3 6.4 %collective-permute-done.27 = bf16[1,64,1536]{2,1,0:T(8,128)(2,1)S(1)} collective-permute-done((bf16[1,64,1536]{2,1,0:T(8,128)(2,1)S(1)}, bf16[1,64,1536]{2,1,0:T(8,128)(2,1)S(1)}, u32[]{:S(2)}, u32[]{:S(2)}) %collective-permute-start.27) | collective-permute-done | bytes 196640 | tf_op jit(solution)/shard_map/ppermute | solution.py:38
  180.0 4.8 project.4
  192.9 15.0 %experts_turn.2 = (bf16[256,2048]{1,0:T(8,128)(2,1)}, bf16[256,2048]{1,0:T(8,128)(2,1)}, bf16[256,2048]{1,0:T(8,128)(2,1)}, bf16[1,64,1536]{2,1,0:T(8,128)(2,1)}...) custom-call(bf16[256,1536]{1,0:T(8,128)(2,1)} %bitcast.370, ...), custom_call_target="tpu_custom_call" | custom-call | tf_op jit(solution)/shard_map/experts_turn/pallas_call | solution.py:402
  213.3 4.8 project.5
  218.2 4.8 attend.5.o_ref
  226.3 14.7 %experts_turn.3 = (bf16[256,2048]{1,0:T(8,128)(2,1)}, bf16[256,2048]{1,0:T(8,128)(2,1)}, bf16[256,2048]{1,0:T(8,128)(2,1)}, bf16[1,64,1536]{2,1,0:T(8,128)(2,1)}...) custom-call(bf16[256,1536]{1,0:T(8,128)(2,1)} %bitcast.372, ...), custom_call_target="tpu_custom_call" | custom-call | tf_op jit(solution)/shard_map/experts_turn/pallas_call | solution.py:402
  252.0 8.1 %own_backward.2 = (bf16[1,64,1536]{2,1,0:T(8,128)(2,1)S(1)}, bf16[1,64,1024]{2,1,0:T(8,128)(2,1)S(1)}, bf16[1,64,1024]{2,1,0:T(8,128)(2,1)S(1)}, bf16[1,64,1024]...) custom-call(bf16[1,256,2560]{2,1,0:T(8,128)(2,1)S(1)} %bitcast.337, bf16[1,256,2560]{2,1,0:T(8,128)(2,1)S(1)} %bitcast.338, ...), custom_call_target="tpu_custom_call" | custom-call | tf_op jit(solution)/shard_map/own_backward/pallas_call | solution.py:578
  265.2 8.2 %own_backward.3 = (bf16[1,64,1536]{2,1,0:T(8,128)(2,1)S(1)}, bf16[1,64,1024]{2,1,0:T(8,128)(2,1)S(1)}, bf16[1,64,1024]{2,1,0:T(8,128)(2,1)S(1)}, bf16[1,64,1024]...) custom-call(bf16[1,256,2560]{2,1,0:T(8,128)(2,1)S(1)} %bitcast.346, bf16[1,256,2560]{2,1,0:T(8,128)(2,1)S(1)} %bitcast.347, ...), custom_call_target="tpu_custom_call" | custom-call | tf_op jit(solution)/shard_map/own_backward/pallas_call | solution.py:578
  301.5 5.5 collective-permute-done.54
  310.2 14.9 %experts_backward.1 = (bf16[2,64,1536]{2,1,0:T(8,128)(2,1)S(1)}, bf16[2,64,1536]{2,1,0:T(8,128)(2,1)S(1)}, bf16[2,64,1536]{2,1,0:T(8,128)(2,1)S(1)}, bf16[2,64,1...) custom-call(bf16[256,1536]{1,0:T(8,128)(2,1)S(1)} %bitcast.367, bf16[256,1536]{1,0:T(8,128)(2,1)S(1)} %bitcast.366, ...), custom_call_target="tpu_custom_call" | custom-call | tf_op jit(solution)/shard_map/experts_backward/pallas_call | solution.py:442
  327.3 5.5 expert_grad.3
  334.5 10.7 %expert_grad.2 = (bf16[2,2,16,96,512]{4,3,2,1,0:T(8,128)(2,1)S(1)}, bf16[2,2,16,96,512]{4,3,2,1,0:T(8,128)(2,1)S(1)}) custom-call(s32[3]{0:T(128)S(1)} %copy-done.52, bf16[256,1536]{1,0:T(8,128)(2,1)S(1)} %bitcast.371, bf16[256,1536]{1,0:T(8,128)(2,1)S(1)} %bitcast.373, bf16[2,512,2048]{2,1,0:T(8,128)(2,1)S(1)} %get-tuple-element.285.refs_2_), custom_call_target="tpu_custom_call" | custom-call | tf_op jit(solution)/shard_map/expert_grad/pallas_call | solution.py:658
  347.9 6.3 %collective-permute-start.63 = (bf16[2,2,16,96,512]{4,3,2,1,0:T(8,128)(2,1)S(1)}, bf16[2,2,16,96,512]{4,3,2,1,0:T(8,128)(2,1)}, u32[]{:S(2)}, u32[]{:S(2)}) collective-permute-start(bf16[2,2,16,96,512]{4,3,2,1,0:T(8,128)(2,1)S(1)} %get-tuple-element.293), channel_id=1, source_target_pairs={{0,4},{4,0},{8,12},{12,8},{16,20},{20,16},{24,28},{28,24},{32,36},... | collective-permute-start | bytes 18874376 | tf_op jit(solution)/shard_map/ppermute | solution.py:68
  358.9 9.5 %collective-permute-done.64.other_outer = bf16[1,2,16,96,512]{4,3,2,1,0:T(8,128)(2,1)S(1)} collective-permute-done((bf16[1,2,16,96,512]{4,3,2,1,0:T(8,128)(2,1)S(1)}, bf16[1,2,16,96,512]{4,3,2,1,0:T(8,128)(2,1)S(1)}, u32[]{:S(2)}, u32[]{:S(2)}) %collective-permute-start.64) | collective-permute-done | bytes 3145760 | tf_op jit(solution)/shard_map/ppermute | solution.py:68
  370.0 12.8 %chip_sum.1 = (bf16[3,4,2,96,512]{4,3,2,1,0:T(8,128)(2,1)}, bf16[3,2,2,96,512]{4,3,2,1,0:T(8,128)(2,1)}, bf16[3,2,2,96,512]{4,3,2,1,0:T(8,128)(2,1)}, bf16[3,8,9...) custom-call(bf16[2,2,16,96,512]{4,3,2,1,0:T(8,128)(2,1)} %copy-done.21, ...), custom_call_target="tpu_custom_call" | custom-call | tf_op jit(solution)/shard_map/chip_sum/pallas_call | solution.py:705
  389.9 11.4 %attend_backward.1 = (bf16[512,640]{1,0:T(8,128)(2,1)}, bf16[4,2,64,1536]{3,2,1,0:T(8,128)(2,1)}) custom-call(s32[1]{0:T(128)} %bitcast.50.z_ref, bf16[1,256,2560]{2,1,0:T(8,128)(2,1)} %bitcast.340, bf16[1,256,2560]{2,1,0:T(8,128)(2,1)} %bitcast.349, bf16[1,256,2560]{2,1,0:T(8,128)(2,1)} %bitcast.341, bf16[1,256,2560]{2,1,0:T(8,128)(2,1)} %bitcast.350, ...), custom_call_target="tpu_custom_call" | custom-call | tf_op jit(solution)/shard_map/attend_backward/pallas_call | solution.py:522
  404.0 6.8 %dense_grad.1 = (bf16[1,8,2,48,1024]{4,3,2,1,0:T(8,128)(2,1)}, bf16[1,8,2,48,1024]{4,3,2,1,0:T(8,128)(2,1)}) custom-call(s32[3]{0:T(128)} %copy-done.51, s32[1]{0:T(128)} %bitcast.50.z_ref, bf16[256,1536]{1,0:T(8,128)(2,1)} %bitcast.368, bf16[256,1536]{1,0:T(8,128)(2,1)} %bitcast.369, bf16[256,1536]{1,0:T(8,128)(2,1)} %copy-done.47, ...), custom_call_target="tpu_custom_call" | custom-call | tf_op jit(solution)/shard_map/dense_grad/pallas_call | solution.py:751
  440.2 7.4 %collective-permute-done.70 = bf16[1,2,2,48,1024]{4,3,2,1,0:T(8,128)(2,1)} collective-permute-done((bf16[1,2,2,48,1024]{4,3,2,1,0:T(8,128)(2,1)S(1)}, bf16[1,2,2,48,1024]{4,3,2,1,0:T(8,128)(2,1)}, u32[]{:S(2)}, u32[]{:S(2)}) %collective-permute-start.70) | collective-permute-done | bytes 393248 | tf_op jit(solution)/shard_map/ppermute | solution.py:68
  486.9 7.4 %collective-permute-start.87 = (f32[2,1536]{1,0:T(2,128)S(1)}, f32[2,1536]{1,0:T(2,128)S(1)}, u32[]{:S(2)}, u32[]{:S(2)}) collective-permute-start(f32[2,1536]{1,0:T(2,128)S(1)} %add.464), channel_id=1, source_target_pairs={{0,4},{4,0},{8,12},{12,8},{16,20},{20,16},{24,28},{28,24},{32,36},... | collective-permute-start | bytes 36872 | tf_op jit(solution)/shard_map/ppermute | solution.py:120
  507.7 7.1 %collective-permute-done.94 = bf16[2,3,96,512]{3,2,0,1:T(8,128)(2,1)S(1)} collective-permute-done((bf16[2,3,96,512]{3,2,0,1:T(8,128)(2,1)S(1)}, bf16[2,3,96,512]{3,2,0,1:T(8,128)(2,1)S(1)}, u32[]{:S(2)}, u32[]{:S(2)}) %collective-permute-start.94) | collective-permute-done | bytes 589856 | tf_op jit(solution)/shard_map/ppermute | solution.py:68
  524.5 9.5 %collective-permute-done.100 = bf16[3,96,512]{2,1,0:T(8,128)(2,1)S(1)} collective-permute-done((bf16[3,96,512]{2,1,0:T(8,128)(2,1)}, bf16[3,96,512]{2,1,0:T(8,128)(2,1)S(1)}, u32[]{:S(2)}, u32[]{:S(2)}) %collective-permute-start.100) | collective-permute-done | bytes 294944 | tf_op jit(solution)/shard_map/ppermute | solution.py:68
  535.7 12.1 %collective-permute-start.102 = (bf16[4,2,2,4,48,512]{5,4,3,2,1,0:T(8,128)(2,1)S(1)}, bf16[4,2,2,4,48,512]{5,4,3,2,1,0:T(8,128)(2,1)S(1)}, u32[]{:S(2)}, u32[]{:S(2)}) collective-permute-start(bf16[4,2,2,4,48,512]{5,4,3,2,1,0:T(8,128)(2,1)S(1)} %pad_maximum_fusion.2.mine_ref), channel_id=1, source_target_pairs={{0,4},{4,0},{8,12},{12,8},{16,20},{20,16},{24,28},{28,24},{32,36},... | collective-permute-start | bytes 9437192 | tf_op jit(solution)/shard_map/ppermute | solution.py:68
  568.8 5.5 dense_layout.2
  575.6 7.4 %dense_layout.3 = (f32[4,2,2,2,48,1536]{5,4,3,2,1,0:T(8,128)}, f32[4,2,2,2,48,512]{5,4,3,2,1,0:T(8,128)}, f32[4,2,2,2,48,512]{5,4,3,2,1,0:T(8,128)}, f32[4,4,2,48,1536]{4,3,2,1,0:T(8,128)}) custom-call(s32[3]{0:T(128)S(1)} %copy-done.53, s32[1]{0:T(128)} %bitcast.50.z_ref, ...), custom_call_target="tpu_custom_call", output_to_operand_aliasing={{0}: (4, {}), {1}: (5, {}), {2}: (6, {}), {3}: (7, {})} | custom-call | bytes 37748736 | tf_op jit(solution)/shard_map/dense_layout/pallas_call | solution.py:807
  (648 shorter events, 300.5 us)
Async XLA Ops:
  7.2 129.8 %all-gather.3.cloned.1.call-start = ((), (), s32[]{:S(2)}) async-start(), calls=%async_computation.4 | async-start | bytes 1966080 | tf_op jit(solution)/shard_map/all_gather | solution.py:907
  37.8 37.0 %collective-permute-start.10 = (bf16[2,2,3,96,512]{4,3,2,1,0:T(8,128)(2,1)S(1)}, bf16[2,2,3,96,512]{4,3,2,1,0:T(8,128)(2,1)S(1)}, u32[]{:S(2)}, u32[]{:S(2)}) collective-permute-start(bf16[2,2,3,96,512]{4,3,2,1,0:T(8,128)(2,1)S(1)} %get-tuple-element.424), channel_id=1, source_target_pairs={{0,48},{4,52},{8,56},{12,60},{16,0},{20,4},{24,8},{28,12},{32,16},... | collective-permute-start | bytes 3538952 | tf_op jit(solution)/shard_map/ppermute | solution.py:68
  42.1 37.3 %collective-permute-start.13 = (bf16[3,2,3,96,512]{4,3,2,1,0:T(8,128)(2,1)}, bf16[3,2,3,96,512]{4,3,2,1,0:T(8,128)(2,1)}, u32[]{:S(2)}, u32[]{:S(2)}) collective-permute-start(bf16[3,2,3,96,512]{4,3,2,1,0:T(8,128)(2,1)} %pad_maximum_fusion.4.refs_2_), channel_id=1, source_target_pairs={{0,8},{4,12},{8,0},{12,4},{16,24},{20,28},{24,16},{28,20},{32,40},... | collective-permute-start | bytes 5308424 | tf_op jit(solution)/shard_map/ppermute | solution.py:68
  43.7 25.6 %collective-permute-start.12 = (bf16[3,96,512]{2,1,0:T(8,128)(2,1)S(1)}, bf16[3,96,512]{2,1,0:T(8,128)(2,1)S(1)}, u32[]{:S(2)}, u32[]{:S(2)}) collective-permute-start(bf16[3,96,512]{2,1,0:T(8,128)(2,1)S(1)} %slice_bitcast_fusion.14), channel_id=1, source_target_pairs={{0,48},{4,52},{8,56},{12,60},{16,0},{20,4},{24,8},{28,12},{32,16},... | collective-permute-start | bytes 884744 | tf_op jit(solution)/shard_map/ppermute | solution.py:68
  44.0 25.4 %collective-permute-start.11 = (bf16[3,96,512]{2,1,0:T(8,128)(2,1)S(1)}, bf16[3,96,512]{2,1,0:T(8,128)(2,1)S(1)}, u32[]{:S(2)}, u32[]{:S(2)}) collective-permute-start(bf16[3,96,512]{2,1,0:T(8,128)(2,1)S(1)} %slice_bitcast_fusion.15), channel_id=1, source_target_pairs={{0,16},{4,20},{8,24},{12,28},{16,32},{20,36},{24,40},{28,44},{32,4... | collective-permute-start | bytes 884744 | tf_op jit(solution)/shard_map/ppermute | solution.py:68
  45.4 29.3 %collective-permute-start.9 = (bf16[2,2,3,96,512]{4,3,2,0,1:T(8,128)(2,1)S(1)}, bf16[2,2,3,96,512]{4,3,2,0,1:T(8,128)(2,1)S(1)}, u32[]{:S(2)}, u32[]{:S(2)}) collective-permute-start(bf16[2,2,3,96,512]{4,3,2,0,1:T(8,128)(2,1)S(1)} %copy.182), channel_id=1, source_target_pairs={{0,16},{4,20},{8,24},{12,28},{16,32},{20,36},{24,40},{28,44},{32,4... | collective-permute-start | bytes 3538952 | tf_op jit(solution)/shard_map/ppermute | solution.py:68
  81.5 21.4 %collective-permute-start.17 = (bf16[3,2,2,3,96,512]{5,4,3,2,1,0:T(8,128)(2,1)}, bf16[3,2,2,3,96,512]{5,4,3,2,1,0:T(8,128)(2,1)}, u32[]{:S(2)}, u32[]{:S(2)}) collective-permute-start(bf16[3,2,2,3,96,512]{5,4,3,2,1,0:T(8,128)(2,1)} %pad_maximum_fusion.refs_0_), channel_id=1, source_target_pairs={{0,4},{4,0},{8,12},{12,8},{16,20},{20,16},{24,28},{28,24},{32,36},... | collective-permute-start | bytes 10616840 | tf_op jit(solution)/shard_map/ppermute | solution.py:68
  85.8 353.3 %reduce-scatter.3.cloned.1.call-start = ((), (), s32[]{:S(2)}) async-start(), calls=%async_computation.2 | async-start | bytes 1966080 | tf_op jit(solution)/shard_map/reduce_scatter | solution.py:968
  165.5 42.5 %collective-permute-start.36 = (bf16[1,64,1536]{2,1,0:T(8,128)(2,1)}, bf16[1,64,1536]{2,1,0:T(8,128)(2,1)}, u32[]{:S(2)}, u32[]{:S(2)}) collective-permute-start(bf16[1,64,1536]{2,1,0:T(8,128)(2,1)} %collective-permute-done.33), channel_id=1, source_target_pairs={{0,3},{1,0},{2,1},{3,2},{4,7},{5,4},{6,5},{7,6},{8,11},{9,8},{10,9... | collective-permute-start | bytes 589832 | tf_op jit(solution)/shard_map/ppermute | solution.py:38
  167.8 40.2 %collective-permute-start.35 = (bf16[1,64,1536]{2,1,0:T(8,128)(2,1)}, bf16[1,64,1536]{2,1,0:T(8,128)(2,1)}, u32[]{:S(2)}, u32[]{:S(2)}) collective-permute-start(bf16[1,64,1536]{2,1,0:T(8,128)(2,1)} %collective-permute-done.33), channel_id=1, source_target_pairs={{0,2},{1,3},{2,0},{3,1},{4,6},{5,7},{6,4},{7,5},{8,10},{9,11},{10,... | collective-permute-start | bytes 589832 | tf_op jit(solution)/shard_map/ppermute | solution.py:38
  169.1 38.9 %collective-permute-start.34 = (bf16[1,64,1536]{2,1,0:T(8,128)(2,1)}, bf16[1,64,1536]{2,1,0:T(8,128)(2,1)}, u32[]{:S(2)}, u32[]{:S(2)}) collective-permute-start(bf16[1,64,1536]{2,1,0:T(8,128)(2,1)} %collective-permute-done.33), channel_id=1, source_target_pairs={{0,1},{1,2},{2,3},{3,0},{4,5},{5,6},{6,7},{7,4},{8,9},{9,10},{10,1... | collective-permute-start | bytes 589832 | tf_op jit(solution)/shard_map/ppermute | solution.py:38
  210.3 35.6 %collective-permute-start.37 = (bf16[1,64,1536]{2,1,0:T(8,128)(2,1)}, bf16[1,64,1536]{2,1,0:T(8,128)(2,1)}, u32[]{:S(2)}, u32[]{:S(2)}) collective-permute-start(bf16[1,64,1536]{2,1,0:T(8,128)(2,1)} %get-tuple-element.247), channel_id=1, source_target_pairs={{0,3},{1,0},{2,1},{3,2},{4,7},{5,4},{6,5},{7,6},{8,11},{9,8},{10,9... | collective-permute-start | bytes 589832 | tf_op jit(solution)/shard_map/ppermute | solution.py:38
  210.3 36.4 %collective-permute-start.38 = (bf16[1,64,1536]{2,1,0:T(8,128)(2,1)}, bf16[1,64,1536]{2,1,0:T(8,128)(2,1)}, u32[]{:S(2)}, u32[]{:S(2)}) collective-permute-start(bf16[1,64,1536]{2,1,0:T(8,128)(2,1)} %get-tuple-element.248), channel_id=1, source_target_pairs={{0,2},{1,3},{2,0},{3,1},{4,6},{5,7},{6,4},{7,5},{8,10},{9,11},{10,... | collective-permute-start | bytes 589832 | tf_op jit(solution)/shard_map/ppermute | solution.py:38
  210.3 36.4 %collective-permute-start.39 = (bf16[1,64,1536]{2,1,0:T(8,128)(2,1)}, bf16[1,64,1536]{2,1,0:T(8,128)(2,1)}, u32[]{:S(2)}, u32[]{:S(2)}) collective-permute-start(bf16[1,64,1536]{2,1,0:T(8,128)(2,1)} %get-tuple-element.249), channel_id=1, source_target_pairs={{0,1},{1,2},{2,3},{3,0},{4,5},{5,6},{6,7},{7,4},{8,9},{9,10},{10,1... | collective-permute-start | bytes 589832 | tf_op jit(solution)/shard_map/ppermute | solution.py:38
  241.0 23.2 %collective-permute-start.43 = (bf16[1,64,1536]{2,1,0:T(8,128)(2,1)}, bf16[1,64,1536]{2,1,0:T(8,128)(2,1)S(1)}, u32[]{:S(2)}, u32[]{:S(2)}) collective-permute-start(bf16[1,64,1536]{2,1,0:T(8,128)(2,1)} %get-tuple-element.257), channel_id=1, source_target_pairs={{0,3},{1,0},{2,1},{3,2},{4,7},{5,4},{6,5},{7,6},{8,11},{9,8},{10,9... | collective-permute-start | bytes 589832 | tf_op jit(solution)/shard_map/ppermute | solution.py:38
  243.5 21.1 %collective-permute-start.44 = (bf16[1,64,1536]{2,1,0:T(8,128)(2,1)}, bf16[1,64,1536]{2,1,0:T(8,128)(2,1)S(1)}, u32[]{:S(2)}, u32[]{:S(2)}) collective-permute-start(bf16[1,64,1536]{2,1,0:T(8,128)(2,1)} %get-tuple-element.258), channel_id=1, source_target_pairs={{0,2},{1,3},{2,0},{3,1},{4,6},{5,7},{6,4},{7,5},{8,10},{9,11},{10,... | collective-permute-start | bytes 589832 | tf_op jit(solution)/shard_map/ppermute | solution.py:38
  325.2 20.1 %collective-permute-start.57 = (bf16[2,64,1536]{2,1,0:T(8,128)(2,1)S(1)}, bf16[2,64,1536]{2,1,0:T(8,128)(2,1)S(1)}, u32[]{:S(2)}, u32[]{:S(2)}) collective-permute-start(bf16[2,64,1536]{2,1,0:T(8,128)(2,1)S(1)} %get-tuple-element.282), channel_id=1, source_target_pairs={{0,3},{1,0},{2,1},{3,2},{4,7},{5,4},{6,5},{7,6},{8,11},{9,8},{10,9... | collective-permute-start | bytes 1179656 | tf_op jit(solution)/shard_map/ppermute | solution.py:38
  325.2 20.0 %collective-permute-start.58 = (bf16[2,64,1536]{2,1,0:T(8,128)(2,1)S(1)}, bf16[2,64,1536]{2,1,0:T(8,128)(2,1)S(1)}, u32[]{:S(2)}, u32[]{:S(2)}) collective-permute-start(bf16[2,64,1536]{2,1,0:T(8,128)(2,1)S(1)} %get-tuple-element.283), channel_id=1, source_target_pairs={{0,2},{1,3},{2,0},{3,1},{4,6},{5,7},{6,4},{7,5},{8,10},{9,11},{10,... | collective-permute-start | bytes 1179656 | tf_op jit(solution)/shard_map/ppermute | solution.py:38
  325.4 19.9 %collective-permute-start.59 = (bf16[2,64,1536]{2,1,0:T(8,128)(2,1)S(1)}, bf16[2,64,1536]{2,1,0:T(8,128)(2,1)S(1)}, u32[]{:S(2)}, u32[]{:S(2)}) collective-permute-start(bf16[2,64,1536]{2,1,0:T(8,128)(2,1)S(1)} %get-tuple-element.284), channel_id=1, source_target_pairs={{0,1},{1,2},{2,3},{3,0},{4,5},{5,6},{6,7},{7,4},{8,9},{9,10},{10,1... | collective-permute-start | bytes 1179656 | tf_op jit(solution)/shard_map/ppermute | solution.py:38
  347.9 20.7 %collective-permute-start.63 = (bf16[2,2,16,96,512]{4,3,2,1,0:T(8,128)(2,1)S(1)}, bf16[2,2,16,96,512]{4,3,2,1,0:T(8,128)(2,1)}, u32[]{:S(2)}, u32[]{:S(2)}) collective-permute-start(bf16[2,2,16,96,512]{4,3,2,1,0:T(8,128)(2,1)S(1)} %get-tuple-element.293), channel_id=1, source_target_pairs={{0,4},{4,0},{8,12},{12,8},{16,20},{20,16},{24,28},{28,24},{32,36},... | collective-permute-start | bytes 18874376 | tf_op jit(solution)/shard_map/ppermute | solution.py:68
  354.3 28.6 %collective-permute-start.62 = (bf16[2,64,1536]{2,1,0:T(8,128)(2,1)S(1)}, bf16[2,64,1536]{2,1,0:T(8,128)(2,1)S(1)}, u32[]{:S(2)}, u32[]{:S(2)}) collective-permute-start(bf16[2,64,1536]{2,1,0:T(8,128)(2,1)S(1)} %convert_element_type.458.refs_6_.refs_4_), channel_id=1, source_target_pairs={{0,3},{1,0},{2,1},{3,2},{4,7},{5,4},{6,5},{7,6},{8,11},{9,8},{10,9... | collective-permute-start | bytes 1179656 | tf_op jit(solution)/shard_map/ppermute | solution.py:38
  356.6 26.2 %collective-permute-start.61 = (bf16[2,64,1536]{2,1,0:T(8,128)(2,1)S(1)}, bf16[2,64,1536]{2,1,0:T(8,128)(2,1)S(1)}, u32[]{:S(2)}, u32[]{:S(2)}) collective-permute-start(bf16[2,64,1536]{2,1,0:T(8,128)(2,1)S(1)} %convert_element_type.458.refs_6_.refs_4_), channel_id=1, source_target_pairs={{0,2},{1,3},{2,0},{3,1},{4,6},{5,7},{6,4},{7,5},{8,10},{9,11},{10,... | collective-permute-start | bytes 1179656 | tf_op jit(solution)/shard_map/ppermute | solution.py:38
  358.2 24.7 %collective-permute-start.60 = (bf16[2,64,1536]{2,1,0:T(8,128)(2,1)S(1)}, bf16[2,64,1536]{2,1,0:T(8,128)(2,1)S(1)}, u32[]{:S(2)}, u32[]{:S(2)}) collective-permute-start(bf16[2,64,1536]{2,1,0:T(8,128)(2,1)S(1)} %convert_element_type.458.refs_6_.refs_4_), channel_id=1, source_target_pairs={{0,1},{1,2},{2,3},{3,0},{4,5},{5,6},{6,7},{7,4},{8,9},{9,10},{10,1... | collective-permute-start | bytes 1179656 | tf_op jit(solution)/shard_map/ppermute | solution.py:38
  386.9 27.9 %collective-permute-start.66 = (bf16[3,2,2,96,512]{4,3,0,2,1:T(8,128)(2,1)}, bf16[3,2,2,96,512]{4,3,0,2,1:T(8,128)(2,1)}, u32[]{:S(2)}, u32[]{:S(2)}) collective-permute-start(bf16[3,2,2,96,512]{4,3,0,2,1:T(8,128)(2,1)} %copy.189), channel_id=1, source_target_pairs={{0,48},{4,52},{8,56},{12,60},{16,0},{20,4},{24,8},{28,12},{32,16},... | collective-permute-start | bytes 3538952 | tf_op jit(solution)/shard_map/ppermute | solution.py:68
  389.3 28.6 %collective-permute-start.65 = (bf16[3,2,2,96,512]{4,3,0,2,1:T(8,128)(2,1)}, bf16[3,2,2,96,512]{4,3,0,2,1:T(8,128)(2,1)}, u32[]{:S(2)}, u32[]{:S(2)}) collective-permute-start(bf16[3,2,2,96,512]{4,3,0,2,1:T(8,128)(2,1)} %copy.188), channel_id=1, source_target_pairs={{0,16},{4,20},{8,24},{12,28},{16,32},{20,36},{24,40},{28,44},{32,4... | collective-permute-start | bytes 3538952 | tf_op jit(solution)/shard_map/ppermute | solution.py:68
  389.3 28.6 %collective-permute-start.67 = (bf16[3,4,96,512]{3,2,1,0:T(8,128)(2,1)}, bf16[3,4,96,512]{3,2,1,0:T(8,128)(2,1)}, u32[]{:S(2)}, u32[]{:S(2)}) collective-permute-start(bf16[3,4,96,512]{3,2,1,0:T(8,128)(2,1)} %get-tuple-element.309), channel_id=1, source_target_pairs={{0,8},{4,12},{8,0},{12,4},{16,24},{20,28},{24,16},{28,20},{32,40},... | collective-permute-start | bytes 3538952 | tf_op jit(solution)/shard_map/ppermute | solution.py:68
  401.3 116.3 %reduce-scatter.5.cloned.1.call-start = ((), (), s32[]{:S(2)}) async-start(), calls=%async_computation.3 | async-start | bytes 1966080 | tf_op jit(solution)/shard_map/reduce_scatter | solution.py:982
  403.1 69.9 %collective-permute-start.84 = (bf16[3,4,96,512]{3,2,1,0:T(8,128)(2,1)}, bf16[3,4,96,512]{3,2,1,0:T(8,128)(2,1)}, u32[]{:S(2)}, u32[]{:S(2)}) collective-permute-start(bf16[3,4,96,512]{3,2,1,0:T(8,128)(2,1)} %get-tuple-element.328), channel_id=1, source_target_pairs={{0,8},{4,12},{8,0},{12,4},{16,24},{20,28},{24,16},{28,20},{32,40},... | collective-permute-start | bytes 3538952 | tf_op jit(solution)/shard_map/ppermute | solution.py:68
  420.7 36.4 %collective-permute-start.75 = (bf16[3,2,96,512]{3,2,0,1:T(8,128)(2,1)}, bf16[3,2,96,512]{3,2,0,1:T(8,128)(2,1)}, u32[]{:S(2)}, u32[]{:S(2)}) collective-permute-start(bf16[3,2,96,512]{3,2,0,1:T(8,128)(2,1)} %get-tuple-element.400), channel_id=1, source_target_pairs={{0,48},{4,52},{8,56},{12,60},{16,0},{20,4},{24,8},{28,12},{32,16},... | collective-permute-start | bytes 1769480 | tf_op jit(solution)/shard_map/ppermute | solution.py:68
  422.0 35.1 %collective-permute-start.74 = (bf16[3,2,96,512]{3,2,0,1:T(8,128)(2,1)}, bf16[3,2,96,512]{3,2,0,1:T(8,128)(2,1)}, u32[]{:S(2)}, u32[]{:S(2)}) collective-permute-start(bf16[3,2,96,512]{3,2,0,1:T(8,128)(2,1)} %get-tuple-element.401), channel_id=1, source_target_pairs={{0,16},{4,20},{8,24},{12,28},{16,32},{20,36},{24,40},{28,44},{32,4... | collective-permute-start | bytes 1769480 | tf_op jit(solution)/shard_map/ppermute | solution.py:68
  535.7 19.5 %collective-permute-start.102 = (bf16[4,2,2,4,48,512]{5,4,3,2,1,0:T(8,128)(2,1)S(1)}, bf16[4,2,2,4,48,512]{5,4,3,2,1,0:T(8,128)(2,1)S(1)}, u32[]{:S(2)}, u32[]{:S(2)}) collective-permute-start(bf16[4,2,2,4,48,512]{5,4,3,2,1,0:T(8,128)(2,1)S(1)} %pad_maximum_fusion.2.mine_ref), channel_id=1, source_target_pairs={{0,4},{4,0},{8,12},{12,8},{16,20},{20,16},{24,28},{28,24},{32,36},... | collective-permute-start | bytes 9437192 | tf_op jit(solution)/shard_map/ppermute | solution.py:68
  555.2 20.3 %collective-permute-start.105 = (bf16[4,2,2,4,48,512]{5,4,3,2,1,0:T(8,128)(2,1)S(1)}, bf16[4,2,2,4,48,512]{5,4,3,2,1,0:T(8,128)(2,1)}, u32[]{:S(2)}, u32[]{:S(2)}) collective-permute-start(bf16[4,2,2,4,48,512]{5,4,3,2,1,0:T(8,128)(2,1)S(1)} %pad_maximum_fusion.1.mine_ref), channel_id=1, source_target_pairs={{0,4},{4,0},{8,12},{12,8},{16,20},{20,16},{24,28},{28,24},{32,36},... | collective-permute-start | bytes 9437192 | tf_op jit(solution)/shard_map/ppermute | solution.py:68
  (219 other events, 2172.6 us)
Sparse Core Ops, SparseCore 0:
  86.0 25.6 all-gather.2
  401.5 25.7 reduce-scatter.2
  451.0 23.3 reduce-scatter.4

commit v4 on v3

--- a/solution.py
+++ b/solution.py
@@ -51,8 +51,8 @@
     return [blocks[0]] + [shifted(blocks[j], size - j) for j in range(1, size)]
 
 
-def to_section(block, target):
-    return lax.ppermute(block, "section", [(1 - target, target)])
+def across(block):
+    return lax.ppermute(block, "section", [(0, 1), (1, 0)])
 
 
 RING, PAIR, CORES = 4, 2, 2
@@ -76,19 +76,17 @@
 
 
 def ring_step(blocks):
-    return moved(blocks[:, 3:5], x=1), moved(blocks[:, 5:7], x=-1)
-
-
-def ring_next(blocks, step):
-    from_below, from_above = step
-    below = moved(added(blocks[:, 2], from_below[:, 1]).astype(LOW), x=1)
-    above = moved(added(blocks[:, 7], from_above[:, 0]).astype(LOW), x=-1)
+    return moved(blocks[3:5], x=1), moved(blocks[5:7], x=-1)
+
+
+def ring_next(stays, step):
+    below = moved(added(stays[0], step[0][1]).astype(LOW), x=1)
+    above = moved(added(stays[1], step[1][0]).astype(LOW), x=-1)
     return below, above
 
 
-def ring_end(blocks, step, last):
-    first = added(blocks[:, 0], step[1][:, 1], last[0])
-    return jnp.stack([first, added(blocks[:, 1], step[0][:, 0], last[1])])
+def ring_end(stays, step, last):
+    return jnp.stack([added(stays[0], step[1][1], last[0]), added(stays[1], step[0][0], last[1])])
 
 
 def ring_gather_step(block):
@@ -97,23 +95,6 @@
 
 def ring_gather_next(step):
     return moved(step[0][0], x=1), moved(step[1][1], x=-1)
-
-
-def group_gather_step(block):
-    return shifted(block, 1), shifted(block, 3)
-
-
-def group_gather_next(step):
-    return shifted(step[0][0], 1), shifted(step[1][1], 3)
-
-
-def ring_stack(block, step, last):
-    return jnp.stack([block, step[0], jnp.stack(last), step[1]])
-
-
-def by_lanes(block):
-    lanes = block.shape[-1] // 2
-    return jnp.stack([block[..., :lanes], block[..., lanes:]])
 
 
 def exchanged(values, axis, bit):
@@ -679,14 +660,14 @@
 
     def add(mine, other, ring_first):
         for index in range(2 * RING * PAIR):
-            value = (mine[0, 0, index].astype(F32) + other[0, 0, index].astype(F32)).astype(LOW)
+            value = mine[0, 0, index] + other[0, 0, index]
             if ring_first:
                 ref, at = ring[index // PAIR]
-                ref[0, at, index % PAIR] = value
+                ref[at, index % PAIR, 0] = value
             elif index < 2 * RING:
-                keep_pair[0, index] = value
+                keep_pair[index, 0] = value
             else:
-                (to_pair if index < 3 * RING else to_pair_next)[0, index % RING] = value
+                (to_pair if index < 3 * RING else to_pair_next)[index % RING, 0] = value
 
     for inner in (True, False):
         for ring_first in (True, False):
@@ -706,8 +687,8 @@
         chip_sum_kernel,
         grid=(3, 2),
         in_specs=[inner_spec, inner_spec, outer_spec, outer_spec],
-        out_specs=[pl.BlockSpec((1,) + shape + tile, lambda m, k, n=len(shape) + 2: (m,) + (0,) * n) for shape in shapes],
-        out_shape=[jax.ShapeDtypeStruct((3,) + shape + tile, LOW) for shape in shapes],
+        out_specs=[pl.BlockSpec(shape + (1,) + tile, lambda m, k, n=len(shape): (0,) * n + (m, 0, 0)) for shape in shapes],
+        out_shape=[jax.ShapeDtypeStruct(shape + (3,) + tile, LOW) for shape in shapes],
         compiler_params=params("arbitrary", "arbitrary", mib=56),
         name="chip_sum",
     )(*inner, *outer)
@@ -736,8 +717,8 @@
             for y in range(PAIR):
                 owner = chip_block(place_ref, x, y, core)
                 for half in range(2):
-                    ref[0, x * 2 + half, y, :, :wide] = into_ref[owner, half]
-                    ref[0, x * 2 + half, y, :, wide:] = out_of_ref[owner, half]
+                    ref[x * 2 + half, y, :, :wide] = into_ref[owner, half]
+                    ref[x * 2 + half, y, :, wide:] = out_of_ref[owner, half]
 
 
 def dense_grad(place, z, mixed, da, xn, dqkv, parts):
@@ -746,7 +727,7 @@
     owners = RING * PAIR * CORES
     q_lanes, wide = mixed[0].shape[1] // parts, dqkv.shape[1]
     high, lanes = width // owners // 2, width // CORES // 2
-    shape = (1, 2 * RING, PAIR, high, wide + lanes)
+    shape = (2 * RING, PAIR, high, wide + lanes)
     whole = lambda *shape: pl.BlockSpec(shape, lambda i, p, z: (0,) * len(shape))
     return pl.pallas_call(
         functools.partial(dense_grad_kernel, batches, parts),
@@ -757,7 +738,7 @@
             + [whole(rows, width)] * batches
             + [whole(*da[0].shape)] * parts
             + [whole(*dqkv.shape)],
-            out_specs=[pl.BlockSpec(shape, lambda i, p, z: (0,) * 5)] * 2,
+            out_specs=[pl.BlockSpec(shape, lambda i, p, z: (0,) * 4)] * 2,
             scratch_shapes=[pltpu.VMEM((owners, 2, high, wide), LOW), pltpu.VMEM((owners, 2, high, lanes), LOW)],
         ),
         out_shape=[jax.ShapeDtypeStruct(shape, LOW)] * 2,
@@ -768,8 +749,7 @@
 
 def dense_layout_kernel(by_x, place_ref, z_ref, mine_ref, other_ref, *refs):
     outs = refs[-4:]
-    parts = mine_ref.shape[3] if by_x else mine_ref.shape[0]
-    wide = mine_ref.shape[-1]
+    parts = mine_ref.shape[2] if by_x else mine_ref.shape[0]
     for core, ref in enumerate((mine_ref, other_ref)):
         to_core = lax.rem(place_ref[2] + core, CORES)
         for y in range(PAIR):
@@ -780,9 +760,8 @@
                 for out in outs:
                     to_rows = out is outs[3]
                     lanes = out.shape[-1] // (CORES if to_rows else parts)
-                    by, begin = divmod(start, wide)
-                    index = (0, by, y, k) if by_x else (k, by, y, 0)
-                    value = ref[index + (slice(None), slice(begin, begin + lanes))].astype(F32)
+                    index = (0, y, k) if by_x else (k, y, 0)
+                    value = ref[index + (slice(None), slice(start, start + lanes))].astype(F32)
                     if to_rows:
                         out[at, 0, to_y, :, pl.ds(pl.multiple_of(to_core * lanes, 128), lanes)] = value
                     else:
@@ -793,11 +772,11 @@
 def dense_layout(place, z, half, mine, other, shapes, before):
     by_x = half == 0
     high, lanes = mine.shape[-2:]
-    parts = mine.shape[3] if by_x else mine.shape[0]
+    parts = mine.shape[2] if by_x else mine.shape[0]
     if by_x:
-        source = pl.BlockSpec((1, 2, PAIR, parts, high, lanes), lambda x, p, z: (x, 0, 0, 0, 0, 0))
+        source = pl.BlockSpec((1, PAIR, parts, high, lanes), lambda x, p, z: (x, 0, 0, 0, 0))
     else:
-        source = pl.BlockSpec((parts, 2, PAIR, 1, high, lanes), lambda x, p, z: (0, 0, 0, x, 0, 0))
+        source = pl.BlockSpec((parts, PAIR, 1, high, lanes), lambda x, p, z: (0, 0, x, 0, 0))
     ring = lambda x, p: lax.rem(p[0] + RING - x, RING)
     width = shapes[3][1]
     shapes = [(RING, PAIR, CORES, 2, high, shape[1]) for shape in shapes[:3]] + [(parts, RING, PAIR, high, width)]
@@ -914,7 +893,7 @@
         if b > 0:
             came = once(came, result)
         result = (h1[b : b + 1] + added(*came)).astype(LOW)
-        received.append(spread_group(to_section(result, 1)))
+        received.append(spread_group(across(result)))
 
     biases = [bias[b : b + 1] for b in range(batches)]
     x, qkv, xn, mixed, h1, xn2, hidden, to_up, to_gate, blocks = ([None] * batches for _ in range(10))
@@ -944,7 +923,7 @@
         dn_own = dot_nt(dq[b].reshape(own, -1), wq)
         dn_own = dn_own + dot_nt(dkv[:, : wk.shape[1]], wk) + dot_nt(dkv[:, wk.shape[1] :], wv)
         input_grad = after[b] + norm_back(dn_own[None], x_own[b : b + 1], attn_gain)[0]
-        received_own.append(to_section(input_grad.astype(LOW), 0))
+        received_own.append(across(input_grad.astype(LOW)))
 
     c_own = jnp.where(section == 1, out_grad, jnp.concatenate(received_own, 0))
     c = [jnp.where(section == 1, c_second[b : b + 1], gather_group(received_own[b])).reshape(rows, width) for b in range(batches)]
@@ -958,6 +937,10 @@
     after, both = hold(after, both)
     inner, outer = [(mine, moved(other, core=1)) for mine, other in both]
     da = spread_group(after.astype(LOW))
+    outputs = [dot(units_of, wd.reshape(local_experts * units, width)).astype(LOW) for units_of in once(hidden, inner[1])]
+    outputs = jnp.stack(outputs).reshape(batches, parts, own, width)
+    outputs = jnp.stack([lax.dynamic_index_in_dim(outputs, (z + parts - i) % parts, 1, False) for i in range(parts)])
+    outer, outputs = hold(outer, outputs)
     keep_ring, to_above, to_below, keep_pair, *to_pair = chip_sum(inner, outer)
     da, to_above, to_below, to_pair = hold(da, to_above, to_below, to_pair)
 
@@ -966,85 +949,71 @@
     dqkv, dn = attend_backward(z_at, qkv, da, wo, wq, wk, wv, bias, cos, sin, parts)
     mine, other = dense_grad(dp_place, z_at, mixed, da, xn, dqkv, parts)
     dn_own = lax.psum_scatter(dn, "expert", scatter_dimension=0, tiled=True)[0].astype(F32)
-
     mine, other, ring_1, pair_1[0] = hold(mine, other, ring_1, pair_1[0])
-    other = moved(other, core=1)
-    outputs = jnp.stack([dot(units_of, wd.reshape(local_experts * units, width)).astype(LOW) for units_of in once(hidden, mine)])
-    other = once(other, outputs)
-    dense = added(mine, other).astype(LOW)
+    dense = added(mine, moved(other, core=1)).astype(LOW)
 
     (dense,) = hold(dense)
     dense_1 = ring_step(dense)
-    outputs = outputs.reshape(batches, parts, own, width)
-    outputs = jnp.stack([lax.dynamic_index_in_dim(outputs, (z + parts - i) % parts, 1, False) for i in range(parts)])
-
-    dense_1, outputs, dn_own = hold(dense_1, outputs, dn_own)
+
+    dense_1, outputs, dn_own, ring_1 = hold(dense_1, outputs, dn_own, ring_1)
     outputs = lax.psum_scatter(outputs, "expert", scatter_dimension=0, tiled=True)[0]
-    dense_2 = ring_next(dense, dense_1)
+    dense_2 = ring_next((dense[2], dense[7]), dense_1)
     norm_part, attn_grad = norm_back(dn_own, x_own, attn_gain)
     input_grad = after + norm_part
     gains = jnp.stack([attn_grad, ffn_grad])
     gains = gains + exchanged(gains, "expert", 1)
-    ring_2 = (
-        moved(added(keep_ring[:, 2], ring_1[0][:, 1]).astype(LOW), x=1),
-        moved(added(keep_ring[:, 3], ring_1[1][:, 0]).astype(LOW), x=-1),
-    )
-
-    dense_2, gains, ring_2 = hold(dense_2, gains, ring_2)
-    dense = ring_end(dense, dense_1, dense_2)[:, 0]
+    ring_2 = ring_next((keep_ring[2], keep_ring[3]), ring_1)
+
+    dense_2, gains, pair_1 = hold(dense_2, gains, pair_1)
+    dense = ring_end(dense, dense_1, dense_2)
     dense_3 = moved(dense[:, 1].astype(LOW), y=1)
+    pair_sums = added(keep_pair, jnp.concatenate(pair_1, 0)).astype(LOW)
+    pair_2 = ring_step(pair_sums)
     gains = gains + exchanged(gains, "expert", 2)
-    ring_sums = jnp.stack(
-        [
-            added(keep_ring[:, 0], ring_1[1][:, 1], ring_2[0]),
-            added(keep_ring[:, 1], ring_1[0][:, 0], ring_2[1]),
-        ]
-    )
-
-    dense_3, gains, ring_sums = hold(dense_3, gains, ring_sums)
-    owned = added(dense[:, 0], dense_3).astype(LOW)
-    first, second = owned[0], by_lanes(owned[1])
+
+    dense_3, gains, ring_2, pair_2 = hold(dense_3, gains, ring_2, pair_2)
+    ring_sums = ring_end(keep_ring, ring_1, ring_2)
+    first, second = (added(dense[half, 0], dense_3[half]).astype(LOW) for half in range(2))
     first_1 = [shifted(first, k) for k in range(1, parts)]
     second_1 = [moved(second, x=k) for k in range(1, RING)]
 
-    first_1, second_1, pair_1 = hold(first_1, second_1, pair_1)
-    pair_sums = added(keep_pair, jnp.concatenate(pair_1, 1)).astype(LOW)
+    first_1, second_1 = hold(first_1, second_1)
     first = jnp.stack([first] + first_1)
     first_2 = moved(first, y=1)
     second = jnp.stack([second] + second_1)
     second_2 = moved(second, y=1)
-    pair_2 = ring_step(pair_sums)
+    pair_3 = ring_next((pair_sums[2], pair_sums[7]), pair_2)
     gains = gains + exchanged(gains, "dp", 1)
 
-    first_2, second_2, gains, pair_2 = hold(first_2, second_2, gains, pair_2)
-    first = by_lanes(jnp.stack([first, first_2]))
-    first_3 = ring_gather_step(first)
-    second = jnp.moveaxis(jnp.stack([second, second_2]), 2, 0)
-    second_3 = group_gather_step(second)
-    ring_away = moved(ring_sums[:, :, 1].astype(LOW), y=1)
+    first_2, second_2, gains, pair_3 = hold(first_2, second_2, gains, pair_3)
+    first = jnp.stack([first, first_2])
+    first_3 = moved(first, x=1), moved(first, x=-1)
+    second = jnp.stack([second, second_2])
+    second_3 = shifted(second, 1), shifted(second, parts - 1)
+    ring_away = moved(ring_sums[:, 1].astype(LOW), y=1)
+
+    first_3, second_3, ring_away, gains = hold(first_3, second_3, ring_away, gains)
+    first_4, second_4 = moved(first, x=2), shifted(second, 2)
     gains = gains + exchanged(gains, "dp", 2)
-
-    first_3, second_3, ring_away, gains, outputs = hold(first_3, second_3, ring_away, gains, outputs)
-    first_4 = ring_gather_next(first_3)
-    second_4 = group_gather_next(second_3)
-    pair_3 = ring_next(pair_sums, pair_2)
-    ring_sums = added(ring_sums[:, :, 0], ring_away)
-
-    first_4, second_4, pair_3, ring_sums = hold(first_4, second_4, pair_3, ring_sums)
-    first = ring_stack(first, first_3, first_4)
+    ring_sums = added(ring_sums[:, 0], ring_away)
+    pair_sums = ring_end(pair_sums, pair_2, pair_3)
+    w_gate_grad, w_up_grad, w_down_grad = (jnp.concatenate([ring_sums[:, i], pair_sums[:, i]], 0) for i in range(3))
+    w_down_grad = w_down_grad.reshape(local_experts, width // units, -1, units)
+    w_down_grad = jnp.swapaxes(w_down_grad, 1, 2).reshape(local_experts, -1, width)
+
+    first_4, second_4, w_gate_grad, w_up_grad, w_down_grad, gains, outputs = hold(
+        first_4, second_4, w_gate_grad, w_up_grad, w_down_grad, gains, outputs
+    )
+    first = jnp.stack([first, first_3[0], first_4, first_3[1]])
     first_other = moved(first, core=1)
-    pair_sums = ring_end(pair_sums, pair_2, pair_3)
     gains = gains + exchanged(gains, "dp", 4)
 
-    second = ring_stack(second, second_3, second_4)
-    second, first_other, gains, pair_sums = hold(second, first_other, gains, pair_sums)
+    second = jnp.stack([second, second_3[0], second_4, second_3[1]])
+    second, first_other, gains = hold(second, first_other, gains)
     second_other = moved(second, core=1)
     shapes = (wq.shape, wk.shape, wv.shape, wo.shape)
     laid = dense_layout(dp_place, z_at, 0, first, first_other, shapes, ())
     gains = gains + exchanged(gains, "dp", 8)
-    w_gate_grad, w_up_grad, w_down_grad = (jnp.concatenate([ring_sums[:, i], pair_sums[:, i]], 0) for i in range(3))
-    w_down_grad = w_down_grad.reshape(local_experts, width // units, -1, units)
-    w_down_grad = jnp.swapaxes(w_down_grad, 1, 2).reshape(local_experts, -1, width)
 
     second_other, laid = hold(second_other, laid)
     laid = dense_layout(dp_place, z_at, 1, second, second_other, shapes, laid)

time: 597 us -> 583 us (0.977)
  waiting for transfers between devices: 128 us -> 145 us
  local copies, waits for them, and re-layouts: 48.9 us -> 34.2 us
  starting transfers between devices: 141 us -> 132 us
    ppermute x49 -> x48, waiting for transfers between devices: 37.1 us -> 49.7 us  [shifted(): lax.ppermute(block, 'expert', [(i, (i + by) % size) for i in range(size)])]
    ppermute x47 -> x46, waiting for transfers between devices: 79.4 us -> 87.5 us  [moved(): return lax.ppermute(block, 'dp', route)]
    unnamed x290 -> x300, local copies, waits for them, and re-layouts: 30.1 us -> 22.8 us
    ppermute x4, starting transfers between devices: 13 us -> 6.25 us  [across(): return lax.ppermute(block, 'section', [(0, 1), (1, 0)])]
    ppermute x47 -> x46, starting transfers between devices: 65.1 us -> 61.2 us  [moved(): return lax.ppermute(block, 'dp', route)]
    ppermute x49 -> x48, starting transfers between devices: 50.9 us -> 50.6 us  [shifted(): lax.ppermute(block, 'expert', [(i, (i + by) % size) for i in range(size)])]
  transfers between devices with their start and end apart: 109 -> 107, of which waited for: 42 -> 47; matrix products, arithmetic and copies ran while one was open for 13% -> 11% of each run, Pallas kernels for 28% -> 28%
where the time goes in v4:
time: 583 us; the launch traced here: 576 us
  Pallas kernels  184 us (32%)
  waiting for transfers between devices  145 us (25%)
  starting transfers between devices  132 us (23%)
  other arithmetic  54.8 us (9%)
  local copies, waits for them, and re-layouts  34.2 us (6%)
  between operations  16.4 us (3%)
  matrix products  9.24 us (2%)
    ppermute x46, waiting for transfers between devices, moved(): return lax.ppermute(block, 'dp', route)  87.5 us
    ppermute x46, starting transfers between devices, moved(): return lax.ppermute(block, 'dp', route)  61.2 us
    ppermute x48, starting transfers between devices, shifted(): lax.ppermute(block, 'expert', [(i, (i + by) % size) for i in range(size)])  50.6 us
    ppermute x48, waiting for transfers between devices, shifted(): lax.ppermute(block, 'expert', [(i, (i + by) % size) for i in range(size)])  49.7 us
    pallas_call x2, Pallas kernels, experts_turn(): pl.pallas_call(experts_turn_kernel, grid=(count,), in_specs=[pl.BlockSpec...  29.7 us
    unnamed x300, local copies, waits for them, and re-layouts  22.8 us
    pallas_call x1, Pallas kernels, experts_forward(): pl.pallas_call(experts_forward_kernel, grid_spec=pltpu.PrefetchScalarGrid...  20.5 us
    pallas_call x3, Pallas kernels, attend(): pl.pallas_call(attend_kernel, grid=(batches, parts), in_specs=[pl.BlockSp...  19.2 us
  transfers between devices with their start and end apart: 107, of which 47 were waited for; matrix products, arithmetic and copies ran while one was open for 11% of the time, Pallas kernels for 28%

profile of v4, /device:TPU:1, one launch (start us, length us, event | category | flops | bytes accessed | tf_op | source)
XLA Modules:
  0.0 575.9 jit_solution(7591646348951722117)
XLA Ops:
  47.0 9.2 %project.3 = (bf16[512,2560]{1,0:T(8,128)(2,1)S(1)}, bf16[512,1536]{1,0:T(8,128)(2,1)}) custom-call(bf16[512,1536]{1,0:T(8,128)(2,1)S(1)} %bitcast.324, f32[1,1536]{1,0:T(1,128)S(1)} %copy-done.45, bf16[1536,1536]{1,0:T(8,128)(2,1)S(1)} %bitcast.278, bf16[1536,512]{1,0:T(8,128)(2,1)S(1)} %bitcast.314, bf16[1536,512]{1,0:T(8,128)(2,1)S(1)} %bitcast.318, ...), custom_call_target="tpu_custom_call" | custom-call | tf_op jit(solution)/shard_map/project/pallas_call | solution.py:158
  56.4 9.6 %attend.3.o_ref = bf16[2,256,1536]{2,1,0:T(8,128)(2,1)S(1)} custom-call(bf16[2,256,2560]{2,1,0:T(8,128)(2,1)S(1)} %bitcast.321, bf16[2,256,2560]{2,1,0:T(8,128)(2,1)S(1)} %bitcast.322, bf16[2,256,2560]{2,1,0:T(8,128)(2,1)S(1)} %bitcast.323, f32[2,256,256]{2,1,0:T(8,128)S(1)} %and_select_fusion.bias_ref.refs_14_), custom_call_target="tpu_custom_call" | custom-call | tf_op jit(solution)/shard_map/attend/pallas_call | solution.py:209
  69.4 5.3 collective-permute-done.9
  94.8 5.8 %collective-permute-done.15 = bf16[2,3,96,512]{3,2,1,0:T(8,128)(2,1)S(1)} collective-permute-done((bf16[2,3,96,512]{3,2,1,0:T(8,128)(2,1)S(1)}, bf16[2,3,96,512]{3,2,1,0:T(8,128)(2,1)S(1)}, u32[]{:S(2)}, u32[]{:S(2)}) %collective-permute-start.15) | collective-permute-done | bytes 589856 | tf_op jit(solution)/shard_map/ppermute | solution.py:68
  111.7 20.5 %experts_forward.1 = (bf16[1,64,1536]{2,1,0:T(8,128)(2,1)S(1)}, bf16[1,64,1536]{2,1,0:T(8,128)(2,1)}, bf16[1,64,1536]{2,1,0:T(8,128)(2,1)}, bf16[1,64,1536]{2,1,...) custom-call(s32[3]{0:T(128)S(1)} %pad_add_fusion.place_ref, ...), custom_call_target="tpu_custom_call" | custom-call | tf_op jit(solution)/shard_map/experts_forward/pallas_call | solution.py:333
  144.0 5.2 collective-permute-done.25
  167.8 6.4 %collective-permute-done.27 = bf16[1,64,1536]{2,1,0:T(8,128)(2,1)S(1)} collective-permute-done((bf16[1,64,1536]{2,1,0:T(8,128)(2,1)S(1)}, bf16[1,64,1536]{2,1,0:T(8,128)(2,1)S(1)}, u32[]{:S(2)}, u32[]{:S(2)}) %collective-permute-start.27) | collective-permute-done | bytes 196640 | tf_op jit(solution)/shard_map/ppermute | solution.py:38
  177.5 4.8 project.4
  190.4 15.0 %experts_turn.2 = (bf16[256,2048]{1,0:T(8,128)(2,1)}, bf16[256,2048]{1,0:T(8,128)(2,1)}, bf16[256,2048]{1,0:T(8,128)(2,1)}, bf16[1,64,1536]{2,1,0:T(8,128)(2,1)}...) custom-call(bf16[256,1536]{1,0:T(8,128)(2,1)} %bitcast.331, ...), custom_call_target="tpu_custom_call" | custom-call | tf_op jit(solution)/shard_map/experts_turn/pallas_call | solution.py:383
  210.8 4.8 project.5
  223.7 14.7 %experts_turn.3 = (bf16[256,2048]{1,0:T(8,128)(2,1)}, bf16[256,2048]{1,0:T(8,128)(2,1)}, bf16[256,2048]{1,0:T(8,128)(2,1)}, bf16[1,64,1536]{2,1,0:T(8,128)(2,1)}...) custom-call(bf16[256,1536]{1,0:T(8,128)(2,1)} %bitcast.333, ...), custom_call_target="tpu_custom_call" | custom-call | tf_op jit(solution)/shard_map/experts_turn/pallas_call | solution.py:383
  249.4 8.1 %own_backward.2 = (bf16[1,64,1536]{2,1,0:T(8,128)(2,1)S(1)}, bf16[1,64,1024]{2,1,0:T(8,128)(2,1)S(1)}, bf16[1,64,1024]{2,1,0:T(8,128)(2,1)S(1)}, bf16[1,64,1024]...) custom-call(bf16[1,256,2560]{2,1,0:T(8,128)(2,1)S(1)} %bitcast.298, bf16[1,256,2560]{2,1,0:T(8,128)(2,1)S(1)} %bitcast.299, ...), custom_call_target="tpu_custom_call" | custom-call | tf_op jit(solution)/shard_map/own_backward/pallas_call | solution.py:559
  262.6 8.2 %own_backward.3 = (bf16[1,64,1536]{2,1,0:T(8,128)(2,1)S(1)}, bf16[1,64,1024]{2,1,0:T(8,128)(2,1)S(1)}, bf16[1,64,1024]{2,1,0:T(8,128)(2,1)S(1)}, bf16[1,64,1024]...) custom-call(bf16[1,256,2560]{2,1,0:T(8,128)(2,1)S(1)} %bitcast.307, bf16[1,256,2560]{2,1,0:T(8,128)(2,1)S(1)} %bitcast.308, ...), custom_call_target="tpu_custom_call" | custom-call | tf_op jit(solution)/shard_map/own_backward/pallas_call | solution.py:559
  297.1 5.5 collective-permute-done.54
  305.8 14.9 %experts_backward.1 = (bf16[2,64,1536]{2,1,0:T(8,128)(2,1)S(1)}, bf16[2,64,1536]{2,1,0:T(8,128)(2,1)S(1)}, bf16[2,64,1536]{2,1,0:T(8,128)(2,1)S(1)}, bf16[2,64,1...) custom-call(bf16[256,1536]{1,0:T(8,128)(2,1)S(1)} %bitcast.328, bf16[256,1536]{1,0:T(8,128)(2,1)S(1)} %bitcast.327, ...), custom_call_target="tpu_custom_call" | custom-call | tf_op jit(solution)/shard_map/experts_backward/pallas_call | solution.py:423
  322.8 5.5 expert_grad.3
  330.0 10.7 %expert_grad.2 = (bf16[2,2,16,96,512]{4,3,2,1,0:T(8,128)(2,1)S(1)}, bf16[2,2,16,96,512]{4,3,2,1,0:T(8,128)(2,1)S(1)}) custom-call(s32[3]{0:T(128)S(1)} %copy-done.48, bf16[256,1536]{1,0:T(8,128)(2,1)S(1)} %bitcast.332, bf16[256,1536]{1,0:T(8,128)(2,1)S(1)} %bitcast.334, bf16[2,512,2048]{2,1,0:T(8,128)(2,1)S(1)} %get-tuple-element.289.refs_2_), custom_call_target="tpu_custom_call" | custom-call | tf_op jit(solution)/shard_map/expert_grad/pallas_call | solution.py:639
  343.5 6.3 %collective-permute-start.63 = (bf16[2,2,16,96,512]{4,3,2,1,0:T(8,128)(2,1)S(1)}, bf16[2,2,16,96,512]{4,3,2,1,0:T(8,128)(2,1)S(1)}, u32[]{:S(2)}, u32[]{:S(2)}) collective-permute-start(bf16[2,2,16,96,512]{4,3,2,1,0:T(8,128)(2,1)S(1)} %get-tuple-element.297), channel_id=1, source_target_pairs={{0,4},{4,0},{8,12},{12,8},{16,20},{20,16},{24,28},{28,24},{32,36},... | collective-permute-start | bytes 18874376 | tf_op jit(solution)/shard_map/ppermute | solution.py:68
  354.5 9.6 %collective-permute-done.63.other_inner = bf16[2,2,16,96,512]{4,3,2,1,0:T(8,128)(2,1)S(1)} collective-permute-done((bf16[2,2,16,96,512]{4,3,2,1,0:T(8,128)(2,1)S(1)}, bf16[2,2,16,96,512]{4,3,2,1,0:T(8,128)(2,1)S(1)}, u32[]{:S(2)}, u32[]{:S(2)}) %collective-permute-start.63) | collective-permute-done | bytes 6291488 | tf_op jit(solution)/shard_map/ppermute | solution.py:68
  370.1 12.2 %chip_sum.1 = (bf16[4,2,3,96,512]{4,3,2,1,0:T(8,128)(2,1)}, bf16[2,2,3,96,512]{4,3,2,1,0:T(8,128)(2,1)}, bf16[2,2,3,96,512]{4,3,2,1,0:T(8,128)(2,1)}, bf16[8,3,9...) custom-call(bf16[2,2,16,96,512]{4,3,2,1,0:T(8,128)(2,1)} %copy-done.19, ...), custom_call_target="tpu_custom_call" | custom-call | tf_op jit(solution)/shard_map/chip_sum/pallas_call | solution.py:686
  385.7 11.4 %attend_backward.1 = (bf16[512,640]{1,0:T(8,128)(2,1)}, bf16[4,2,64,1536]{3,2,1,0:T(8,128)(2,1)}) custom-call(s32[1]{0:T(128)} %bitcast.50.z_ref, bf16[1,256,2560]{2,1,0:T(8,128)(2,1)} %bitcast.301, bf16[1,256,2560]{2,1,0:T(8,128)(2,1)} %bitcast.310, bf16[1,256,2560]{2,1,0:T(8,128)(2,1)} %bitcast.302, bf16[1,256,2560]{2,1,0:T(8,128)(2,1)} %bitcast.311, ...), custom_call_target="tpu_custom_call" | custom-call | tf_op jit(solution)/shard_map/attend_backward/pallas_call | solution.py:503
  397.2 6.8 %dense_grad.1 = (bf16[8,2,48,1024]{3,2,1,0:T(8,128)(2,1)}, bf16[8,2,48,1024]{3,2,1,0:T(8,128)(2,1)}) custom-call(s32[3]{0:T(128)} %copy-done.47, s32[1]{0:T(128)} %bitcast.50.z_ref, bf16[256,1536]{1,0:T(8,128)(2,1)} %bitcast.329, bf16[256,1536]{1,0:T(8,128)(2,1)} %bitcast.330, bf16[256,1536]{1,0:T(8,128)(2,1)} %copy-done.43, bf16[256,1536]{1,0:T(8,128)(2,1)} %copy-done.44, ...), custom_call_target="tpu_custom_call" | custom-call | tf_op jit(solution)/shard_map/dense_grad/pallas_call | solution.py:732
  404.0 7.1 %collective-permute-done.65 = bf16[2,2,3,96,512]{4,3,2,1,0:T(8,128)(2,1)S(1)} collective-permute-done((bf16[2,2,3,96,512]{4,3,2,1,0:T(8,128)(2,1)}, bf16[2,2,3,96,512]{4,3,2,1,0:T(8,128)(2,1)S(1)}, u32[]{:S(2)}, u32[]{:S(2)}) %collective-permute-start.65) | collective-permute-done | bytes 1179680 | tf_op jit(solution)/shard_map/ppermute | solution.py:68
  423.0 7.9 %collective-permute-done.70 = bf16[2,2,48,1024]{3,2,1,0:T(8,128)(2,1)S(1)} collective-permute-done((bf16[2,2,48,1024]{3,2,1,0:T(8,128)(2,1)}, bf16[2,2,48,1024]{3,2,1,0:T(8,128)(2,1)S(1)}, u32[]{:S(2)}, u32[]{:S(2)}) %collective-permute-start.70) | collective-permute-done | bytes 393248 | tf_op jit(solution)/shard_map/ppermute | solution.py:68
  456.7 10.6 %collective-permute-done.80 = bf16[2,3,96,512]{3,2,1,0:T(8,128)(2,1)S(1)} collective-permute-done((bf16[2,3,96,512]{3,2,1,0:T(8,128)(2,1)S(1)}, bf16[2,3,96,512]{3,2,1,0:T(8,128)(2,1)S(1)}, u32[]{:S(2)}, u32[]{:S(2)}) %collective-permute-start.80) | collective-permute-done | bytes 589856 | tf_op jit(solution)/shard_map/ppermute | solution.py:68
  485.5 7.4 %collective-permute-start.89 = (f32[2,1536]{1,0:T(2,128)S(1)}, f32[2,1536]{1,0:T(2,128)S(1)}, u32[]{:S(2)}, u32[]{:S(2)}) collective-permute-start(f32[2,1536]{1,0:T(2,128)S(1)} %copy-done.131), channel_id=1, source_target_pairs={{0,4},{4,0},{8,12},{12,8},{16,20},{20,16},{24,28},{28,24},{32,36},... | collective-permute-start | bytes 36872 | tf_op jit(solution)/shard_map/ppermute | solution.py:101
  503.7 8.4 %collective-permute-done.98 = bf16[2,3,96,512]{3,2,0,1:T(8,128)(2,1)S(1)} collective-permute-done((bf16[2,3,96,512]{3,2,0,1:T(8,128)(2,1)S(1)}, bf16[2,3,96,512]{3,2,0,1:T(8,128)(2,1)S(1)}, u32[]{:S(2)}, u32[]{:S(2)}) %collective-permute-start.98) | collective-permute-done | bytes 589856 | tf_op jit(solution)/shard_map/ppermute | solution.py:68
  522.5 6.5 %collective-permute-done.92 = bf16[2,4,48,1024]{3,2,1,0:T(8,128)(2,1)} collective-permute-done((bf16[2,4,48,1024]{3,2,1,0:T(8,128)(2,1)}, bf16[2,4,48,1024]{3,2,1,0:T(8,128)(2,1)}, u32[]{:S(2)}, u32[]{:S(2)}) %collective-permute-start.92) | collective-permute-done | bytes 786464 | tf_op jit(solution)/shard_map/ppermute | solution.py:68
  529.0 6.2 %collective-permute-done.93 = bf16[2,4,48,1024]{3,2,1,0:T(8,128)(2,1)} collective-permute-done((bf16[2,4,48,1024]{3,2,1,0:T(8,128)(2,1)}, bf16[2,4,48,1024]{3,2,1,0:T(8,128)(2,1)}, u32[]{:S(2)}, u32[]{:S(2)}) %collective-permute-start.93) | collective-permute-done | bytes 786464 | tf_op jit(solution)/shard_map/ppermute | solution.py:38
  537.2 11.1 %collective-permute-start.100 = (bf16[4,2,4,48,1024]{4,3,2,1,0:T(8,128)(2,1)S(1)}, bf16[4,2,4,48,1024]{4,3,2,1,0:T(8,128)(2,1)S(1)}, u32[]{:S(2)}, u32[]{:S(2)}) collective-permute-start(bf16[4,2,4,48,1024]{4,3,2,1,0:T(8,128)(2,1)S(1)} %pad_maximum_fusion.2.mine_ref), channel_id=1, source_target_pairs={{0,4},{4,0},{8,12},{12,8},{16,20},{20,16},{24,28},{28,24},{32,36},... | collective-permute-start | bytes 9437192 | tf_op jit(solution)/shard_map/ppermute | solution.py:68
  557.1 5.5 dense_layout.2
  563.2 5.7 dense_layout.3
  (639 shorter events, 282.6 us)
Async XLA Ops:
  7.2 129.8 %all-gather.3.cloned.1.call-start = ((), (), s32[]{:S(2)}) async-start(), calls=%async_computation.4 | async-start | bytes 1966080 | tf_op jit(solution)/shard_map/all_gather | solution.py:886
  37.8 37.0 %collective-permute-start.10 = (bf16[2,2,3,96,512]{4,3,2,1,0:T(8,128)(2,1)S(1)}, bf16[2,2,3,96,512]{4,3,2,1,0:T(8,128)(2,1)S(1)}, u32[]{:S(2)}, u32[]{:S(2)}) collective-permute-start(bf16[2,2,3,96,512]{4,3,2,1,0:T(8,128)(2,1)S(1)} %get-tuple-element.437), channel_id=1, source_target_pairs={{0,48},{4,52},{8,56},{12,60},{16,0},{20,4},{24,8},{28,12},{32,16},... | collective-permute-start | bytes 3538952 | tf_op jit(solution)/shard_map/ppermute | solution.py:68
  42.1 37.3 %collective-permute-start.13 = (bf16[3,2,3,96,512]{4,3,2,1,0:T(8,128)(2,1)}, bf16[3,2,3,96,512]{4,3,2,1,0:T(8,128)(2,1)}, u32[]{:S(2)}, u32[]{:S(2)}) collective-permute-start(bf16[3,2,3,96,512]{4,3,2,1,0:T(8,128)(2,1)} %pad_maximum_fusion.3.refs_2_), channel_id=1, source_target_pairs={{0,8},{4,12},{8,0},{12,4},{16,24},{20,28},{24,16},{28,20},{32,40},... | collective-permute-start | bytes 5308424 | tf_op jit(solution)/shard_map/ppermute | solution.py:68
  43.7 25.6 %collective-permute-start.12 = (bf16[3,96,512]{2,1,0:T(8,128)(2,1)S(1)}, bf16[3,96,512]{2,1,0:T(8,128)(2,1)S(1)}, u32[]{:S(2)}, u32[]{:S(2)}) collective-permute-start(bf16[3,96,512]{2,1,0:T(8,128)(2,1)S(1)} %slice_bitcast_fusion.4), channel_id=1, source_target_pairs={{0,48},{4,52},{8,56},{12,60},{16,0},{20,4},{24,8},{28,12},{32,16},... | collective-permute-start | bytes 884744 | tf_op jit(solution)/shard_map/ppermute | solution.py:68
  44.0 25.4 %collective-permute-start.11 = (bf16[3,96,512]{2,1,0:T(8,128)(2,1)S(1)}, bf16[3,96,512]{2,1,0:T(8,128)(2,1)S(1)}, u32[]{:S(2)}, u32[]{:S(2)}) collective-permute-start(bf16[3,96,512]{2,1,0:T(8,128)(2,1)S(1)} %slice_bitcast_fusion.5), channel_id=1, source_target_pairs={{0,16},{4,20},{8,24},{12,28},{16,32},{20,36},{24,40},{28,44},{32,4... | collective-permute-start | bytes 884744 | tf_op jit(solution)/shard_map/ppermute | solution.py:68
  45.4 29.3 %collective-permute-start.9 = (bf16[2,2,3,96,512]{4,3,2,0,1:T(8,128)(2,1)S(1)}, bf16[2,2,3,96,512]{4,3,2,0,1:T(8,128)(2,1)S(1)}, u32[]{:S(2)}, u32[]{:S(2)}) collective-permute-start(bf16[2,2,3,96,512]{4,3,2,0,1:T(8,128)(2,1)S(1)} %copy.97), channel_id=1, source_target_pairs={{0,16},{4,20},{8,24},{12,28},{16,32},{20,36},{24,40},{28,44},{32,4... | collective-permute-start | bytes 3538952 | tf_op jit(solution)/shard_map/ppermute | solution.py:68
  81.5 21.4 %collective-permute-start.17 = (bf16[3,2,2,3,96,512]{5,4,3,2,1,0:T(8,128)(2,1)}, bf16[3,2,2,3,96,512]{5,4,3,2,1,0:T(8,128)(2,1)}, u32[]{:S(2)}, u32[]{:S(2)}) collective-permute-start(bf16[3,2,2,3,96,512]{5,4,3,2,1,0:T(8,128)(2,1)} %pad_maximum_fusion.refs_0_), channel_id=1, source_target_pairs={{0,4},{4,0},{8,12},{12,8},{16,20},{20,16},{24,28},{28,24},{32,36},... | collective-permute-start | bytes 10616840 | tf_op jit(solution)/shard_map/ppermute | solution.py:68
  85.8 336.0 %reduce-scatter.3.cloned.1.call-start = ((), (), s32[]{:S(2)}) async-start(), calls=%async_computation.2 | async-start | bytes 1966080 | tf_op jit(solution)/shard_map/reduce_scatter | solution.py:951
  164.5 40.9 %collective-permute-start.36 = (bf16[1,64,1536]{2,1,0:T(8,128)(2,1)}, bf16[1,64,1536]{2,1,0:T(8,128)(2,1)}, u32[]{:S(2)}, u32[]{:S(2)}) collective-permute-start(bf16[1,64,1536]{2,1,0:T(8,128)(2,1)} %collective-permute-done.33), channel_id=1, source_target_pairs={{0,3},{1,0},{2,1},{3,2},{4,7},{5,4},{6,5},{7,6},{8,11},{9,8},{10,9... | collective-permute-start | bytes 589832 | tf_op jit(solution)/shard_map/ppermute | solution.py:38
  165.3 40.1 %collective-permute-start.35 = (bf16[1,64,1536]{2,1,0:T(8,128)(2,1)}, bf16[1,64,1536]{2,1,0:T(8,128)(2,1)}, u32[]{:S(2)}, u32[]{:S(2)}) collective-permute-start(bf16[1,64,1536]{2,1,0:T(8,128)(2,1)} %collective-permute-done.33), channel_id=1, source_target_pairs={{0,2},{1,3},{2,0},{3,1},{4,6},{5,7},{6,4},{7,5},{8,10},{9,11},{10,... | collective-permute-start | bytes 589832 | tf_op jit(solution)/shard_map/ppermute | solution.py:38
  166.6 38.9 %collective-permute-start.34 = (bf16[1,64,1536]{2,1,0:T(8,128)(2,1)}, bf16[1,64,1536]{2,1,0:T(8,128)(2,1)}, u32[]{:S(2)}, u32[]{:S(2)}) collective-permute-start(bf16[1,64,1536]{2,1,0:T(8,128)(2,1)} %collective-permute-done.33), channel_id=1, source_target_pairs={{0,1},{1,2},{2,3},{3,0},{4,5},{5,6},{6,7},{7,4},{8,9},{9,10},{10,1... | collective-permute-start | bytes 589832 | tf_op jit(solution)/shard_map/ppermute | solution.py:38
  207.7 35.6 %collective-permute-start.37 = (bf16[1,64,1536]{2,1,0:T(8,128)(2,1)}, bf16[1,64,1536]{2,1,0:T(8,128)(2,1)}, u32[]{:S(2)}, u32[]{:S(2)}) collective-permute-start(bf16[1,64,1536]{2,1,0:T(8,128)(2,1)} %get-tuple-element.251), channel_id=1, source_target_pairs={{0,3},{1,0},{2,1},{3,2},{4,7},{5,4},{6,5},{7,6},{8,11},{9,8},{10,9... | collective-permute-start | bytes 589832 | tf_op jit(solution)/shard_map/ppermute | solution.py:38
  207.7 36.4 %collective-permute-start.38 = (bf16[1,64,1536]{2,1,0:T(8,128)(2,1)}, bf16[1,64,1536]{2,1,0:T(8,128)(2,1)}, u32[]{:S(2)}, u32[]{:S(2)}) collective-permute-start(bf16[1,64,1536]{2,1,0:T(8,128)(2,1)} %get-tuple-element.252), channel_id=1, source_target_pairs={{0,2},{1,3},{2,0},{3,1},{4,6},{5,7},{6,4},{7,5},{8,10},{9,11},{10,... | collective-permute-start | bytes 589832 | tf_op jit(solution)/shard_map/ppermute | solution.py:38
  207.7 36.4 %collective-permute-start.39 = (bf16[1,64,1536]{2,1,0:T(8,128)(2,1)}, bf16[1,64,1536]{2,1,0:T(8,128)(2,1)}, u32[]{:S(2)}, u32[]{:S(2)}) collective-permute-start(bf16[1,64,1536]{2,1,0:T(8,128)(2,1)} %get-tuple-element.253), channel_id=1, source_target_pairs={{0,1},{1,2},{2,3},{3,0},{4,5},{5,6},{6,7},{7,4},{8,9},{9,10},{10,1... | collective-permute-start | bytes 589832 | tf_op jit(solution)/shard_map/ppermute | solution.py:38
  238.4 23.1 %collective-permute-start.43 = (bf16[1,64,1536]{2,1,0:T(8,128)(2,1)}, bf16[1,64,1536]{2,1,0:T(8,128)(2,1)S(1)}, u32[]{:S(2)}, u32[]{:S(2)}) collective-permute-start(bf16[1,64,1536]{2,1,0:T(8,128)(2,1)} %get-tuple-element.261), channel_id=1, source_target_pairs={{0,3},{1,0},{2,1},{3,2},{4,7},{5,4},{6,5},{7,6},{8,11},{9,8},{10,9... | collective-permute-start | bytes 589832 | tf_op jit(solution)/shard_map/ppermute | solution.py:38
  240.9 21.1 %collective-permute-start.44 = (bf16[1,64,1536]{2,1,0:T(8,128)(2,1)}, bf16[1,64,1536]{2,1,0:T(8,128)(2,1)S(1)}, u32[]{:S(2)}, u32[]{:S(2)}) collective-permute-start(bf16[1,64,1536]{2,1,0:T(8,128)(2,1)} %get-tuple-element.262), channel_id=1, source_target_pairs={{0,2},{1,3},{2,0},{3,1},{4,6},{5,7},{6,4},{7,5},{8,10},{9,11},{10,... | collective-permute-start | bytes 589832 | tf_op jit(solution)/shard_map/ppermute | solution.py:38
  243.3 18.8 %collective-permute-start.45 = (bf16[1,64,1536]{2,1,0:T(8,128)(2,1)}, bf16[1,64,1536]{2,1,0:T(8,128)(2,1)S(1)}, u32[]{:S(2)}, u32[]{:S(2)}) collective-permute-start(bf16[1,64,1536]{2,1,0:T(8,128)(2,1)} %get-tuple-element.263), channel_id=1, source_target_pairs={{0,1},{1,2},{2,3},{3,0},{4,5},{5,6},{6,7},{7,4},{8,9},{9,10},{10,1... | collective-permute-start | bytes 589832 | tf_op jit(solution)/shard_map/ppermute | solution.py:38
  257.6 18.6 %collective-permute-start.40 = (bf16[1,64,1024]{2,1,0:T(8,128)(2,1)S(1)}, bf16[1,64,1024]{2,1,0:T(8,128)(2,1)S(1)}, u32[]{:S(2)}, u32[]{:S(2)}) collective-permute-start(bf16[1,64,1024]{2,1,0:T(8,128)(2,1)S(1)} %get-tuple-element.256), channel_id=1, source_target_pairs={{0,3},{1,0},{2,1},{3,2},{4,7},{5,4},{6,5},{7,6},{8,11},{9,8},{10,9... | collective-permute-start | bytes 393224 | tf_op jit(solution)/shard_map/ppermute | solution.py:38
  320.7 20.1 %collective-permute-start.57 = (bf16[2,64,1536]{2,1,0:T(8,128)(2,1)S(1)}, bf16[2,64,1536]{2,1,0:T(8,128)(2,1)S(1)}, u32[]{:S(2)}, u32[]{:S(2)}) collective-permute-start(bf16[2,64,1536]{2,1,0:T(8,128)(2,1)S(1)} %get-tuple-element.286), channel_id=1, source_target_pairs={{0,3},{1,0},{2,1},{3,2},{4,7},{5,4},{6,5},{7,6},{8,11},{9,8},{10,9... | collective-permute-start | bytes 1179656 | tf_op jit(solution)/shard_map/ppermute | solution.py:38
  320.8 20.0 %collective-permute-start.58 = (bf16[2,64,1536]{2,1,0:T(8,128)(2,1)S(1)}, bf16[2,64,1536]{2,1,0:T(8,128)(2,1)S(1)}, u32[]{:S(2)}, u32[]{:S(2)}) collective-permute-start(bf16[2,64,1536]{2,1,0:T(8,128)(2,1)S(1)} %get-tuple-element.287), channel_id=1, source_target_pairs={{0,2},{1,3},{2,0},{3,1},{4,6},{5,7},{6,4},{7,5},{8,10},{9,11},{10,... | collective-permute-start | bytes 1179656 | tf_op jit(solution)/shard_map/ppermute | solution.py:38
  320.9 19.9 %collective-permute-start.59 = (bf16[2,64,1536]{2,1,0:T(8,128)(2,1)S(1)}, bf16[2,64,1536]{2,1,0:T(8,128)(2,1)S(1)}, u32[]{:S(2)}, u32[]{:S(2)}) collective-permute-start(bf16[2,64,1536]{2,1,0:T(8,128)(2,1)S(1)} %get-tuple-element.288), channel_id=1, source_target_pairs={{0,1},{1,2},{2,3},{3,0},{4,5},{5,6},{6,7},{7,4},{8,9},{9,10},{10,1... | collective-permute-start | bytes 1179656 | tf_op jit(solution)/shard_map/ppermute | solution.py:38
  343.5 20.6 %collective-permute-start.63 = (bf16[2,2,16,96,512]{4,3,2,1,0:T(8,128)(2,1)S(1)}, bf16[2,2,16,96,512]{4,3,2,1,0:T(8,128)(2,1)S(1)}, u32[]{:S(2)}, u32[]{:S(2)}) collective-permute-start(bf16[2,2,16,96,512]{4,3,2,1,0:T(8,128)(2,1)S(1)} %get-tuple-element.297), channel_id=1, source_target_pairs={{0,4},{4,0},{8,12},{12,8},{16,20},{20,16},{24,28},{28,24},{32,36},... | collective-permute-start | bytes 18874376 | tf_op jit(solution)/shard_map/ppermute | solution.py:68
  349.8 20.3 %collective-permute-start.64 = (bf16[1,2,16,96,512]{4,3,2,1,0:T(8,128)(2,1)S(1)}, bf16[1,2,16,96,512]{4,3,2,1,0:T(8,128)(2,1)}, u32[]{:S(2)}, u32[]{:S(2)}) collective-permute-start(bf16[1,2,16,96,512]{4,3,2,1,0:T(8,128)(2,1)S(1)} %get-tuple-element.299), channel_id=1, source_target_pairs={{0,4},{4,0},{8,12},{12,8},{16,20},{20,16},{24,28},{28,24},{32,36},... | collective-permute-start | bytes 9437192 | tf_op jit(solution)/shard_map/ppermute | solution.py:68
  349.8 32.4 %collective-permute-start.62 = (bf16[2,64,1536]{2,1,0:T(8,128)(2,1)S(1)}, bf16[2,64,1536]{2,1,0:T(8,128)(2,1)}, u32[]{:S(2)}, u32[]{:S(2)}) collective-permute-start(bf16[2,64,1536]{2,1,0:T(8,128)(2,1)S(1)} %convert_element_type.402.refs_6_.refs_4_), channel_id=1, source_target_pairs={{0,3},{1,0},{2,1},{3,2},{4,7},{5,4},{6,5},{7,6},{8,11},{9,8},{10,9... | collective-permute-start | bytes 1179656 | tf_op jit(solution)/shard_map/ppermute | solution.py:38
  352.2 30.1 %collective-permute-start.61 = (bf16[2,64,1536]{2,1,0:T(8,128)(2,1)S(1)}, bf16[2,64,1536]{2,1,0:T(8,128)(2,1)}, u32[]{:S(2)}, u32[]{:S(2)}) collective-permute-start(bf16[2,64,1536]{2,1,0:T(8,128)(2,1)S(1)} %convert_element_type.402.refs_6_.refs_4_), channel_id=1, source_target_pairs={{0,2},{1,3},{2,0},{3,1},{4,6},{5,7},{6,4},{7,5},{8,10},{9,11},{10,... | collective-permute-start | bytes 1179656 | tf_op jit(solution)/shard_map/ppermute | solution.py:38
  353.7 28.6 %collective-permute-start.60 = (bf16[2,64,1536]{2,1,0:T(8,128)(2,1)S(1)}, bf16[2,64,1536]{2,1,0:T(8,128)(2,1)}, u32[]{:S(2)}, u32[]{:S(2)}) collective-permute-start(bf16[2,64,1536]{2,1,0:T(8,128)(2,1)S(1)} %convert_element_type.402.refs_6_.refs_4_), channel_id=1, source_target_pairs={{0,1},{1,2},{2,3},{3,0},{4,5},{5,6},{6,7},{7,4},{8,9},{9,10},{10,1... | collective-permute-start | bytes 1179656 | tf_op jit(solution)/shard_map/ppermute | solution.py:38
  382.3 28.8 %collective-permute-start.65 = (bf16[2,2,3,96,512]{4,3,2,1,0:T(8,128)(2,1)}, bf16[2,2,3,96,512]{4,3,2,1,0:T(8,128)(2,1)S(1)}, u32[]{:S(2)}, u32[]{:S(2)}) collective-permute-start(bf16[2,2,3,96,512]{4,3,2,1,0:T(8,128)(2,1)} %get-tuple-element.315), channel_id=1, source_target_pairs={{0,16},{4,20},{8,24},{12,28},{16,32},{20,36},{24,40},{28,44},{32,4... | collective-permute-start | bytes 3538952 | tf_op jit(solution)/shard_map/ppermute | solution.py:68
  382.5 28.6 %collective-permute-start.66 = (bf16[2,2,3,96,512]{4,3,2,1,0:T(8,128)(2,1)}, bf16[2,2,3,96,512]{4,3,2,1,0:T(8,128)(2,1)S(1)}, u32[]{:S(2)}, u32[]{:S(2)}) collective-permute-start(bf16[2,2,3,96,512]{4,3,2,1,0:T(8,128)(2,1)} %get-tuple-element.316), channel_id=1, source_target_pairs={{0,48},{4,52},{8,56},{12,60},{16,0},{20,4},{24,8},{28,12},{32,16},... | collective-permute-start | bytes 3538952 | tf_op jit(solution)/shard_map/ppermute | solution.py:68
  385.0 27.0 %collective-permute-start.67 = (bf16[4,3,96,512]{3,2,1,0:T(8,128)(2,1)}, bf16[4,3,96,512]{3,2,1,0:T(8,128)(2,1)}, u32[]{:S(2)}, u32[]{:S(2)}) collective-permute-start(bf16[4,3,96,512]{3,2,1,0:T(8,128)(2,1)} %get-tuple-element.317), channel_id=1, source_target_pairs={{0,8},{4,12},{8,0},{12,4},{16,24},{20,28},{24,16},{28,20},{32,40},... | collective-permute-start | bytes 3538952 | tf_op jit(solution)/shard_map/ppermute | solution.py:68
  397.1 138.1 %reduce-scatter.5.cloned.1.call-start = ((), (), s32[]{:S(2)}) async-start(), calls=%async_computation.3 | async-start | bytes 1966080 | tf_op jit(solution)/shard_map/reduce_scatter | solution.py:959
  414.6 28.0 %collective-permute-start.74 = (bf16[4,3,96,512]{3,2,1,0:T(8,128)(2,1)}, bf16[4,3,96,512]{3,2,1,0:T(8,128)(2,1)}, u32[]{:S(2)}, u32[]{:S(2)}) collective-permute-start(bf16[4,3,96,512]{3,2,1,0:T(8,128)(2,1)} %get-tuple-element.328), channel_id=1, source_target_pairs={{0,8},{4,12},{8,0},{12,4},{16,24},{20,28},{24,16},{28,20},{32,40},... | collective-permute-start | bytes 3538952 | tf_op jit(solution)/shard_map/ppermute | solution.py:68
  513.7 21.5 %collective-permute-start.93 = (bf16[2,4,48,1024]{3,2,1,0:T(8,128)(2,1)}, bf16[2,4,48,1024]{3,2,1,0:T(8,128)(2,1)}, u32[]{:S(2)}, u32[]{:S(2)}) collective-permute-start(bf16[2,4,48,1024]{3,2,1,0:T(8,128)(2,1)} %get-tuple-element.445), channel_id=1, source_target_pairs={{0,2},{1,3},{2,0},{3,1},{4,6},{5,7},{6,4},{7,5},{8,10},{9,11},{10,... | collective-permute-start | bytes 2359304 | tf_op jit(solution)/shard_map/ppermute | solution.py:38
  (223 other events, 2323.3 us)
Sparse Core Ops, SparseCore 0:
  85.9 25.6 all-gather.2
  397.2 24.5 reduce-scatter.2
  469.5 27.6 reduce-scatter.4

commit v5 on v4

--- a/solution.py
+++ b/solution.py
@@ -651,45 +651,45 @@
     )(place, *lefts, *rights)
 
 
-def chip_sum_kernel(
-    mine_inner, other_inner, mine_outer, other_outer, keep_ring, to_above, to_below, keep_pair, to_pair, to_pair_next
-):
-    matrix, kind = pl.program_id(0), pl.program_id(1)
-    ring = {index: (keep_ring, at) for at, index in enumerate((0, 1, 2, 7))}
-    ring.update({3: (to_above, 0), 4: (to_above, 1), 5: (to_below, 0), 6: (to_below, 1)})
-
-    def add(mine, other, ring_first):
+def chip_sum_kernel(ring_first, mine_inner, other_inner, mine_outer, other_outer, *refs):
+    matrix = pl.program_id(0)
+    keep, *away = refs
+    places = [(keep, 0), (keep, 1), (keep, 2), (away[0], 0), (away[0], 1), (away[1], 0), (away[1], 1), (keep, 3)]
+
+    def add(mine, other):
         for index in range(2 * RING * PAIR):
             value = mine[0, 0, index] + other[0, 0, index]
             if ring_first:
-                ref, at = ring[index // PAIR]
+                ref, at = places[index // PAIR]
                 ref[at, index % PAIR, 0] = value
             elif index < 2 * RING:
-                keep_pair[index, 0] = value
+                keep[index, 0] = value
             else:
-                (to_pair if index < 3 * RING else to_pair_next)[index % RING, 0] = value
-
-    for inner in (True, False):
-        for ring_first in (True, False):
-
-            @pl.when(((matrix < 2) == inner) & ((kind == 0) == ring_first))
-            def _(inner=inner, ring_first=ring_first):
-                add(*((mine_inner, other_inner) if inner else (mine_outer, other_outer)), ring_first)
-
-
-def chip_sum(inner, outer):
+                away[index // RING - 2][index % RING, 0] = value
+
+    @pl.when(matrix < 2)
+    def _():
+        add(mine_inner, other_inner)
+
+    @pl.when(matrix == 2)
+    def _():
+        add(mine_outer, other_outer)
+
+
+def chip_sum(inner, outer, ring_first):
     tile = inner[0].shape[3:]
+    kind = 0 if ring_first else 1
     block = (1, 1, 2 * RING * PAIR) + tile
-    inner_spec = pl.BlockSpec(block, lambda m, k: (jnp.minimum(m, 1), jnp.where(m < 2, k, 1), 0, 0, 0))
-    outer_spec = pl.BlockSpec(block, lambda m, k: (0, jnp.where(m < 2, 0, k), 0, 0, 0))
-    shapes = [(4, PAIR), (2, PAIR), (2, PAIR), (2 * RING,), (RING,), (RING,)]
-    return pl.pallas_call(
-        chip_sum_kernel,
-        grid=(3, 2),
+    inner_spec = pl.BlockSpec(block, lambda m: (jnp.minimum(m, 1), kind, 0, 0, 0))
+    outer_spec = pl.BlockSpec(block, lambda m: (0, kind, 0, 0, 0))
+    shapes = [(4, PAIR), (2, PAIR), (2, PAIR)] if ring_first else [(2 * RING,), (RING,), (RING,)]
+    return pl.pallas_call(
+        functools.partial(chip_sum_kernel, ring_first),
+        grid=(3,),
         in_specs=[inner_spec, inner_spec, outer_spec, outer_spec],
-        out_specs=[pl.BlockSpec(shape + (1,) + tile, lambda m, k, n=len(shape): (0,) * n + (m, 0, 0)) for shape in shapes],
+        out_specs=[pl.BlockSpec(shape + (1,) + tile, lambda m, n=len(shape): (0,) * n + (m, 0, 0)) for shape in shapes],
         out_shape=[jax.ShapeDtypeStruct(shape + (3,) + tile, LOW) for shape in shapes],
-        compiler_params=params("arbitrary", "arbitrary", mib=56),
+        compiler_params=params("arbitrary", mib=56),
         name="chip_sum",
     )(*inner, *outer)
 
@@ -941,8 +941,9 @@
     outputs = jnp.stack(outputs).reshape(batches, parts, own, width)
     outputs = jnp.stack([lax.dynamic_index_in_dim(outputs, (z + parts - i) % parts, 1, False) for i in range(parts)])
     outer, outputs = hold(outer, outputs)
-    keep_ring, to_above, to_below, keep_pair, *to_pair = chip_sum(inner, outer)
-    da, to_above, to_below, to_pair = hold(da, to_above, to_below, to_pair)
+    keep_ring, to_above, to_below = chip_sum(inner, outer, True)
+    keep_pair, *to_pair = chip_sum(once(inner, to_above), outer, False)
+    da, to_pair = hold(da, to_pair)
 
     ring_1 = moved(to_above, x=1), moved(to_below, x=-1)
     pair_1 = [moved(block, y=1) for block in to_pair]

time: 583 us -> 582 us (level)
    pallas_call x1 -> x2, Pallas kernels: 12.2 us -> 11.3 us  [chip_sum(): pl.pallas_call(functools.partial(chip_sum_kernel, ring_first), grid=(3,),...]
where the time goes in v5:
time: 582 us; the launch traced here: 576 us
  Pallas kernels  183 us (31%)
  waiting for transfers between devices  144 us (25%)
  starting transfers between devices  135 us (23%)
  other arithmetic  54.9 us (9%)
  local copies, waits for them, and re-layouts  33.5 us (6%)
  between operations  16.4 us (3%)
  matrix products  9.24 us (2%)
    ppermute x46, waiting for transfers between devices, moved(): return lax.ppermute(block, 'dp', route)  86.6 us
    ppermute x46, starting transfers between devices, moved(): return lax.ppermute(block, 'dp', route)  62.3 us
    ppermute x48, starting transfers between devices, shifted(): lax.ppermute(block, 'expert', [(i, (i + by) % size) for i in range(size)])  50.5 us
    ppermute x48, waiting for transfers between devices, shifted(): lax.ppermute(block, 'expert', [(i, (i + by) % size) for i in range(size)])  49.6 us
    pallas_call x2, Pallas kernels, experts_turn(): pl.pallas_call(experts_turn_kernel, grid=(count,), in_specs=[pl.BlockSpec...  29.7 us
    unnamed x300, local copies, waits for them, and re-layouts  22.2 us
    pallas_call x1, Pallas kernels, experts_forward(): pl.pallas_call(experts_forward_kernel, grid_spec=pltpu.PrefetchScalarGrid...  20.5 us
    pallas_call x3, Pallas kernels, attend(): pl.pallas_call(attend_kernel, grid=(batches, parts), in_specs=[pl.BlockSp...  19.2 us
  transfers between devices with their start and end apart: 107, of which 47 were waited for; matrix products, arithmetic and copies ran while one was open for 11% of the time, Pallas kernels for 28%

profile of v5, /device:TPU:1, one launch (start us, length us, event | category | flops | bytes accessed | tf_op | source)
XLA Modules:
  0.0 575.6 jit_solution(9657690998107125427)
XLA Ops:
  47.0 9.2 %project.3 = (bf16[512,2560]{1,0:T(8,128)(2,1)S(1)}, bf16[512,1536]{1,0:T(8,128)(2,1)}) custom-call(bf16[512,1536]{1,0:T(8,128)(2,1)S(1)} %bitcast.324, f32[1,1536]{1,0:T(1,128)S(1)} %copy-done.45, bf16[1536,1536]{1,0:T(8,128)(2,1)S(1)} %bitcast.278, bf16[1536,512]{1,0:T(8,128)(2,1)S(1)} %bitcast.314, bf16[1536,512]{1,0:T(8,128)(2,1)S(1)} %bitcast.318, ...), custom_call_target="tpu_custom_call" | custom-call | tf_op jit(solution)/shard_map/project/pallas_call | solution.py:158
  56.4 9.6 %attend.3.o_ref = bf16[2,256,1536]{2,1,0:T(8,128)(2,1)S(1)} custom-call(bf16[2,256,2560]{2,1,0:T(8,128)(2,1)S(1)} %bitcast.321, bf16[2,256,2560]{2,1,0:T(8,128)(2,1)S(1)} %bitcast.322, bf16[2,256,2560]{2,1,0:T(8,128)(2,1)S(1)} %bitcast.323, f32[2,256,256]{2,1,0:T(8,128)S(1)} %and_select_fusion.bias_ref.refs_14_), custom_call_target="tpu_custom_call" | custom-call | tf_op jit(solution)/shard_map/attend/pallas_call | solution.py:209
  69.4 5.3 collective-permute-done.9
  94.8 5.8 %collective-permute-done.15 = bf16[2,3,96,512]{3,2,1,0:T(8,128)(2,1)S(1)} collective-permute-done((bf16[2,3,96,512]{3,2,1,0:T(8,128)(2,1)S(1)}, bf16[2,3,96,512]{3,2,1,0:T(8,128)(2,1)S(1)}, u32[]{:S(2)}, u32[]{:S(2)}) %collective-permute-start.15) | collective-permute-done | bytes 589856 | tf_op jit(solution)/shard_map/ppermute | solution.py:68
  111.7 20.5 %experts_forward.1 = (bf16[1,64,1536]{2,1,0:T(8,128)(2,1)S(1)}, bf16[1,64,1536]{2,1,0:T(8,128)(2,1)}, bf16[1,64,1536]{2,1,0:T(8,128)(2,1)}, bf16[1,64,1536]{2,1,...) custom-call(s32[3]{0:T(128)S(1)} %pad_add_fusion.place_ref, ...), custom_call_target="tpu_custom_call" | custom-call | tf_op jit(solution)/shard_map/experts_forward/pallas_call | solution.py:333
  144.0 5.2 collective-permute-done.25
  167.8 6.4 %collective-permute-done.27 = bf16[1,64,1536]{2,1,0:T(8,128)(2,1)S(1)} collective-permute-done((bf16[1,64,1536]{2,1,0:T(8,128)(2,1)S(1)}, bf16[1,64,1536]{2,1,0:T(8,128)(2,1)S(1)}, u32[]{:S(2)}, u32[]{:S(2)}) %collective-permute-start.27) | collective-permute-done | bytes 196640 | tf_op jit(solution)/shard_map/ppermute | solution.py:38
  177.5 4.8 project.4
  190.4 15.0 %experts_turn.2 = (bf16[256,2048]{1,0:T(8,128)(2,1)}, bf16[256,2048]{1,0:T(8,128)(2,1)}, bf16[256,2048]{1,0:T(8,128)(2,1)}, bf16[1,64,1536]{2,1,0:T(8,128)(2,1)}...) custom-call(bf16[256,1536]{1,0:T(8,128)(2,1)} %bitcast.331, ...), custom_call_target="tpu_custom_call" | custom-call | tf_op jit(solution)/shard_map/experts_turn/pallas_call | solution.py:383
  223.7 14.7 %experts_turn.3 = (bf16[256,2048]{1,0:T(8,128)(2,1)}, bf16[256,2048]{1,0:T(8,128)(2,1)}, bf16[256,2048]{1,0:T(8,128)(2,1)}, bf16[1,64,1536]{2,1,0:T(8,128)(2,1)}...) custom-call(bf16[256,1536]{1,0:T(8,128)(2,1)} %bitcast.333, ...), custom_call_target="tpu_custom_call" | custom-call | tf_op jit(solution)/shard_map/experts_turn/pallas_call | solution.py:383
  249.5 8.1 %own_backward.2 = (bf16[1,64,1536]{2,1,0:T(8,128)(2,1)S(1)}, bf16[1,64,1024]{2,1,0:T(8,128)(2,1)S(1)}, bf16[1,64,1024]{2,1,0:T(8,128)(2,1)S(1)}, bf16[1,64,1024]...) custom-call(bf16[1,256,2560]{2,1,0:T(8,128)(2,1)S(1)} %bitcast.298, bf16[1,256,2560]{2,1,0:T(8,128)(2,1)S(1)} %bitcast.299, ...), custom_call_target="tpu_custom_call" | custom-call | tf_op jit(solution)/shard_map/own_backward/pallas_call | solution.py:559
  262.6 8.2 %own_backward.3 = (bf16[1,64,1536]{2,1,0:T(8,128)(2,1)S(1)}, bf16[1,64,1024]{2,1,0:T(8,128)(2,1)S(1)}, bf16[1,64,1024]{2,1,0:T(8,128)(2,1)S(1)}, bf16[1,64,1024]...) custom-call(bf16[1,256,2560]{2,1,0:T(8,128)(2,1)S(1)} %bitcast.307, bf16[1,256,2560]{2,1,0:T(8,128)(2,1)S(1)} %bitcast.308, ...), custom_call_target="tpu_custom_call" | custom-call | tf_op jit(solution)/shard_map/own_backward/pallas_call | solution.py:559
  297.1 5.5 collective-permute-done.54
  305.8 14.9 %experts_backward.1 = (bf16[2,64,1536]{2,1,0:T(8,128)(2,1)S(1)}, bf16[2,64,1536]{2,1,0:T(8,128)(2,1)S(1)}, bf16[2,64,1536]{2,1,0:T(8,128)(2,1)S(1)}, bf16[2,64,1...) custom-call(bf16[256,1536]{1,0:T(8,128)(2,1)S(1)} %bitcast.328, bf16[256,1536]{1,0:T(8,128)(2,1)S(1)} %bitcast.327, ...), custom_call_target="tpu_custom_call" | custom-call | tf_op jit(solution)/shard_map/experts_backward/pallas_call | solution.py:423
  322.8 5.5 expert_grad.3
  330.0 10.7 %expert_grad.2 = (bf16[2,2,16,96,512]{4,3,2,1,0:T(8,128)(2,1)S(1)}, bf16[2,2,16,96,512]{4,3,2,1,0:T(8,128)(2,1)S(1)}) custom-call(s32[3]{0:T(128)S(1)} %copy-done.48, bf16[256,1536]{1,0:T(8,128)(2,1)S(1)} %bitcast.332, bf16[256,1536]{1,0:T(8,128)(2,1)S(1)} %bitcast.334, bf16[2,512,2048]{2,1,0:T(8,128)(2,1)S(1)} %get-tuple-element.289.refs_2_), custom_call_target="tpu_custom_call" | custom-call | tf_op jit(solution)/shard_map/expert_grad/pallas_call | solution.py:639
  343.5 6.3 %collective-permute-start.63 = (bf16[2,2,16,96,512]{4,3,2,1,0:T(8,128)(2,1)S(1)}, bf16[2,2,16,96,512]{4,3,2,1,0:T(8,128)(2,1)S(1)}, u32[]{:S(2)}, u32[]{:S(2)}) collective-permute-start(bf16[2,2,16,96,512]{4,3,2,1,0:T(8,128)(2,1)S(1)} %get-tuple-element.297), channel_id=1, source_target_pairs={{0,4},{4,0},{8,12},{12,8},{16,20},{20,16},{24,28},{28,24},{32,36},... | collective-permute-start | bytes 18874376 | tf_op jit(solution)/shard_map/ppermute | solution.py:68
  354.5 9.6 %collective-permute-done.63.other_inner = bf16[2,2,16,96,512]{4,3,2,1,0:T(8,128)(2,1)S(1)} collective-permute-done((bf16[2,2,16,96,512]{4,3,2,1,0:T(8,128)(2,1)S(1)}, bf16[2,2,16,96,512]{4,3,2,1,0:T(8,128)(2,1)S(1)}, u32[]{:S(2)}, u32[]{:S(2)}) %collective-permute-start.63) | collective-permute-done | bytes 6291488 | tf_op jit(solution)/shard_map/ppermute | solution.py:68
  370.1 5.6 chip_sum.2
  375.7 5.7 chip_sum.3
  384.5 11.4 %attend_backward.1 = (bf16[512,640]{1,0:T(8,128)(2,1)}, bf16[4,2,64,1536]{3,2,1,0:T(8,128)(2,1)}) custom-call(s32[1]{0:T(128)} %bitcast.50.z_ref, bf16[1,256,2560]{2,1,0:T(8,128)(2,1)} %bitcast.301, bf16[1,256,2560]{2,1,0:T(8,128)(2,1)} %bitcast.310, bf16[1,256,2560]{2,1,0:T(8,128)(2,1)} %bitcast.302, bf16[1,256,2560]{2,1,0:T(8,128)(2,1)} %bitcast.311, ...), custom_call_target="tpu_custom_call" | custom-call | tf_op jit(solution)/shard_map/attend_backward/pallas_call | solution.py:503
  396.0 6.8 %dense_grad.1 = (bf16[8,2,48,1024]{3,2,1,0:T(8,128)(2,1)}, bf16[8,2,48,1024]{3,2,1,0:T(8,128)(2,1)}) custom-call(s32[3]{0:T(128)} %copy-done.47, s32[1]{0:T(128)} %bitcast.50.z_ref, bf16[256,1536]{1,0:T(8,128)(2,1)} %bitcast.329, bf16[256,1536]{1,0:T(8,128)(2,1)} %bitcast.330, bf16[256,1536]{1,0:T(8,128)(2,1)} %copy-done.43, bf16[256,1536]{1,0:T(8,128)(2,1)} %copy-done.44, ...), custom_call_target="tpu_custom_call" | custom-call | tf_op jit(solution)/shard_map/dense_grad/pallas_call | solution.py:732
  402.8 6.2 %collective-permute-done.67 = bf16[4,3,96,512]{3,2,1,0:T(8,128)(2,1)} collective-permute-done((bf16[4,3,96,512]{3,2,1,0:T(8,128)(2,1)}, bf16[4,3,96,512]{3,2,1,0:T(8,128)(2,1)}, u32[]{:S(2)}, u32[]{:S(2)}) %collective-permute-start.67) | collective-permute-done | bytes 1179680 | tf_op jit(solution)/shard_map/ppermute | solution.py:68
  423.4 7.9 %collective-permute-done.70 = bf16[2,2,48,1024]{3,2,1,0:T(8,128)(2,1)S(1)} collective-permute-done((bf16[2,2,48,1024]{3,2,1,0:T(8,128)(2,1)}, bf16[2,2,48,1024]{3,2,1,0:T(8,128)(2,1)S(1)}, u32[]{:S(2)}, u32[]{:S(2)}) %collective-permute-start.70) | collective-permute-done | bytes 393248 | tf_op jit(solution)/shard_map/ppermute | solution.py:68
  456.9 9.7 %collective-permute-done.80 = bf16[2,3,96,512]{3,2,1,0:T(8,128)(2,1)S(1)} collective-permute-done((bf16[2,3,96,512]{3,2,1,0:T(8,128)(2,1)S(1)}, bf16[2,3,96,512]{3,2,1,0:T(8,128)(2,1)S(1)}, u32[]{:S(2)}, u32[]{:S(2)}) %collective-permute-start.80) | collective-permute-done | bytes 589856 | tf_op jit(solution)/shard_map/ppermute | solution.py:68
  484.8 7.4 %collective-permute-start.89 = (f32[2,1536]{1,0:T(2,128)S(1)}, f32[2,1536]{1,0:T(2,128)S(1)}, u32[]{:S(2)}, u32[]{:S(2)}) collective-permute-start(f32[2,1536]{1,0:T(2,128)S(1)} %copy-done.131), channel_id=1, source_target_pairs={{0,4},{4,0},{8,12},{12,8},{16,20},{20,16},{24,28},{28,24},{32,36},... | collective-permute-start | bytes 36872 | tf_op jit(solution)/shard_map/ppermute | solution.py:101
  503.8 7.8 %collective-permute-done.98 = bf16[2,3,96,512]{3,2,0,1:T(8,128)(2,1)S(1)} collective-permute-done((bf16[2,3,96,512]{3,2,0,1:T(8,128)(2,1)S(1)}, bf16[2,3,96,512]{3,2,0,1:T(8,128)(2,1)S(1)}, u32[]{:S(2)}, u32[]{:S(2)}) %collective-permute-start.98) | collective-permute-done | bytes 589856 | tf_op jit(solution)/shard_map/ppermute | solution.py:68
  522.0 6.5 %collective-permute-done.92 = bf16[2,4,48,1024]{3,2,1,0:T(8,128)(2,1)} collective-permute-done((bf16[2,4,48,1024]{3,2,1,0:T(8,128)(2,1)}, bf16[2,4,48,1024]{3,2,1,0:T(8,128)(2,1)}, u32[]{:S(2)}, u32[]{:S(2)}) %collective-permute-start.92) | collective-permute-done | bytes 786464 | tf_op jit(solution)/shard_map/ppermute | solution.py:68
  528.5 6.2 %collective-permute-done.93 = bf16[2,4,48,1024]{3,2,1,0:T(8,128)(2,1)} collective-permute-done((bf16[2,4,48,1024]{3,2,1,0:T(8,128)(2,1)}, bf16[2,4,48,1024]{3,2,1,0:T(8,128)(2,1)}, u32[]{:S(2)}, u32[]{:S(2)}) %collective-permute-start.93) | collective-permute-done | bytes 786464 | tf_op jit(solution)/shard_map/ppermute | solution.py:38
  536.7 11.3 %collective-permute-start.100 = (bf16[4,2,4,48,1024]{4,3,2,1,0:T(8,128)(2,1)S(1)}, bf16[4,2,4,48,1024]{4,3,2,1,0:T(8,128)(2,1)S(1)}, u32[]{:S(2)}, u32[]{:S(2)}) collective-permute-start(bf16[4,2,4,48,1024]{4,3,2,1,0:T(8,128)(2,1)S(1)} %pad_maximum_fusion.2.mine_ref), channel_id=1, source_target_pairs={{0,4},{4,0},{8,12},{12,8},{16,20},{20,16},{24,28},{28,24},{32,36},... | collective-permute-start | bytes 9437192 | tf_op jit(solution)/shard_map/ppermute | solution.py:68
  556.9 5.5 dense_layout.2
  563.0 5.7 dense_layout.3
  (640 shorter events, 290.0 us)
Async XLA Ops:
  7.2 129.8 %all-gather.3.cloned.1.call-start = ((), (), s32[]{:S(2)}) async-start(), calls=%async_computation.4 | async-start | bytes 1966080 | tf_op jit(solution)/shard_map/all_gather | solution.py:886
  37.8 37.0 %collective-permute-start.10 = (bf16[2,2,3,96,512]{4,3,2,1,0:T(8,128)(2,1)S(1)}, bf16[2,2,3,96,512]{4,3,2,1,0:T(8,128)(2,1)S(1)}, u32[]{:S(2)}, u32[]{:S(2)}) collective-permute-start(bf16[2,2,3,96,512]{4,3,2,1,0:T(8,128)(2,1)S(1)} %get-tuple-element.437), channel_id=1, source_target_pairs={{0,48},{4,52},{8,56},{12,60},{16,0},{20,4},{24,8},{28,12},{32,16},... | collective-permute-start | bytes 3538952 | tf_op jit(solution)/shard_map/ppermute | solution.py:68
  42.1 37.3 %collective-permute-start.13 = (bf16[3,2,3,96,512]{4,3,2,1,0:T(8,128)(2,1)}, bf16[3,2,3,96,512]{4,3,2,1,0:T(8,128)(2,1)}, u32[]{:S(2)}, u32[]{:S(2)}) collective-permute-start(bf16[3,2,3,96,512]{4,3,2,1,0:T(8,128)(2,1)} %pad_maximum_fusion.3.refs_2_), channel_id=1, source_target_pairs={{0,8},{4,12},{8,0},{12,4},{16,24},{20,28},{24,16},{28,20},{32,40},... | collective-permute-start | bytes 5308424 | tf_op jit(solution)/shard_map/ppermute | solution.py:68
  43.7 25.6 %collective-permute-start.12 = (bf16[3,96,512]{2,1,0:T(8,128)(2,1)S(1)}, bf16[3,96,512]{2,1,0:T(8,128)(2,1)S(1)}, u32[]{:S(2)}, u32[]{:S(2)}) collective-permute-start(bf16[3,96,512]{2,1,0:T(8,128)(2,1)S(1)} %slice_bitcast_fusion.4), channel_id=1, source_target_pairs={{0,48},{4,52},{8,56},{12,60},{16,0},{20,4},{24,8},{28,12},{32,16},... | collective-permute-start | bytes 884744 | tf_op jit(solution)/shard_map/ppermute | solution.py:68
  44.0 25.4 %collective-permute-start.11 = (bf16[3,96,512]{2,1,0:T(8,128)(2,1)S(1)}, bf16[3,96,512]{2,1,0:T(8,128)(2,1)S(1)}, u32[]{:S(2)}, u32[]{:S(2)}) collective-permute-start(bf16[3,96,512]{2,1,0:T(8,128)(2,1)S(1)} %slice_bitcast_fusion.5), channel_id=1, source_target_pairs={{0,16},{4,20},{8,24},{12,28},{16,32},{20,36},{24,40},{28,44},{32,4... | collective-permute-start | bytes 884744 | tf_op jit(solution)/shard_map/ppermute | solution.py:68
  45.4 29.3 %collective-permute-start.9 = (bf16[2,2,3,96,512]{4,3,2,0,1:T(8,128)(2,1)S(1)}, bf16[2,2,3,96,512]{4,3,2,0,1:T(8,128)(2,1)S(1)}, u32[]{:S(2)}, u32[]{:S(2)}) collective-permute-start(bf16[2,2,3,96,512]{4,3,2,0,1:T(8,128)(2,1)S(1)} %copy.97), channel_id=1, source_target_pairs={{0,16},{4,20},{8,24},{12,28},{16,32},{20,36},{24,40},{28,44},{32,4... | collective-permute-start | bytes 3538952 | tf_op jit(solution)/shard_map/ppermute | solution.py:68
  81.5 21.4 %collective-permute-start.17 = (bf16[3,2,2,3,96,512]{5,4,3,2,1,0:T(8,128)(2,1)}, bf16[3,2,2,3,96,512]{5,4,3,2,1,0:T(8,128)(2,1)}, u32[]{:S(2)}, u32[]{:S(2)}) collective-permute-start(bf16[3,2,2,3,96,512]{5,4,3,2,1,0:T(8,128)(2,1)} %pad_maximum_fusion.refs_0_), channel_id=1, source_target_pairs={{0,4},{4,0},{8,12},{12,8},{16,20},{20,16},{24,28},{28,24},{32,36},... | collective-permute-start | bytes 10616840 | tf_op jit(solution)/shard_map/ppermute | solution.py:68
  85.8 336.3 %reduce-scatter.3.cloned.1.call-start = ((), (), s32[]{:S(2)}) async-start(), calls=%async_computation.2 | async-start | bytes 1966080 | tf_op jit(solution)/shard_map/reduce_scatter | solution.py:952
  164.5 40.9 %collective-permute-start.36 = (bf16[1,64,1536]{2,1,0:T(8,128)(2,1)}, bf16[1,64,1536]{2,1,0:T(8,128)(2,1)}, u32[]{:S(2)}, u32[]{:S(2)}) collective-permute-start(bf16[1,64,1536]{2,1,0:T(8,128)(2,1)} %collective-permute-done.33), channel_id=1, source_target_pairs={{0,3},{1,0},{2,1},{3,2},{4,7},{5,4},{6,5},{7,6},{8,11},{9,8},{10,9... | collective-permute-start | bytes 589832 | tf_op jit(solution)/shard_map/ppermute | solution.py:38
  165.3 40.1 %collective-permute-start.35 = (bf16[1,64,1536]{2,1,0:T(8,128)(2,1)}, bf16[1,64,1536]{2,1,0:T(8,128)(2,1)}, u32[]{:S(2)}, u32[]{:S(2)}) collective-permute-start(bf16[1,64,1536]{2,1,0:T(8,128)(2,1)} %collective-permute-done.33), channel_id=1, source_target_pairs={{0,2},{1,3},{2,0},{3,1},{4,6},{5,7},{6,4},{7,5},{8,10},{9,11},{10,... | collective-permute-start | bytes 589832 | tf_op jit(solution)/shard_map/ppermute | solution.py:38
  166.6 38.9 %collective-permute-start.34 = (bf16[1,64,1536]{2,1,0:T(8,128)(2,1)}, bf16[1,64,1536]{2,1,0:T(8,128)(2,1)}, u32[]{:S(2)}, u32[]{:S(2)}) collective-permute-start(bf16[1,64,1536]{2,1,0:T(8,128)(2,1)} %collective-permute-done.33), channel_id=1, source_target_pairs={{0,1},{1,2},{2,3},{3,0},{4,5},{5,6},{6,7},{7,4},{8,9},{9,10},{10,1... | collective-permute-start | bytes 589832 | tf_op jit(solution)/shard_map/ppermute | solution.py:38
  207.7 35.6 %collective-permute-start.37 = (bf16[1,64,1536]{2,1,0:T(8,128)(2,1)}, bf16[1,64,1536]{2,1,0:T(8,128)(2,1)}, u32[]{:S(2)}, u32[]{:S(2)}) collective-permute-start(bf16[1,64,1536]{2,1,0:T(8,128)(2,1)} %get-tuple-element.251), channel_id=1, source_target_pairs={{0,3},{1,0},{2,1},{3,2},{4,7},{5,4},{6,5},{7,6},{8,11},{9,8},{10,9... | collective-permute-start | bytes 589832 | tf_op jit(solution)/shard_map/ppermute | solution.py:38
  207.7 36.4 %collective-permute-start.38 = (bf16[1,64,1536]{2,1,0:T(8,128)(2,1)}, bf16[1,64,1536]{2,1,0:T(8,128)(2,1)}, u32[]{:S(2)}, u32[]{:S(2)}) collective-permute-start(bf16[1,64,1536]{2,1,0:T(8,128)(2,1)} %get-tuple-element.252), channel_id=1, source_target_pairs={{0,2},{1,3},{2,0},{3,1},{4,6},{5,7},{6,4},{7,5},{8,10},{9,11},{10,... | collective-permute-start | bytes 589832 | tf_op jit(solution)/shard_map/ppermute | solution.py:38
  207.7 36.4 %collective-permute-start.39 = (bf16[1,64,1536]{2,1,0:T(8,128)(2,1)}, bf16[1,64,1536]{2,1,0:T(8,128)(2,1)}, u32[]{:S(2)}, u32[]{:S(2)}) collective-permute-start(bf16[1,64,1536]{2,1,0:T(8,128)(2,1)} %get-tuple-element.253), channel_id=1, source_target_pairs={{0,1},{1,2},{2,3},{3,0},{4,5},{5,6},{6,7},{7,4},{8,9},{9,10},{10,1... | collective-permute-start | bytes 589832 | tf_op jit(solution)/shard_map/ppermute | solution.py:38
  238.5 23.1 %collective-permute-start.43 = (bf16[1,64,1536]{2,1,0:T(8,128)(2,1)}, bf16[1,64,1536]{2,1,0:T(8,128)(2,1)S(1)}, u32[]{:S(2)}, u32[]{:S(2)}) collective-permute-start(bf16[1,64,1536]{2,1,0:T(8,128)(2,1)} %get-tuple-element.261), channel_id=1, source_target_pairs={{0,3},{1,0},{2,1},{3,2},{4,7},{5,4},{6,5},{7,6},{8,11},{9,8},{10,9... | collective-permute-start | bytes 589832 | tf_op jit(solution)/shard_map/ppermute | solution.py:38
  241.0 21.1 %collective-permute-start.44 = (bf16[1,64,1536]{2,1,0:T(8,128)(2,1)}, bf16[1,64,1536]{2,1,0:T(8,128)(2,1)S(1)}, u32[]{:S(2)}, u32[]{:S(2)}) collective-permute-start(bf16[1,64,1536]{2,1,0:T(8,128)(2,1)} %get-tuple-element.262), channel_id=1, source_target_pairs={{0,2},{1,3},{2,0},{3,1},{4,6},{5,7},{6,4},{7,5},{8,10},{9,11},{10,... | collective-permute-start | bytes 589832 | tf_op jit(solution)/shard_map/ppermute | solution.py:38
  243.3 18.8 %collective-permute-start.45 = (bf16[1,64,1536]{2,1,0:T(8,128)(2,1)}, bf16[1,64,1536]{2,1,0:T(8,128)(2,1)S(1)}, u32[]{:S(2)}, u32[]{:S(2)}) collective-permute-start(bf16[1,64,1536]{2,1,0:T(8,128)(2,1)} %get-tuple-element.263), channel_id=1, source_target_pairs={{0,1},{1,2},{2,3},{3,0},{4,5},{5,6},{6,7},{7,4},{8,9},{9,10},{10,1... | collective-permute-start | bytes 589832 | tf_op jit(solution)/shard_map/ppermute | solution.py:38
  257.6 18.6 %collective-permute-start.40 = (bf16[1,64,1024]{2,1,0:T(8,128)(2,1)S(1)}, bf16[1,64,1024]{2,1,0:T(8,128)(2,1)S(1)}, u32[]{:S(2)}, u32[]{:S(2)}) collective-permute-start(bf16[1,64,1024]{2,1,0:T(8,128)(2,1)S(1)} %get-tuple-element.256), channel_id=1, source_target_pairs={{0,3},{1,0},{2,1},{3,2},{4,7},{5,4},{6,5},{7,6},{8,11},{9,8},{10,9... | collective-permute-start | bytes 393224 | tf_op jit(solution)/shard_map/ppermute | solution.py:38
  320.7 20.1 %collective-permute-start.57 = (bf16[2,64,1536]{2,1,0:T(8,128)(2,1)S(1)}, bf16[2,64,1536]{2,1,0:T(8,128)(2,1)S(1)}, u32[]{:S(2)}, u32[]{:S(2)}) collective-permute-start(bf16[2,64,1536]{2,1,0:T(8,128)(2,1)S(1)} %get-tuple-element.286), channel_id=1, source_target_pairs={{0,3},{1,0},{2,1},{3,2},{4,7},{5,4},{6,5},{7,6},{8,11},{9,8},{10,9... | collective-permute-start | bytes 1179656 | tf_op jit(solution)/shard_map/ppermute | solution.py:38
  320.8 20.0 %collective-permute-start.58 = (bf16[2,64,1536]{2,1,0:T(8,128)(2,1)S(1)}, bf16[2,64,1536]{2,1,0:T(8,128)(2,1)S(1)}, u32[]{:S(2)}, u32[]{:S(2)}) collective-permute-start(bf16[2,64,1536]{2,1,0:T(8,128)(2,1)S(1)} %get-tuple-element.287), channel_id=1, source_target_pairs={{0,2},{1,3},{2,0},{3,1},{4,6},{5,7},{6,4},{7,5},{8,10},{9,11},{10,... | collective-permute-start | bytes 1179656 | tf_op jit(solution)/shard_map/ppermute | solution.py:38
  320.9 19.9 %collective-permute-start.59 = (bf16[2,64,1536]{2,1,0:T(8,128)(2,1)S(1)}, bf16[2,64,1536]{2,1,0:T(8,128)(2,1)S(1)}, u32[]{:S(2)}, u32[]{:S(2)}) collective-permute-start(bf16[2,64,1536]{2,1,0:T(8,128)(2,1)S(1)} %get-tuple-element.288), channel_id=1, source_target_pairs={{0,1},{1,2},{2,3},{3,0},{4,5},{5,6},{6,7},{7,4},{8,9},{9,10},{10,1... | collective-permute-start | bytes 1179656 | tf_op jit(solution)/shard_map/ppermute | solution.py:38
  343.5 20.6 %collective-permute-start.63 = (bf16[2,2,16,96,512]{4,3,2,1,0:T(8,128)(2,1)S(1)}, bf16[2,2,16,96,512]{4,3,2,1,0:T(8,128)(2,1)S(1)}, u32[]{:S(2)}, u32[]{:S(2)}) collective-permute-start(bf16[2,2,16,96,512]{4,3,2,1,0:T(8,128)(2,1)S(1)} %get-tuple-element.297), channel_id=1, source_target_pairs={{0,4},{4,0},{8,12},{12,8},{16,20},{20,16},{24,28},{28,24},{32,36},... | collective-permute-start | bytes 18874376 | tf_op jit(solution)/shard_map/ppermute | solution.py:68
  349.8 20.3 %collective-permute-start.64 = (bf16[1,2,16,96,512]{4,3,2,1,0:T(8,128)(2,1)S(1)}, bf16[1,2,16,96,512]{4,3,2,1,0:T(8,128)(2,1)}, u32[]{:S(2)}, u32[]{:S(2)}) collective-permute-start(bf16[1,2,16,96,512]{4,3,2,1,0:T(8,128)(2,1)S(1)} %get-tuple-element.299), channel_id=1, source_target_pairs={{0,4},{4,0},{8,12},{12,8},{16,20},{20,16},{24,28},{28,24},{32,36},... | collective-permute-start | bytes 9437192 | tf_op jit(solution)/shard_map/ppermute | solution.py:68
  349.9 31.5 %collective-permute-start.62 = (bf16[2,64,1536]{2,1,0:T(8,128)(2,1)S(1)}, bf16[2,64,1536]{2,1,0:T(8,128)(2,1)}, u32[]{:S(2)}, u32[]{:S(2)}) collective-permute-start(bf16[2,64,1536]{2,1,0:T(8,128)(2,1)S(1)} %convert_element_type.402.refs_6_.refs_4_), channel_id=1, source_target_pairs={{0,3},{1,0},{2,1},{3,2},{4,7},{5,4},{6,5},{7,6},{8,11},{9,8},{10,9... | collective-permute-start | bytes 1179656 | tf_op jit(solution)/shard_map/ppermute | solution.py:38
  352.2 29.2 %collective-permute-start.61 = (bf16[2,64,1536]{2,1,0:T(8,128)(2,1)S(1)}, bf16[2,64,1536]{2,1,0:T(8,128)(2,1)}, u32[]{:S(2)}, u32[]{:S(2)}) collective-permute-start(bf16[2,64,1536]{2,1,0:T(8,128)(2,1)S(1)} %convert_element_type.402.refs_6_.refs_4_), channel_id=1, source_target_pairs={{0,2},{1,3},{2,0},{3,1},{4,6},{5,7},{6,4},{7,5},{8,10},{9,11},{10,... | collective-permute-start | bytes 1179656 | tf_op jit(solution)/shard_map/ppermute | solution.py:38
  353.7 27.6 %collective-permute-start.60 = (bf16[2,64,1536]{2,1,0:T(8,128)(2,1)S(1)}, bf16[2,64,1536]{2,1,0:T(8,128)(2,1)}, u32[]{:S(2)}, u32[]{:S(2)}) collective-permute-start(bf16[2,64,1536]{2,1,0:T(8,128)(2,1)S(1)} %convert_element_type.402.refs_6_.refs_4_), channel_id=1, source_target_pairs={{0,1},{1,2},{2,3},{3,0},{4,5},{5,6},{6,7},{7,4},{8,9},{9,10},{10,1... | collective-permute-start | bytes 1179656 | tf_op jit(solution)/shard_map/ppermute | solution.py:38
  381.4 27.6 %collective-permute-start.67 = (bf16[4,3,96,512]{3,2,1,0:T(8,128)(2,1)}, bf16[4,3,96,512]{3,2,1,0:T(8,128)(2,1)}, u32[]{:S(2)}, u32[]{:S(2)}) collective-permute-start(bf16[4,3,96,512]{3,2,1,0:T(8,128)(2,1)} %get-tuple-element.317), channel_id=1, source_target_pairs={{0,8},{4,12},{8,0},{12,4},{16,24},{20,28},{24,16},{28,20},{32,40},... | collective-permute-start | bytes 3538952 | tf_op jit(solution)/shard_map/ppermute | solution.py:68
  382.0 27.3 %collective-permute-start.66 = (bf16[2,2,3,96,512]{4,3,2,1,0:T(8,128)(2,1)}, bf16[2,2,3,96,512]{4,3,2,1,0:T(8,128)(2,1)S(1)}, u32[]{:S(2)}, u32[]{:S(2)}) collective-permute-start(bf16[2,2,3,96,512]{4,3,2,1,0:T(8,128)(2,1)} %get-tuple-element.316), channel_id=1, source_target_pairs={{0,48},{4,52},{8,56},{12,60},{16,0},{20,4},{24,8},{28,12},{32,16},... | collective-permute-start | bytes 3538952 | tf_op jit(solution)/shard_map/ppermute | solution.py:68
  384.3 28.2 %collective-permute-start.65 = (bf16[2,2,3,96,512]{4,3,2,1,0:T(8,128)(2,1)}, bf16[2,2,3,96,512]{4,3,2,1,0:T(8,128)(2,1)S(1)}, u32[]{:S(2)}, u32[]{:S(2)}) collective-permute-start(bf16[2,2,3,96,512]{4,3,2,1,0:T(8,128)(2,1)} %get-tuple-element.304), channel_id=1, source_target_pairs={{0,16},{4,20},{8,24},{12,28},{16,32},{20,36},{24,40},{28,44},{32,4... | collective-permute-start | bytes 3538952 | tf_op jit(solution)/shard_map/ppermute | solution.py:68
  395.9 138.8 %reduce-scatter.5.cloned.1.call-start = ((), (), s32[]{:S(2)}) async-start(), calls=%async_computation.3 | async-start | bytes 1966080 | tf_op jit(solution)/shard_map/reduce_scatter | solution.py:960
  415.0 27.8 %collective-permute-start.74 = (bf16[4,3,96,512]{3,2,1,0:T(8,128)(2,1)}, bf16[4,3,96,512]{3,2,1,0:T(8,128)(2,1)}, u32[]{:S(2)}, u32[]{:S(2)}) collective-permute-start(bf16[4,3,96,512]{3,2,1,0:T(8,128)(2,1)} %get-tuple-element.328), channel_id=1, source_target_pairs={{0,8},{4,12},{8,0},{12,4},{16,24},{20,28},{24,16},{28,20},{32,40},... | collective-permute-start | bytes 3538952 | tf_op jit(solution)/shard_map/ppermute | solution.py:68
  513.2 21.5 %collective-permute-start.93 = (bf16[2,4,48,1024]{3,2,1,0:T(8,128)(2,1)}, bf16[2,4,48,1024]{3,2,1,0:T(8,128)(2,1)}, u32[]{:S(2)}, u32[]{:S(2)}) collective-permute-start(bf16[2,4,48,1024]{3,2,1,0:T(8,128)(2,1)} %get-tuple-element.445), channel_id=1, source_target_pairs={{0,2},{1,3},{2,0},{3,1},{4,6},{5,7},{6,4},{7,5},{8,10},{9,11},{10,... | collective-permute-start | bytes 2359304 | tf_op jit(solution)/shard_map/ppermute | solution.py:38
  (223 other events, 2329.1 us)
Sparse Core Ops, SparseCore 0:
  85.9 25.6 all-gather.2
  396.0 26.0 reduce-scatter.2
  469.1 27.3 reduce-scatter.4
